TPU v7x, 32 devices: a whole 2x2x4 slice. The times are simulated.
32 devices in a mesh: seq: 8 (over y, x, core), exp: 4 (over z).
Axes of the slice: x: 2, y: 2, z: 4, core: 2. Of those that a mesh axis runs over, the one named last changes fastest.
Arguments:
- residual_in: bfloat16 [2048, 3072], P('seq'), may hold values from -6 to 6
- queries: bfloat16 [2048, 4096], P('seq', 'exp'), may hold values from -6 to 6
- keys: bfloat16 [2048, 4096], P('seq', 'exp'), may hold values from -6 to 6
- values: bfloat16 [2048, 4096], P('seq', 'exp'), may hold values from -6 to 6
- rates: float32 [32], P('exp'), may hold values from 3.0517578e-05 to 0.0333333333, as said below
- doc_lengths: int32 [16], replicated, may hold values from 1 to 1024, 2048 in all
- out_weight: bfloat16 [4096, 3072], P('exp'), may hold values from -0.09375 to 0.09375
- router: bfloat16 [3072, 4], replicated, may hold values from -0.109375 to 0.109375
- gate_weight: bfloat16 [8, 3072, 2560], P('seq', None, 'exp'), may hold values from -0.109375 to 0.109375
- up_weight: bfloat16 [8, 3072, 2560], P('seq', None, 'exp'), may hold values from -0.109375 to 0.109375
- down_weight: bfloat16 [8, 2560, 3072], P('seq', 'exp'), may hold values from -0.078125 to 0.078125
- routes: int32 [2048, 2], P('seq'), may hold values from 0 to 3, all different within a row; in each aligned block of 256 rows (0 to 255, 256 to 511, ...) at most 136 rows name the same one
Outputs:
- mixed: bfloat16 [2048, 3072], P(('seq', 'exp'))
Inputs may be any that keep to these rules, and one draw needn't show every extreme that they name: `rates`: each head forgets at its own rate. `doc_lengths`: the lengths sum to 2048; the longest is exactly 1024. `routes`: the two experts of a position differ. In each aligned block of 256 rows no expert is named by more than 136 rows, and in some block one expert is named by exactly 136 rows.
All inputs are finite; a program needn't handle non-finite values.
Results may differ from a plain program's by a relative error of at most 0.014.
Values may be sent and summed in bfloat16 or wider, within the bound.
No kernel may reach another device: no remote copies, remote signals or barrier semaphores. Data moves between devices by JAX's collectives and lax.ppermute only.
A program may use at most 128 MiB of HBM per device.

v0:
```python
import jax
import jax.numpy as jnp
from jax import lax
from jax.sharding import PartitionSpec as P

EPSILON = 1e-06


def rms_rows(rows):
    return (rows * lax.rsqrt(jnp.mean(rows * rows, axis=-1, keepdims=True) + EPSILON)).astype(
        jnp.bfloat16
    )


def body(
    residual_in,
    queries,
    keys,
    values,
    rates,
    doc_lengths,
    out_weight,
    router,
    gate_weight,
    up_weight,
    down_weight,
    routes,
):
    highest = lax.Precision.HIGHEST
    seq_count = lax.axis_size("seq")
    exp_count = lax.axis_size("exp")
    seq_index = lax.axis_index("seq")
    exp_index = lax.axis_index("exp")
    block_len = queries.shape[0]
    head_count = rates.shape[0]
    head_size = queries.shape[1] // head_count
    width = out_weight.shape[1]
    experts = seq_count // 2
    capacity = exp_count * max(1, 2 * block_len // experts * 17 // (16 * exp_count))
    own_count = block_len // exp_count
    local_index = jnp.arange(block_len, dtype=jnp.int32)
    block_base = seq_index * block_len
    position = block_base + local_index
    doc_starts = jnp.cumsum(doc_lengths) - doc_lengths
    doc_of = jnp.sum((doc_starts[None, :] <= position[:, None]).astype(jnp.int32), axis=1) - 1
    first_start = jnp.max(jnp.where(doc_starts <= block_base, doc_starts, 0))
    query_heads = queries.reshape(block_len, head_count, head_size)
    key_heads = keys.reshape(block_len, head_count, head_size)
    value_heads = values.reshape(block_len, head_count, head_size)
    distance_end = (block_len - local_index).astype(jnp.float32)
    same_last = (doc_of == doc_of[-1]).astype(jnp.float32)
    end_weight = jnp.exp(-rates[None, :] * distance_end[:, None]) * same_last[:, None]
    weighted_keys = end_weight[:, :, None] * key_heads.astype(jnp.float32)
    end_state = jnp.einsum(
        "tha,thb->hab", weighted_keys, value_heads.astype(jnp.float32), precision=highest
    )
    shards = lax.all_gather(end_state[None], "seq", axis=0, tiled=True)
    shard_count = shards.shape[0]
    source = jnp.arange(shard_count, dtype=jnp.int32)
    source_end = (source + 1) * block_len
    usable = (source < seq_index) & (source_end - 1 >= first_start)
    distance = jnp.maximum(block_base - source_end, 0).astype(jnp.float32)
    weight = jnp.where(usable[:, None], jnp.exp(-rates[None, :] * distance[:, None]), 0.0)
    incoming = jnp.einsum("jh,jhab->hab", weight, shards, precision=highest)
    carried_rounded = incoming.astype(jnp.bfloat16)
    scores = jnp.einsum("thd,uhd->htu", query_heads, key_heads, preferred_element_type=jnp.float32)
    lag_steps = local_index[:, None] - local_index[None, :]
    allowed = (lag_steps >= 0) & (doc_of[:, None] == doc_of[None, :])
    decay_mask = jnp.where(
        allowed[None],
        jnp.exp(-rates[:, None, None] * jnp.maximum(lag_steps, 0).astype(jnp.float32)[None]),
        0.0,
    )
    scaled_scores = (scores * decay_mask).astype(jnp.bfloat16)
    inside_term = jnp.einsum(
        "htu,uhd->thd", scaled_scores, value_heads, preferred_element_type=jnp.float32
    )
    carried_term = jnp.einsum(
        "thd,hde->the", query_heads, carried_rounded, preferred_element_type=jnp.float32
    )
    carry_scale = (
        jnp.exp(-rates[None, :] * local_index.astype(jnp.float32)[:, None])
        * (doc_of == doc_of[0]).astype(jnp.float32)[:, None]
    )
    heads_raw = inside_term + carried_term * carry_scale[:, :, None]
    attention = rms_rows(heads_raw).reshape(block_len, head_count * head_size)
    partial_value = jnp.dot(attention, out_weight, preferred_element_type=jnp.float32)
    head_total = lax.psum(partial_value.astype(jnp.bfloat16), "exp").astype(jnp.float32)
    hidden = (residual_in.astype(jnp.float32) + head_total).astype(jnp.bfloat16)
    normed = rms_rows(hidden.astype(jnp.float32))
    own_hidden = lax.dynamic_slice_in_dim(hidden, exp_index * own_count, own_count, 0)
    logits = jnp.dot(normed, router, preferred_element_type=jnp.float32)
    expert_ids = jnp.arange(experts, dtype=jnp.int32)
    chosen = routes[:, :, None] == expert_ids[None, None, :]
    route_logits = jnp.sum(jnp.where(chosen, logits[:, None, :], 0.0), axis=2)
    route_weight = jax.nn.sigmoid(route_logits - route_logits[:, ::-1])
    pair_expert = routes.reshape(-1)
    onehot = (pair_expert[:, None] == expert_ids[None, :]).astype(jnp.int32)
    rank_before = jnp.cumsum(onehot, axis=0) - onehot
    slot_index = jnp.sum(rank_before * onehot, axis=1)
    pair_rows = jnp.repeat(normed, 2, axis=0)
    buffer = (
        jnp.zeros((experts, capacity, width), jnp.bfloat16)
        .at[pair_expert, slot_index]
        .set(pair_rows)
    )
    outgoing = jnp.repeat(buffer, 2, axis=0)
    received = lax.all_to_all(outgoing, "seq", split_axis=0, concat_axis=0, tiled=True)
    gate_act = jnp.einsum(
        "sid,df->sif", received, gate_weight[0], preferred_element_type=jnp.float32
    )
    up_act = jnp.einsum("sid,df->sif", received, up_weight[0], preferred_element_type=jnp.float32)
    active = (jax.nn.silu(gate_act) * up_act).astype(jnp.bfloat16)
    partials = jnp.einsum(
        "sif,fd->sid", active, down_weight[0], preferred_element_type=jnp.float32
    ).astype(jnp.bfloat16)
    returned = lax.all_to_all(partials, "seq", split_axis=0, concat_axis=0, tiled=True)
    expert_table = jnp.sum(
        returned.reshape(experts, 2, capacity, width).astype(jnp.float32), axis=1
    ).reshape(experts * capacity, width)
    picked = expert_table[pair_expert * capacity + slot_index]
    expert_mix = jnp.sum(
        (picked * route_weight.reshape(-1)[:, None]).reshape(block_len, 2, width), axis=1
    )
    own_mix = lax.psum_scatter(
        expert_mix.astype(jnp.bfloat16), "exp", scatter_dimension=0, tiled=True
    ).astype(jnp.float32)
    return (own_hidden.astype(jnp.float32) + own_mix).astype(jnp.bfloat16)


def solution(mesh):
    in_specs = (
        P("seq", None),
        P("seq", "exp"),
        P("seq", "exp"),
        P("seq", "exp"),
        P("exp"),
        P(),
        P("exp", None),
        P(),
        P("seq", None, "exp"),
        P("seq", None, "exp"),
        P("seq", "exp", None),
        P("seq", None),
    )
    out_specs = P(("seq", "exp"), None)
    return jax.shard_map(body, mesh=mesh, in_specs=in_specs, out_specs=out_specs, check_vma=False)
```

profile of v0, /device:TPU:0, one launch (start us, length us, event | category | flops | bytes accessed | tf_op | source)
XLA Modules:
  0.0 537.1 jit_solution(6370954812978265688)
XLA Ops:
  6.5 0.0 copy-start
  6.5 0.0 all-gather.3.cloned.1.call-start
  6.5 0.7 neg.15
  7.3 0.7 copy.44
  8.0 0.1 reduce.1
  8.2 1.3 fusion.39
  9.4 0.1 convert_reduce_fusion.1
  9.5 0.7 fusion.41
  10.2 1.2 copy.61
  11.5 1.3 compare_convert_fusion.1
  12.7 0.1 exponential_multiply_fusion.1
  12.8 2.5 fusion.13
  15.3 0.0 all-gather.3.cloned.1.call-update
  15.4 0.0 all-reduce.2.cloned.1.call-start
  15.4 0.7 compare_and_fusion
  16.1 0.1 select_bitcast_fusion
  16.2 0.1 fusion.33
  16.3 38.6 %all-gather.3.cloned.1.call-done = f32[64,128,128]{2,1,0:T(8,128)} async-done(((f32[8,128,128]{2,1,0:T(8,128)}), f32[64,128,128]{2,1,0:T(8,128)}) %all-gather.3.cloned.1.call-update) | async-done | bytes 4194320 | tf_op jit(solution)/shard_map/all_gather | solution.py:57
  54.9 2.6 multiply_reduce_fusion.1
  57.5 0.2 copy.59
  57.7 0.0 copy-done
  57.7 0.3 fusion.12
  58.0 2.0 multiply_reduce_fusion.2
  60.0 0.1 multiply_convert_fusion.2
  60.1 0.0 copy-start.6
  60.1 5.8 %convolution_convert_fusion.1 = bf16[256,3072]{1,0:T(8,128)(2,1)} fusion(bf16[256,1024]{0,1:T(8,128)(2,1)S(1)} %bitcast.111, bf16[1024,3072]{1,0:T(8,128)(2,1)} %param.18), kind=kOutput, calls=%fused_computation.13 | convolution fusion | flops 1611399168 | bytes 8388608 | tf_op jit(solution)/shard_map/dot_general | solution.py:87
  65.9 0.0 all-reduce.2.cloned.1.call-update
  65.9 0.0 copy-done.6
  65.9 0.1 copy.49
  66.0 0.1 eq.86
  66.2 0.1 eq.82
  66.3 0.1 reshape.348
  66.5 1.2 reduce-window.20
  67.7 0.2 slice_reduce_fusion
  67.9 0.2 reduce-window.21
  68.1 0.1 add_bitcast_fusion
  68.2 66.9 %all-reduce.2.cloned.1.call-done = bf16[256,3072]{1,0:T(8,128)(2,1)} async-done(((bf16[256,3072]{1,0:T(8,128)(2,1)}), bf16[256,3072]{1,0:T(8,128)(2,1)}) %all-reduce.2.cloned.1.call-update) | async-done | bytes 1572880 | tf_op jit(solution)/shard_map/psum | solution.py:88
  135.2 0.0 copy-done.4
  135.2 2.1 fusion.5
  137.3 1.1 copy-done.2
  138.5 0.5 fusion.6
  138.9 3.3 broadcast_in_dim.55
  142.2 7.5 %reshape.364 = bf16[512,3072]{1,0:T(8,128)(2,1)} reshape(bf16[256,2,3072]{2,1,0:T(2,128)(2,1)} %broadcast_in_dim.55) | data formatting | bytes 6291456 | tf_op jit(solution)/shard_map/reshape | solution.py:101
  149.7 2.1 broadcast_in_dim.54
  151.8 113.1 %scatter_fusion = bf16[4,136,3072]{2,1,0:T(8,128)(2,1)} fusion(bf16[4,136,3072]{2,1,0:T(8,128)(2,1)} %broadcast_in_dim.54, s32[512]{0:T(512)S(1)} %bitcast.108, bf16[512,3072]{1,0:T(8,128)(2,1)} %reshape.364), kind=kCustom, calls=%fused_computation.1 | custom fusion | bytes 9441280 | tf_op jit(solution)/shard_map/scatter | solution.py:105
  264.9 3.0 broadcast_in_dim.56
  267.9 0.0 copy-start.7
  267.9 79.6 %all_to_all.10 = bf16[8,136,3072]{2,1,0:T(8,128)(2,1)S(1)} all-to-all(bf16[8,136,3072]{2,1,0:T(8,128)(2,1)S(1)} %bitcast.109), channel_id=1, replica_groups=mesh['seq'=8,'exp'=4] {'seq'}, dimensions={0} | all-to-all | bytes 13369344 | tf_op jit(solution)/shard_map/all_to_all | solution.py:108
  347.5 2.8 copy-done.3
  350.3 7.0 %fusion.1 = f32[8,136,640]{2,1,0:T(8,128)} fusion(bf16[8,136,3072]{2,1,0:T(8,128)(2,1)S(1)} %all_to_all.10, bf16[1,3072,640]{2,1,0:T(8,128)(2,1)S(1)} %copy-done.7), kind=kOutput, calls=%fused_computation.7 | convolution fusion | flops 4278190080 | bytes 13402112 | tf_op jit(solution)/shard_map/sid,df->sif/dot_general | solution.py:112
  357.4 20.2 %convolution_convert_fusion = bf16[8,136,3072]{2,1,0:T(8,128)(2,1)} fusion(bf16[1,640,3072]{2,1,0:T(8,128)(2,1)} %param.22, f32[8,136,640]{2,1,0:T(8,128)} %fusion.1, bf16[8,136,3072]{2,1,0:T(8,128)(2,1)} %copy-done.3, bf16[1,3072,640]{2,1,0:T(8,128)(2,1)} %param.20), kind=kOutput, calls=%fused_computation.4 | convolution fusion | flops 8563900416 | bytes 24018944 | tf_op jit(solution)/shard_map/sif,fd->sid/dot_general | solution.py:114
  377.6 4.9 all-to-all-start.1
  382.5 0.3 reduce-scatter.2.cloned.1.call-start
  382.8 0.5 fusion.44
  383.4 0.1 rev.3
  383.5 0.1 copy.52
  383.6 74.7 %all-to-all-done.1 = bf16[8,136,3072]{2,1,0:T(8,128)(2,1)} async-done(((bf16[8,136,3072]{2,1,0:T(8,128)(2,1)}), bf16[8,136,3072]{2,1,0:T(8,128)(2,1)}, u32[]{:S(2)}, u32[]{:S(2)}) %all-to-all-start.1) | async-done | bytes 6684704 | tf_op jit(solution)/shard_map/all_to_all | solution.py:117
  458.3 7.8 %convert_reduce_fusion = f32[4,136,3072]{2,1,0:T(8,128)} fusion(bf16[8,136,3072]{2,1,0:T(8,128)(2,1)} %all-to-all-done.1), kind=kLoop, calls=%fused_computation.2 | loop fusion | flops 5013504 | bytes 13369344 | tf_op jit(solution)/shard_map/reduce_sum | solution.py:118
  466.1 10.2 %gather_fusion = f32[512,3072]{1,0:T(8,128)} fusion(f32[544,3072]{1,0:T(8,128)} %bitcast.107, s32[1024]{0:T(1024)S(1)} %pad_clamp_fusion), kind=kCustom, calls=%fused_computation | custom fusion | bytes 12584960 | tf_op jit(solution)/shard_map/gather | solution.py:121
  476.3 8.1 %gather.6 = f32[256,2,3072]{2,1,0:T(2,128)} reshape(f32[512,3072]{1,0:T(8,128)} %gather_fusion) | data formatting | bytes 12582912 | tf_op jit(solution)/shard_map/gather | solution.py:121
  484.4 11.5 %multiply_reduce_fusion = bf16[256,3072]{1,0:T(8,128)(2,1)} fusion(f32[256,2,3072]{2,1,0:T(2,128)} %gather.6, f32[256,2]{1,0:T(8,128)S(1)} %copy.52), kind=kLoop, calls=%fused_computation.3 | loop fusion | flops 2359296 | bytes 7866368 | tf_op jit(solution)/shard_map/reduce_sum | solution.py:122
  495.9 0.0 reduce-scatter.2.cloned.1.call-update
  496.0 32.7 %reduce-scatter.2.cloned.1.call-done = bf16[64,3072]{1,0:T(8,128)(2,1)} async-done(((bf16[256,3072]{1,0:T(8,128)(2,1)}), bf16[64,3072]{1,0:T(8,128)(2,1)}) %reduce-scatter.2.cloned.1.call-update) | async-done | bytes 393232 | tf_op jit(solution)/shard_map/reduce_scatter | solution.py:125
  528.6 2.0 add_convert_fusion.1
  (22 shorter events, 0.2 us)
Async XLA Ops:
  6.5 51.1 %copy-start = (bf16[256,1024]{1,0:T(8,128)(2,1)S(1)}, bf16[256,1024]{1,0:T(8,128)(2,1)}, u32[]{:S(2)}) copy-start(bf16[256,1024]{1,0:T(8,128)(2,1)} %param.13) | copy-start | bytes 1572868
  6.5 48.4 %all-gather.3.cloned.1.call-start = ((), (), s32[]{:S(2)}) async-start(), calls=%async_computation.5 | async-start | bytes 4718592 | tf_op jit(solution)/shard_map/all_gather | solution.py:57
  15.4 119.8 %all-reduce.2.cloned.1.call-start = ((), (), s32[]{:S(2)}) async-start(), calls=%async_computation.3 | async-start | bytes 3145728 | tf_op jit(solution)/shard_map/psum | solution.py:88
  60.1 5.8 %copy-start.6 = (s32[256,2]{0,1:T(2,128)S(1)}, s32[256,2]{0,1:T(2,128)}, u32[]{:S(2)}) copy-start(s32[256,2]{0,1:T(2,128)} %param.23) | copy-start | bytes 6148
  65.9 69.3 %copy-start.4 = (bf16[256,3072]{1,0:T(8,128)(2,1)S(1)}, bf16[256,3072]{1,0:T(8,128)(2,1)}, u32[]{:S(2)}) copy-start(bf16[256,3072]{1,0:T(8,128)(2,1)} %param.12) | copy-start | bytes 4718596
  137.3 1.2 copy-start.2
  267.9 82.4 %copy-start.7 = (bf16[1,3072,640]{2,1,0:T(8,128)(2,1)S(1)}, bf16[1,3072,640]{2,1,0:T(8,128)(2,1)}, u32[]{:S(2)}) copy-start(bf16[1,3072,640]{2,1,0:T(8,128)(2,1)} %param.21) | copy-start | bytes 11796484
  347.5 2.8 copy-start.3
  377.6 5.2 copy-start.5
  377.6 80.7 %all-to-all-start.1 = ((bf16[8,136,3072]{2,1,0:T(8,128)(2,1)}), bf16[8,136,3072]{2,1,0:T(8,128)(2,1)}, u32[]{:S(2)}, u32[]{:S(2)}) async-start(bf16[8,136,3072]{2,1,0:T(8,128)(2,1)} %convolution_convert_fusion), calls=%async_computation.1 | async-start | bytes 13369344 | tf_op jit(solution)/shard_map/all_to_all | solution.py:117
  382.5 146.1 %reduce-scatter.2.cloned.1.call-start = ((), (), s32[]{:S(2)}) async-start(), calls=%async_computation.4 | async-start | bytes 1966080 | tf_op jit(solution)/shard_map/reduce_scatter | solution.py:125
  484.4 46.2 %copy-start.1 = (bf16[256,1024]{1,0:T(8,128)(2,1)S(1)}, bf16[256,1024]{1,0:T(8,128)(2,1)}, u32[]{:S(2)}) copy-start(bf16[256,1024]{1,0:T(8,128)(2,1)} %param.13) | copy-start | bytes 1572868
Sparse Core Ops, SparseCore 0:
  15.5 39.4 all-gather.2
  66.0 69.1 all-reduce.1
  496.1 32.5 reduce-scatter.1
where the time goes:
time: 539 us; the launch traced here: 537 us
  waiting for transfers between devices  213 us (40%)
  local copies, waits for them, and re-layouts  155 us (29%)
  blocking collectives  79.6 us (15%)
  matrix products  38.3 us (7%)
  other arithmetic  32.6 us (6%)
  between operations  13.4 us (2%)
    scatter x1, local copies, waits for them, and re-layouts, body(): buffer = jnp.zeros((experts, capacity, width), jnp.bfloat16).at[pair_expe...  113 us
    all_to_all x1, blocking collectives, body(): lax.all_to_all(outgoing, 'seq', split_axis=0, concat_axis=0, tiled=True)  79.6 us
    all_to_all x1, waiting for transfers between devices, body(): lax.all_to_all(partials, 'seq', split_axis=0, concat_axis=0, tiled=True)  74.7 us
    psum x1, waiting for transfers between devices, body(): lax.psum(partial_value.astype(jnp.bfloat16), 'exp').astype(jnp.float32)  66.9 us
    all_gather x1, waiting for transfers between devices, body(): shards = lax.all_gather(end_state[None], 'seq', axis=0, tiled=True)  38.6 us
    reduce_scatter x1, waiting for transfers between devices, body(): lax.psum_scatter(expert_mix.astype(jnp.bfloat16), 'exp', scatter_dimensio...  32.7 us
    dot_general x1, matrix products, body(): jnp.einsum('sif,fd->sid', active, down_weight[0], preferred_element_type=...  20.2 us
    gather x2, local copies, waits for them, and re-layouts, body(): picked = expert_table[pair_expert * capacity + slot_index]  18.3 us
  transfers between devices with their start and end apart: 4, of which 4 were waited for; matrix products, arithmetic and copies ran while one was open for 1% of the time, Pallas kernels for 0%

commit v1 on v0

v1 whole, which is shorter than its diff:
```python
import jax
import jax.numpy as jnp
from jax import lax
from jax.sharding import PartitionSpec as P

EPSILON = 1e-06
BF = jnp.bfloat16
F32 = jnp.float32


def xor_pairs(count, step):
    return [(i, i ^ step) for i in range(count)]


def line_scatter(part, rows_each, count, me):
    def rows(index):
        return lax.dynamic_slice_in_dim(part, jnp.clip(index, 0, count - 1) * rows_each, rows_each, 0)

    from_left = None
    from_right = None
    for step in range(1, count):
        to_right = rows(me + count - step)
        to_left = rows(me - count + step)
        if step > 1:
            to_right = (to_right.astype(F32) + from_left.astype(F32)).astype(BF)
            to_left = (to_left.astype(F32) + from_right.astype(F32)).astype(BF)
        from_left = lax.ppermute(to_right, "exp", [(i, i + 1) for i in range(step)])
        from_right = lax.ppermute(to_left, "exp", [(count - 1 - i, count - 2 - i) for i in range(step)])
    total = rows(me).astype(F32)
    if count > 1:
        total = total + from_left.astype(F32) + from_right.astype(F32)
    return total


def line_gather(own, count, me):
    rows_each = own.shape[0]
    lower = []
    upper = []
    left = own
    right = own
    for step in range(1, count):
        left = lax.ppermute(left, "exp", [(i, i + 1) for i in range(step - 1, count - 1)])
        right = lax.ppermute(right, "exp", [(i + 1, i) for i in range(0, count - step)])
        lower.append(left)
        upper.append(right)
    spread = jnp.concatenate(lower[::-1] + [own] + upper, axis=0)
    return lax.dynamic_slice_in_dim(spread, (count - 1 - me) * rows_each, count * rows_each, 0)


def body(
    residual_in,
    queries,
    keys,
    values,
    rates,
    doc_lengths,
    out_weight,
    router,
    gate_weight,
    up_weight,
    down_weight,
    routes,
):
    highest = lax.Precision.HIGHEST
    seq_count = lax.axis_size("seq")
    exp_count = lax.axis_size("exp")
    seq_index = lax.axis_index("seq")
    exp_index = lax.axis_index("exp")
    chips = seq_count // 2
    chip = seq_index // 2
    core = seq_index % 2
    block_len = queries.shape[0]
    head_count = rates.shape[0]
    head_size = queries.shape[1] // head_count
    width = out_weight.shape[1]
    half = width // 2
    experts = seq_count // 2
    capacity = exp_count * max(1, 2 * block_len // experts * 17 // (16 * exp_count))
    own_count = block_len // exp_count
    local_index = jnp.arange(block_len, dtype=jnp.int32)
    block_base = seq_index * block_len
    position = block_base + local_index
    doc_starts = jnp.cumsum(doc_lengths) - doc_lengths
    doc_of = jnp.sum((doc_starts[None, :] <= position[:, None]).astype(jnp.int32), axis=1) - 1
    query_heads = queries.reshape(block_len, head_count, head_size)
    key_heads = keys.reshape(block_len, head_count, head_size)
    value_heads = values.reshape(block_len, head_count, head_size)

    distance_end = (block_len - local_index).astype(F32)
    same_last = (doc_of == doc_of[-1]).astype(F32)
    end_weight = jnp.exp(-rates[None, :] * distance_end[:, None]) * same_last[:, None]
    weighted_keys = end_weight[:, :, None] * key_heads.astype(F32)
    end_state = jnp.einsum(
        "tha,thb->hab", weighted_keys, value_heads.astype(F32), precision=highest
    ).astype(BF)

    half_heads = head_count // 2
    head_at = core * half_heads
    partner_state = lax.ppermute(end_state, "seq", xor_pairs(seq_count, 1))
    mine = lax.dynamic_slice_in_dim(end_state, head_at, half_heads, 0).astype(F32)
    theirs = lax.dynamic_slice_in_dim(partner_state, head_at, half_heads, 0).astype(F32)
    first_state = jnp.where(core == 0, mine, theirs)
    second_state = jnp.where(core == 0, theirs, mine)
    half_rates = lax.dynamic_slice_in_dim(rates, head_at, half_heads, 0)

    def start_at(where):
        return jnp.max(jnp.where(doc_starts <= where, doc_starts, 0))

    chip_base = chip * 2 * block_len
    block_decay = jnp.exp(-half_rates * float(block_len))
    last_start = start_at(chip_base + 2 * block_len - 1)
    keep_first = jnp.where(last_start <= chip_base + block_len - 1, block_decay, 0.0)
    chip_state = (second_state + keep_first[:, None, None] * first_state).astype(BF)
    base_start = start_at(chip_base)
    carried_first = jnp.zeros_like(first_state)
    for step in range(1, chips):
        other_state = lax.ppermute(chip_state, "seq", xor_pairs(seq_count, 2 * step))
        other = jnp.bitwise_xor(chip, step)
        other_end = (other + 1) * 2 * block_len
        usable = (other < chip) & (other_end - 1 >= base_start)
        distance = jnp.maximum(chip_base - other_end, 0).astype(F32)
        weight = jnp.where(usable, jnp.exp(-half_rates * distance), 0.0)
        carried_first = carried_first + weight[:, None, None] * other_state.astype(F32)
    middle = chip_base + block_len
    middle_start = start_at(middle)
    take_first = (middle - 1 >= middle_start).astype(F32)
    take_carried = jnp.where(chip_base - 1 >= middle_start, block_decay, 0.0)
    carried_second = take_first * first_state + take_carried[:, None, None] * carried_first
    carried_first = carried_first.astype(BF)
    carried_second = carried_second.astype(BF)
    carried_mine = jnp.where(core == 0, carried_first, carried_second)
    carried_other = lax.ppermute(
        jnp.where(core == 0, carried_second, carried_first), "seq", xor_pairs(seq_count, 1)
    )
    carried_rounded = jnp.concatenate(
        [
            jnp.where(core == 0, carried_mine, carried_other),
            jnp.where(core == 0, carried_other, carried_mine),
        ],
        axis=0,
    )

    scores = jnp.einsum("thd,uhd->htu", query_heads, key_heads, preferred_element_type=F32)
    lag_steps = local_index[:, None] - local_index[None, :]
    allowed = (lag_steps >= 0) & (doc_of[:, None] == doc_of[None, :])
    decay_mask = jnp.where(
        allowed[None],
        jnp.exp(-rates[:, None, None] * jnp.maximum(lag_steps, 0).astype(F32)[None]),
        0.0,
    )
    scaled_scores = (scores * decay_mask).astype(BF)
    inside_term = jnp.einsum(
        "htu,uhd->thd", scaled_scores, value_heads, preferred_element_type=F32
    )
    carried_term = jnp.einsum(
        "thd,hde->the", query_heads, carried_rounded, preferred_element_type=F32
    )
    carry_scale = (
        jnp.exp(-rates[None, :] * local_index.astype(F32)[:, None])
        * (doc_of == doc_of[0]).astype(F32)[:, None]
    )
    heads_raw = inside_term + carried_term * carry_scale[:, :, None]
    attention = (
        (heads_raw * lax.rsqrt(jnp.mean(heads_raw * heads_raw, axis=-1, keepdims=True) + EPSILON))
        .astype(BF)
        .reshape(block_len, head_count * head_size)
    )
    partial_value = jnp.dot(attention, out_weight, preferred_element_type=F32).astype(BF)

    own_total = line_scatter(partial_value, own_count, exp_count, exp_index)
    own_residual = lax.dynamic_slice_in_dim(residual_in, exp_index * own_count, own_count, 0)
    own_hidden = (own_residual.astype(F32) + own_total).astype(BF)
    hidden = line_gather(own_hidden, exp_count, exp_index)
    hidden_wide = hidden.astype(F32)
    row_scale = lax.rsqrt(jnp.mean(hidden_wide * hidden_wide, axis=-1, keepdims=True) + EPSILON)
    logits = jnp.dot(hidden, router, preferred_element_type=F32) * row_scale
    expert_ids = jnp.arange(experts, dtype=jnp.int32)
    chosen = routes[:, :, None] == expert_ids[None, None, :]
    route_logits = jnp.sum(jnp.where(chosen, logits[:, None, :], 0.0), axis=2)
    route_weight = jax.nn.sigmoid(route_logits - route_logits[:, ::-1])

    onehot = jnp.sum(chosen.astype(jnp.int32), axis=1)
    before = (local_index[:, None] > local_index[None, :]).astype(BF)
    rank = jnp.dot(before, onehot.astype(BF), preferred_element_type=F32).astype(jnp.int32)
    slot = jnp.sum(jnp.where(chosen, rank[:, None, :], 0), axis=2)
    group = jnp.bitwise_xor(routes, chip)
    place = group * capacity + slot
    slots = experts * capacity
    slot_ids = jnp.arange(slots, dtype=jnp.int32)
    pick = [(place[:, k][:, None] == slot_ids[None, :]).astype(BF) for k in range(2)]
    spread = jnp.transpose(pick[0] + pick[1])

    here = lax.dynamic_slice_in_dim(hidden, core * half, half, 1)
    there = lax.dynamic_slice_in_dim(hidden, (1 - core) * half, half, 1)
    send_here = jnp.dot(spread, here, preferred_element_type=F32).astype(BF)
    send_there = jnp.dot(spread, there, preferred_element_type=F32).astype(BF)
    arrived = []
    for g in range(chips):
        rows = slice(g * capacity, (g + 1) * capacity)
        for b in range(2):
            block = (send_here if b == 0 else send_there)[rows]
            if g or b:
                block = lax.ppermute(block, "seq", xor_pairs(seq_count, 2 * g + b))
            arrived.append(block)
    mine = jnp.concatenate(arrived, axis=0)
    swap = jnp.concatenate([arrived[i ^ 1] for i in range(seq_count)], axis=0)
    theirs = lax.ppermute(swap, "seq", xor_pairs(seq_count, 1))
    received = jnp.concatenate(
        [jnp.where(core == 0, mine, theirs), jnp.where(core == 0, theirs, mine)], axis=1
    )
    received_wide = received.astype(F32)
    in_scale = lax.rsqrt(
        jnp.mean(received_wide * received_wide, axis=-1, keepdims=True) + EPSILON
    )
    gate_act = jnp.dot(received, gate_weight[0], preferred_element_type=F32) * in_scale
    up_act = jnp.dot(received, up_weight[0], preferred_element_type=F32) * in_scale
    active = (jax.nn.silu(gate_act) * up_act).astype(BF)
    partials = jnp.dot(active, down_weight[0], preferred_element_type=F32).astype(BF)

    keep = lax.dynamic_slice_in_dim(partials, core * half, half, 1)
    give = lax.dynamic_slice_in_dim(partials, (1 - core) * half, half, 1)
    give = give.reshape(chips, 2, capacity, half)[:, ::-1].reshape(seq_count * capacity, half)
    got = lax.ppermute(give, "seq", xor_pairs(seq_count, 1))
    sums = (keep.astype(F32) + got.astype(F32)).astype(BF)
    tables = [[], []]
    for g in range(chips):
        for b in range(2):
            i = 2 * g + b
            block = sums[i * capacity : (i + 1) * capacity]
            if i:
                block = lax.ppermute(block, "seq", xor_pairs(seq_count, i))
            tables[b].append(block)
    mixes = []
    for b in range(2):
        table = jnp.concatenate(tables[b], axis=0)
        mix = sum(
            jnp.dot(pick[k], table, preferred_element_type=F32) * route_weight[:, k : k + 1]
            for k in range(2)
        )
        mixes.append(line_scatter(mix.astype(BF), own_count, exp_count, exp_index))
    own_mix = jnp.concatenate(
        [jnp.where(core == 0, mixes[0], mixes[1]), jnp.where(core == 0, mixes[1], mixes[0])],
        axis=1,
    )
    return (own_hidden.astype(F32) + own_mix).astype(BF)


def solution(mesh):
    in_specs = (
        P("seq", None),
        P("seq", "exp"),
        P("seq", "exp"),
        P("seq", "exp"),
        P("exp"),
        P(),
        P("exp", None),
        P(),
        P("seq", None, "exp"),
        P("seq", None, "exp"),
        P("seq", "exp", None),
        P("seq", None),
    )
    out_specs = P(("seq", "exp"), None)
    return jax.shard_map(body, mesh=mesh, in_specs=in_specs, out_specs=out_specs, check_vma=False)
```

time: 539 us -> 285 us (0.53)
  local copies, waits for them, and re-layouts: 155 us -> 16.4 us
  blocking collectives: 79.6 us -> 0 us
  waiting for transfers between devices: 213 us -> 151 us
  starting transfers between devices: 5.23 us -> 65.1 us
  other arithmetic: 32.6 us -> 15.3 us
  between operations: 13.4 us -> 4.85 us
  matrix products: 38.3 us -> 31.4 us
    ppermute x0 -> x45, waiting for transfers between devices: none -> 151 us  [the longest x7 34.1 us: body(): block = lax.ppermute(block, 'seq', xor_pairs(seq_count, 2 * g + b))]
    scatter x1 -> x0, local copies, waits for them, and re-layouts: 113 us -> none  [body(): buffer = jnp.zeros((experts, capacity, width), jnp.bfloat16).at[pair_expe...]
    all_to_all x1 -> x0, blocking collectives: 79.6 us -> none  [body(): lax.all_to_all(outgoing, 'seq', split_axis=0, concat_axis=0, tiled=True)]
    all_to_all x1 -> x0, waiting for transfers between devices: 74.7 us -> none  [body(): lax.all_to_all(partials, 'seq', split_axis=0, concat_axis=0, tiled=True)]
    psum x1 -> x0, waiting for transfers between devices: 66.9 us -> none  [body(): lax.psum(partial_value.astype(jnp.bfloat16), 'exp').astype(jnp.float32)]
    ppermute x0 -> x45, starting transfers between devices: none -> 65.1 us  [the longest x9 29.4 us: line_scatter(): from_left = lax.ppermute(to_right, 'exp', [(i, i + 1) for i in range(step)])]
    all_gather x1 -> x0, waiting for transfers between devices: 38.6 us -> none  [body(): shards = lax.all_gather(end_state[None], 'seq', axis=0, tiled=True)]
    reduce_scatter x1 -> x0, waiting for transfers between devices: 32.7 us -> none  [body(): lax.psum_scatter(expert_mix.astype(jnp.bfloat16), 'exp', scatter_dimensio...]
  transfers between devices with their start and end apart: 4 -> 45, of which waited for: 4 -> 25; matrix products, arithmetic and copies ran while one was open for 1% -> 3% of each run, Pallas kernels for 0% -> 0%
where the time goes in v1:
time: 285 us; the launch traced here: 284 us
  waiting for transfers between devices  151 us (53%)
  starting transfers between devices  65.1 us (23%)
  matrix products  31.4 us (11%)
  local copies, waits for them, and re-layouts  16.4 us (6%)
  other arithmetic  15.3 us (5%)
  between operations  4.85 us (2%)
    ppermute x7, waiting for transfers between devices, body(): block = lax.ppermute(block, 'seq', xor_pairs(seq_count, 2 * g + b))  34.1 us
    ppermute x7, waiting for transfers between devices, body(): block = lax.ppermute(block, 'seq', xor_pairs(seq_count, i))  30.3 us
    ppermute x9, starting transfers between devices, line_scatter(): from_left = lax.ppermute(to_right, 'exp', [(i, i + 1) for i in range(step)])  29.4 us
    ppermute x9, waiting for transfers between devices, line_scatter(): from_left = lax.ppermute(to_right, 'exp', [(i, i + 1) for i in range(step)])  23.8 us
    ppermute x9, waiting for transfers between devices, line_scatter(): lax.ppermute(to_left, 'exp', [(count - 1 - i, count - 2 - i) for i in ran...  21.2 us
    ppermute x3, waiting for transfers between devices, line_gather(): lax.ppermute(right, 'exp', [(i + 1, i) for i in range(0, count - step)])  19.9 us
    ppermute x9, starting transfers between devices, line_scatter(): lax.ppermute(to_left, 'exp', [(count - 1 - i, count - 2 - i) for i in ran...  8.07 us
    ppermute x7, starting transfers between devices, body(): block = lax.ppermute(block, 'seq', xor_pairs(seq_count, 2 * g + b))  7.03 us
  transfers between devices with their start and end apart: 45, of which 25 were waited for; matrix products, arithmetic and copies ran while one was open for 3% of the time, Pallas kernels for 0%

profile of v1, /device:TPU:0, one launch (start us, length us, event | category | flops | bytes accessed | tf_op | source)
XLA Modules:
  0.0 284.4 jit_solution(11674599723823111914)
XLA Ops:
  1.6 1.4 fusion.70
  3.7 1.2 copy.40
  5.0 1.2 compare_convert_fusion.1
  6.2 1.7 convolution_convert_fusion.4
  12.6 3.5 %collective-permute-start.3 = (bf16[4,128,128]{2,1,0:T(8,128)(2,1)S(1)}, bf16[4,128,128]{2,1,0:T(8,128)(2,1)S(1)}, u32[]{:S(2)}, u32[]{:S(2)}) collective-permute-start(bf16[4,128,128]{2,1,0:T(8,128)(2,1)S(1)} %fusion.60), channel_id=1, source_target_pairs={{0,24},{4,28},{8,16},{12,20},{16,8},{20,12},{24,0},{28,4},{1,25},{... | collective-permute-start | bytes 393224 | tf_op jit(solution)/shard_map/ppermute | solution.py:117
  17.4 3.0 %collective-permute-done.3 = bf16[4,128,128]{2,1,0:T(8,128)(2,1)S(1)} collective-permute-done((bf16[4,128,128]{2,1,0:T(8,128)(2,1)S(1)}, bf16[4,128,128]{2,1,0:T(8,128)(2,1)S(1)}, u32[]{:S(2)}, u32[]{:S(2)}) %collective-permute-start.3) | collective-permute-done | bytes 131104 | tf_op jit(solution)/shard_map/ppermute | solution.py:117
  20.4 2.7 collective-permute-done.2
  23.8 1.2 collective-permute-done.4
  25.6 2.0 multiply_reduce_fusion.2
  27.7 4.6 %convolution_convert_fusion.1 = bf16[256,3072]{1,0:T(8,128)(2,1)S(1)} fusion(bf16[256,1024]{0,1:T(8,128)(2,1)S(1)} %bitcast.72, bf16[1024,3072]{1,0:T(8,128)(2,1)} %param.18), kind=kOutput, calls=%fused_computation.9 | convolution fusion | flops 1611399168 | bytes 8388608 | tf_op jit(solution)/shard_map/dot_general | solution.py:168
  32.4 3.5 %collective-permute-start.5 = (bf16[64,3072]{1,0:T(8,128)(2,1)S(1)}, bf16[64,3072]{1,0:T(8,128)(2,1)S(1)}, u32[]{:S(2)}, u32[]{:S(2)}) collective-permute-start(bf16[64,3072]{1,0:T(8,128)(2,1)S(1)} %get-tuple-element.36), channel_id=1, source_target_pairs={{0,1},{4,5},{8,9},{12,13},{16,17},{20,21},{24,25},{28,29}} | collective-permute-start | bytes 1179656 | tf_op jit(solution)/shard_map/ppermute | solution.py:27
  36.6 7.9 %collective-permute-done.5 = bf16[64,3072]{1,0:T(8,128)(2,1)S(1)} collective-permute-done((bf16[64,3072]{1,0:T(8,128)(2,1)S(1)}, bf16[64,3072]{1,0:T(8,128)(2,1)S(1)}, u32[]{:S(2)}, u32[]{:S(2)}) %collective-permute-start.5) | collective-permute-done | bytes 393248 | tf_op jit(solution)/shard_map/ppermute | solution.py:27
  44.6 4.4 %collective-permute-start.6 = (bf16[64,3072]{1,0:T(8,128)(2,1)S(1)}, bf16[64,3072]{1,0:T(8,128)(2,1)S(1)}, u32[]{:S(2)}, u32[]{:S(2)}) collective-permute-start(bf16[64,3072]{1,0:T(8,128)(2,1)S(1)} %add_convert_fusion.5), channel_id=1, source_target_pairs={{0,1},{1,2},{4,5},{5,6},{8,9},{9,10},{12,13},{13,14},{16,17},{17,1... | collective-permute-start | bytes 1179656 | tf_op jit(solution)/shard_map/ppermute | solution.py:27
  49.8 7.0 %collective-permute-done.6 = bf16[64,3072]{1,0:T(8,128)(2,1)S(1)} collective-permute-done((bf16[64,3072]{1,0:T(8,128)(2,1)S(1)}, bf16[64,3072]{1,0:T(8,128)(2,1)S(1)}, u32[]{:S(2)}, u32[]{:S(2)}) %collective-permute-start.6) | collective-permute-done | bytes 393248 | tf_op jit(solution)/shard_map/ppermute | solution.py:27
  56.9 1.2 add_convert_fusion.4
  58.7 5.0 %collective-permute-start.7 = (bf16[64,3072]{1,0:T(8,128)(2,1)S(1)}, bf16[64,3072]{1,0:T(8,128)(2,1)S(1)}, u32[]{:S(2)}, u32[]{:S(2)}) collective-permute-start(bf16[64,3072]{1,0:T(8,128)(2,1)S(1)} %get-tuple-element.34), channel_id=1, source_target_pairs={{0,1},{1,2},{2,3},{4,5},{5,6},{6,7},{8,9},{9,10},{10,11},{12,13},{... | collective-permute-start | bytes 1179656 | tf_op jit(solution)/shard_map/ppermute | solution.py:27
  63.9 1.3 collective-permute-start.10
  65.2 5.5 %collective-permute-done.7 = bf16[64,3072]{1,0:T(8,128)(2,1)S(1)} collective-permute-done((bf16[64,3072]{1,0:T(8,128)(2,1)S(1)}, bf16[64,3072]{1,0:T(8,128)(2,1)S(1)}, u32[]{:S(2)}, u32[]{:S(2)}) %collective-permute-start.7) | collective-permute-done | bytes 393248 | tf_op jit(solution)/shard_map/ppermute | solution.py:27
  70.7 9.9 %collective-permute-done.10 = bf16[64,3072]{1,0:T(8,128)(2,1)S(1)} collective-permute-done((bf16[64,3072]{1,0:T(8,128)(2,1)S(1)}, bf16[64,3072]{1,0:T(8,128)(2,1)S(1)}, u32[]{:S(2)}, u32[]{:S(2)}) %collective-permute-start.10) | collective-permute-done | bytes 393248 | tf_op jit(solution)/shard_map/ppermute | solution.py:28
  80.6 1.2 add_convert_fusion.1
  81.8 3.7 %collective-permute-start.11 = (bf16[64,3072]{1,0:T(8,128)(2,1)S(1)}, bf16[64,3072]{1,0:T(8,128)(2,1)S(1)}, u32[]{:S(2)}, u32[]{:S(2)}) collective-permute-start(bf16[64,3072]{1,0:T(8,128)(2,1)S(1)} %add_convert_fusion.1), channel_id=1, source_target_pairs={{0,1},{1,2},{2,3},{4,5},{5,6},{6,7},{8,9},{9,10},{10,11},{12,13},{... | collective-permute-start | bytes 1179656 | tf_op jit(solution)/shard_map/ppermute | solution.py:42
  85.5 1.3 collective-permute-start.14
  86.8 3.9 %collective-permute-done.11 = bf16[64,3072]{1,0:T(8,128)(2,1)S(1)} collective-permute-done((bf16[64,3072]{1,0:T(8,128)(2,1)S(1)}, bf16[64,3072]{1,0:T(8,128)(2,1)S(1)}, u32[]{:S(2)}, u32[]{:S(2)}) %collective-permute-start.11) | collective-permute-done | bytes 393248 | tf_op jit(solution)/shard_map/ppermute | solution.py:42
  91.7 3.8 %collective-permute-done.14 = bf16[64,3072]{1,0:T(8,128)(2,1)S(1)} collective-permute-done((bf16[64,3072]{1,0:T(8,128)(2,1)S(1)}, bf16[64,3072]{1,0:T(8,128)(2,1)S(1)}, u32[]{:S(2)}, u32[]{:S(2)}) %collective-permute-start.14) | collective-permute-done | bytes 393248 | tf_op jit(solution)/shard_map/ppermute | solution.py:43
  95.5 1.3 collective-permute-start.15
  97.5 9.1 %collective-permute-done.15 = bf16[64,3072]{1,0:T(8,128)(2,1)S(1)} collective-permute-done((bf16[64,3072]{1,0:T(8,128)(2,1)S(1)}, bf16[64,3072]{1,0:T(8,128)(2,1)S(1)}, u32[]{:S(2)}, u32[]{:S(2)}) %collective-permute-start.15) | collective-permute-done | bytes 393248 | tf_op jit(solution)/shard_map/ppermute | solution.py:43
  106.6 1.5 collective-permute-start.16
  109.3 7.0 %collective-permute-done.16 = bf16[64,3072]{1,0:T(8,128)(2,1)S(1)} collective-permute-done((bf16[64,3072]{1,0:T(8,128)(2,1)S(1)}, bf16[64,3072]{1,0:T(8,128)(2,1)S(1)}, u32[]{:S(2)}, u32[]{:S(2)}) %collective-permute-start.16) | collective-permute-done | bytes 393248 | tf_op jit(solution)/shard_map/ppermute | solution.py:43
  117.2 1.2 fusion.80
  119.3 1.1 collective-permute-done.17
  120.6 1.6 collective-permute-start.18
  124.8 1.4 collective-permute-start.22
  126.2 1.0 constant_dynamic-update-slice_fusion.13
  127.2 5.9 %collective-permute-done.18 = bf16[136,1536]{1,0:T(8,128)(2,1)S(1)} collective-permute-done((bf16[136,1536]{1,0:T(8,128)(2,1)S(1)}, bf16[136,1536]{1,0:T(8,128)(2,1)S(1)}, u32[]{:S(2)}, u32[]{:S(2)}) %collective-permute-start.18) | collective-permute-done | bytes 417824 | tf_op jit(solution)/shard_map/ppermute | solution.py:203
  133.1 1.4 collective-permute-start.20
  134.6 15.5 %collective-permute-done.19 = bf16[136,1536]{1,0:T(8,128)(2,1)S(1)} collective-permute-done((bf16[136,1536]{1,0:T(8,128)(2,1)S(1)}, bf16[136,1536]{1,0:T(8,128)(2,1)S(1)}, u32[]{:S(2)}, u32[]{:S(2)}) %collective-permute-start.19) | collective-permute-done | bytes 417824 | tf_op jit(solution)/shard_map/ppermute | solution.py:203
  150.2 11.6 %collective-permute-done.20 = bf16[136,1536]{1,0:T(8,128)(2,1)S(1)} collective-permute-done((bf16[136,1536]{1,0:T(8,128)(2,1)S(1)}, bf16[136,1536]{1,0:T(8,128)(2,1)S(1)}, u32[]{:S(2)}, u32[]{:S(2)}) %collective-permute-start.20) | collective-permute-done | bytes 417824 | tf_op jit(solution)/shard_map/ppermute | solution.py:203
  162.2 5.9 %collective-permute-done.24 = bf16[1088,1536]{1,0:T(8,128)(2,1)S(1)} collective-permute-done((bf16[1088,1536]{1,0:T(8,128)(2,1)S(1)}, bf16[1088,1536]{1,0:T(8,128)(2,1)S(1)}, u32[]{:S(2)}, u32[]{:S(2)}) %collective-permute-start.24) | collective-permute-done | bytes 3342368 | tf_op jit(solution)/shard_map/ppermute | solution.py:207
  168.5 1.4 multiply_reduce_fusion
  170.6 5.4 %fusion.5 = f32[1088,640]{1,0:T(8,128)S(1)} fusion(bf16[1,3072,640]{2,1,0:T(8,128)(2,1)S(1)} %copy-done.13, bf16[1088,1536]{1,0:T(8,128)(2,1)S(1)} %get-tuple-element.14, bf16[1088,1536]{1,0:T(8,128)(2,1)S(1)} %get-tuple-element.13, f32[1088]{0:T(1024)S(1)} %add_rsqrt_fusion), kind=kOutput, calls=%fused_computation.10 | convolution fusion | flops 4292255744 | bytes 13406464 | tf_op jit(solution)/shard_map/dot_general | solution.py:215
  176.1 5.9 %multiply_convert_fusion = bf16[1088,640]{1,0:T(8,128)(2,1)S(1)} fusion(f32[1088,640]{1,0:T(8,128)S(1)} %fusion.5, bf16[1,3072,640]{2,1,0:T(8,128)(2,1)S(1)} %copy-done.14, bf16[1088,1536]{1,0:T(8,128)(2,1)S(1)} %get-tuple-element.14, bf16[1088,1536]{1,0:T(8,128)(2,1)S(1)} %get-tuple-element.13, f32[1088]{0:T(1024)S(1)} %add_rsqrt_fusion), kind=kOutput, calls=%fused_computation.23 | convolution fusion | flops 4296433664 | bytes 14799104 | tf_op jit(solution)/shard_map/dot_general | solution.py:216
  182.0 5.6 %convolution_convert_fusion = bf16[1088,3072]{1,0:T(8,128)(2,1)S(1)} fusion(bf16[1088,640]{1,0:T(8,128)(2,1)S(1)} %multiply_convert_fusion, bf16[1,640,3072]{2,1,0:T(8,128)(2,1)S(1)} %copy-done.15), kind=kOutput, calls=%fused_computation.1 | convolution fusion | flops 4281532416 | bytes 12009472 | tf_op jit(solution)/shard_map/dot_general | solution.py:218
  187.7 2.3 constant_dynamic-slice_fusion.4
  190.0 1.4 copy-done.2
  191.4 4.0 %rev.6 = bf16[4,2,136,1536]{3,2,1,0:T(8,128)(2,1)} reverse(bf16[4,2,136,1536]{3,2,1,0:T(8,128)(2,1)} %bitcast.71), dimensions={1} | reverse | bytes 6684672 | tf_op jit(solution)/shard_map/rev | solution.py:222
  196.6 5.1 %collective-permute-done.25 = bf16[1088,1536]{1,0:T(8,128)(2,1)} collective-permute-done((bf16[1088,1536]{1,0:T(8,128)(2,1)}, bf16[1088,1536]{1,0:T(8,128)(2,1)}, u32[]{:S(2)}, u32[]{:S(2)}) %collective-permute-start.25) | collective-permute-done | bytes 3342368 | tf_op jit(solution)/shard_map/ppermute | solution.py:223
  201.6 3.9 %add_convert_fusion = bf16[1088,1536]{1,0:T(8,128)(2,1)S(1)} fusion(bf16[1088,1536]{1,0:T(8,128)(2,1)} %collective-permute-done.25, bf16[1088,3072]{1,0:T(8,128)(2,1)} %copy-done.2, s32[]{:T(128)S(6)} %select_n.216), kind=kLoop, calls=%fused_computation.3 | loop fusion | flops 6684672 | bytes 10027012 | tf_op jit(solution)/shard_map/convert_element_type | solution.py:224
  206.8 1.0 collective-permute-start.38
  207.8 1.4 collective-permute-start.37
  209.2 1.5 collective-permute-start.28
  211.5 6.0 %collective-permute-done.36 = bf16[136,1536]{1,0:T(8,128)(2,1)S(1)} collective-permute-done((bf16[136,1536]{1,0:T(8,128)(2,1)S(1)}, bf16[136,1536]{1,0:T(8,128)(2,1)S(1)}, u32[]{:S(2)}, u32[]{:S(2)}) %collective-permute-start.36) | collective-permute-done | bytes 417824 | tf_op jit(solution)/shard_map/ppermute | solution.py:231
  218.3 18.9 %collective-permute-done.37 = bf16[136,1536]{1,0:T(8,128)(2,1)S(1)} collective-permute-done((bf16[136,1536]{1,0:T(8,128)(2,1)S(1)}, bf16[136,1536]{1,0:T(8,128)(2,1)S(1)}, u32[]{:S(2)}, u32[]{:S(2)}) %collective-permute-start.37) | collective-permute-done | bytes 417824 | tf_op jit(solution)/shard_map/ppermute | solution.py:231
  239.1 1.5 collective-permute-start.39
  241.2 5.4 %collective-permute-done.27 = bf16[136,1536]{1,0:T(8,128)(2,1)S(1)} collective-permute-done((bf16[136,1536]{1,0:T(8,128)(2,1)S(1)}, bf16[136,1536]{1,0:T(8,128)(2,1)S(1)}, u32[]{:S(2)}, u32[]{:S(2)}) %collective-permute-start.27) | collective-permute-done | bytes 417824 | tf_op jit(solution)/shard_map/ppermute | solution.py:231
  248.4 1.5 collective-permute-start.29
  250.7 1.3 collective-permute-start.40
  252.0 3.1 %collective-permute-done.29 = bf16[64,1536]{1,0:T(8,128)(2,1)S(1)} collective-permute-done((bf16[64,1536]{1,0:T(8,128)(2,1)S(1)}, bf16[64,1536]{1,0:T(8,128)(2,1)S(1)}, u32[]{:S(2)}, u32[]{:S(2)}) %collective-permute-start.29) | collective-permute-done | bytes 196640 | tf_op jit(solution)/shard_map/ppermute | solution.py:27
  255.2 4.5 %collective-permute-start.30 = (bf16[64,1536]{1,0:T(8,128)(2,1)S(1)}, bf16[64,1536]{1,0:T(8,128)(2,1)S(1)}, u32[]{:S(2)}, u32[]{:S(2)}) collective-permute-start(bf16[64,1536]{1,0:T(8,128)(2,1)S(1)} %add_convert_fusion.13), channel_id=1, source_target_pairs={{0,1},{1,2},{4,5},{5,6},{8,9},{9,10},{12,13},{13,14},{16,17},{17,1... | collective-permute-start | bytes 589832 | tf_op jit(solution)/shard_map/ppermute | solution.py:27
  259.9 3.3 %collective-permute-start.41 = (bf16[64,1536]{1,0:T(8,128)(2,1)S(1)}, bf16[64,1536]{1,0:T(8,128)(2,1)S(1)}, u32[]{:S(2)}, u32[]{:S(2)}) collective-permute-start(bf16[64,1536]{1,0:T(8,128)(2,1)S(1)} %get-tuple-element.38), channel_id=1, source_target_pairs={{0,1},{1,2},{2,3},{4,5},{5,6},{6,7},{8,9},{9,10},{10,11},{12,13},{... | collective-permute-start | bytes 589832 | tf_op jit(solution)/shard_map/ppermute | solution.py:27
  264.3 4.4 %collective-permute-start.31 = (bf16[64,1536]{1,0:T(8,128)(2,1)S(1)}, bf16[64,1536]{1,0:T(8,128)(2,1)S(1)}, u32[]{:S(2)}, u32[]{:S(2)}) collective-permute-start(bf16[64,1536]{1,0:T(8,128)(2,1)S(1)} %get-tuple-element.42), channel_id=1, source_target_pairs={{0,1},{1,2},{2,3},{4,5},{5,6},{6,7},{8,9},{9,10},{10,11},{12,13},{... | collective-permute-start | bytes 589832 | tf_op jit(solution)/shard_map/ppermute | solution.py:27
  269.4 1.3 collective-permute-start.44
  270.8 1.3 collective-permute-start.34
  272.1 5.3 %collective-permute-done.44 = bf16[64,1536]{1,0:T(8,128)(2,1)S(1)} collective-permute-done((bf16[64,1536]{1,0:T(8,128)(2,1)S(1)}, bf16[64,1536]{1,0:T(8,128)(2,1)S(1)}, u32[]{:S(2)}, u32[]{:S(2)}) %collective-permute-start.44) | collective-permute-done | bytes 196640 | tf_op jit(solution)/shard_map/ppermute | solution.py:28
  277.5 5.9 %collective-permute-done.34 = bf16[64,1536]{1,0:T(8,128)(2,1)S(1)} collective-permute-done((bf16[64,1536]{1,0:T(8,128)(2,1)S(1)}, bf16[64,1536]{1,0:T(8,128)(2,1)S(1)}, u32[]{:S(2)}, u32[]{:S(2)}) %collective-permute-start.34) | collective-permute-done | bytes 196640 | tf_op jit(solution)/shard_map/ppermute | solution.py:28
  (152 shorter events, 29.3 us)
Async XLA Ops:
  0.0 25.2 %copy-start = (bf16[256,1024]{1,0:T(8,128)(2,1)S(1)}, bf16[256,1024]{1,0:T(8,128)(2,1)}, u32[]{:S(2)}) copy-start(bf16[256,1024]{1,0:T(8,128)(2,1)} %param.13) | copy-start | bytes 1572868
  8.0 4.5 %collective-permute-start = (bf16[8,128,128]{2,1,0:T(8,128)(2,1)S(1)}, bf16[8,128,128]{2,1,0:T(8,128)(2,1)S(1)}, u32[]{:S(2)}, u32[]{:S(2)}) collective-permute-start(bf16[8,128,128]{2,1,0:T(8,128)(2,1)S(1)} %convolution_convert_fusion.4), channel_id=1, source_target_pairs={{0,4},{4,0},{8,12},{12,8},{16,20},{20,16},{24,28},{28,24},{1,5},{5... | collective-permute-start | bytes 786440 | tf_op jit(solution)/shard_map/ppermute | solution.py:99
  12.6 7.8 %collective-permute-start.3 = (bf16[4,128,128]{2,1,0:T(8,128)(2,1)S(1)}, bf16[4,128,128]{2,1,0:T(8,128)(2,1)S(1)}, u32[]{:S(2)}, u32[]{:S(2)}) collective-permute-start(bf16[4,128,128]{2,1,0:T(8,128)(2,1)S(1)} %fusion.60), channel_id=1, source_target_pairs={{0,24},{4,28},{8,16},{12,20},{16,8},{20,12},{24,0},{28,4},{1,25},{... | collective-permute-start | bytes 393224 | tf_op jit(solution)/shard_map/ppermute | solution.py:117
  16.1 6.9 %collective-permute-start.2 = (bf16[4,128,128]{2,1,0:T(8,128)(2,1)S(1)}, bf16[4,128,128]{2,1,0:T(8,128)(2,1)S(1)}, u32[]{:S(2)}, u32[]{:S(2)}) collective-permute-start(bf16[4,128,128]{2,1,0:T(8,128)(2,1)S(1)} %fusion.60), channel_id=1, source_target_pairs={{0,16},{4,20},{8,24},{12,28},{16,0},{20,4},{24,8},{28,12},{1,17},{... | collective-permute-start | bytes 393224 | tf_op jit(solution)/shard_map/ppermute | solution.py:117
  16.7 6.7 %collective-permute-start.1 = (bf16[4,128,128]{2,1,0:T(8,128)(2,1)S(1)}, bf16[4,128,128]{2,1,0:T(8,128)(2,1)S(1)}, u32[]{:S(2)}, u32[]{:S(2)}) collective-permute-start(bf16[4,128,128]{2,1,0:T(8,128)(2,1)S(1)} %fusion.60), channel_id=1, source_target_pairs={{0,8},{4,12},{8,0},{12,4},{16,24},{20,28},{24,16},{28,20},{1,9},{5... | collective-permute-start | bytes 393224 | tf_op jit(solution)/shard_map/ppermute | solution.py:117
  23.6 1.4 collective-permute-start.4
  32.4 12.2 %collective-permute-start.5 = (bf16[64,3072]{1,0:T(8,128)(2,1)S(1)}, bf16[64,3072]{1,0:T(8,128)(2,1)S(1)}, u32[]{:S(2)}, u32[]{:S(2)}) collective-permute-start(bf16[64,3072]{1,0:T(8,128)(2,1)S(1)} %get-tuple-element.36), channel_id=1, source_target_pairs={{0,1},{4,5},{8,9},{12,13},{16,17},{20,21},{24,25},{28,29}} | collective-permute-start | bytes 1179656 | tf_op jit(solution)/shard_map/ppermute | solution.py:27
  35.9 55.5 %copy-start.11 = (s32[256,2]{0,1:T(2,128)S(1)}, s32[256,2]{0,1:T(2,128)}, u32[]{:S(2)}) copy-start(s32[256,2]{0,1:T(2,128)} %param.23) | copy-start | bytes 6148
  35.9 13.2 %collective-permute-start.8 = (bf16[64,3072]{1,0:T(8,128)(2,1)S(1)}, bf16[64,3072]{1,0:T(8,128)(2,1)S(1)}, u32[]{:S(2)}, u32[]{:S(2)}) collective-permute-start(bf16[64,3072]{1,0:T(8,128)(2,1)S(1)} %get-tuple-element.37), channel_id=1, source_target_pairs={{3,2},{7,6},{11,10},{15,14},{19,18},{23,22},{27,26},{31,30}} | collective-permute-start | bytes 1179656 | tf_op jit(solution)/shard_map/ppermute | solution.py:28
  44.6 12.2 %collective-permute-start.6 = (bf16[64,3072]{1,0:T(8,128)(2,1)S(1)}, bf16[64,3072]{1,0:T(8,128)(2,1)S(1)}, u32[]{:S(2)}, u32[]{:S(2)}) collective-permute-start(bf16[64,3072]{1,0:T(8,128)(2,1)S(1)} %add_convert_fusion.5), channel_id=1, source_target_pairs={{0,1},{1,2},{4,5},{5,6},{8,9},{9,10},{12,13},{13,14},{16,17},{17,1... | collective-permute-start | bytes 1179656 | tf_op jit(solution)/shard_map/ppermute | solution.py:27
  49.1 0.7 copy-start.10
  58.0 5.7 %collective-permute-start.9 = (bf16[64,3072]{1,0:T(8,128)(2,1)S(1)}, bf16[64,3072]{1,0:T(8,128)(2,1)S(1)}, u32[]{:S(2)}, u32[]{:S(2)}) collective-permute-start(bf16[64,3072]{1,0:T(8,128)(2,1)S(1)} %get-tuple-element.35), channel_id=1, source_target_pairs={{3,2},{2,1},{7,6},{6,5},{11,10},{10,9},{15,14},{14,13},{19,18},{18... | collective-permute-start | bytes 1179656 | tf_op jit(solution)/shard_map/ppermute | solution.py:28
  58.7 11.9 %collective-permute-start.7 = (bf16[64,3072]{1,0:T(8,128)(2,1)S(1)}, bf16[64,3072]{1,0:T(8,128)(2,1)S(1)}, u32[]{:S(2)}, u32[]{:S(2)}) collective-permute-start(bf16[64,3072]{1,0:T(8,128)(2,1)S(1)} %get-tuple-element.34), channel_id=1, source_target_pairs={{0,1},{1,2},{2,3},{4,5},{5,6},{6,7},{8,9},{9,10},{10,11},{12,13},{... | collective-permute-start | bytes 1179656 | tf_op jit(solution)/shard_map/ppermute | solution.py:27
  63.9 16.7 %collective-permute-start.10 = (bf16[64,3072]{1,0:T(8,128)(2,1)S(1)}, bf16[64,3072]{1,0:T(8,128)(2,1)S(1)}, u32[]{:S(2)}, u32[]{:S(2)}) collective-permute-start(bf16[64,3072]{1,0:T(8,128)(2,1)S(1)} %add_convert_fusion.2), channel_id=1, source_target_pairs={{3,2},{2,1},{1,0},{7,6},{6,5},{5,4},{11,10},{10,9},{9,8},{15,14},{... | collective-permute-start | bytes 1179656 | tf_op jit(solution)/shard_map/ppermute | solution.py:28
  81.8 35.4 %copy-start.3 = (bf16[64,3072]{1,0:T(8,128)(2,1)}, bf16[64,3072]{1,0:T(8,128)(2,1)S(1)}, u32[]{:S(2)}) copy-start(bf16[64,3072]{1,0:T(8,128)(2,1)S(1)} %add_convert_fusion.1) | copy-start | bytes 1179652
  81.8 8.9 %collective-permute-start.11 = (bf16[64,3072]{1,0:T(8,128)(2,1)S(1)}, bf16[64,3072]{1,0:T(8,128)(2,1)S(1)}, u32[]{:S(2)}, u32[]{:S(2)}) collective-permute-start(bf16[64,3072]{1,0:T(8,128)(2,1)S(1)} %add_convert_fusion.1), channel_id=1, source_target_pairs={{0,1},{1,2},{2,3},{4,5},{5,6},{6,7},{8,9},{9,10},{10,11},{12,13},{... | collective-permute-start | bytes 1179656 | tf_op jit(solution)/shard_map/ppermute | solution.py:42
  85.5 10.0 %collective-permute-start.14 = (bf16[64,3072]{1,0:T(8,128)(2,1)S(1)}, bf16[64,3072]{1,0:T(8,128)(2,1)S(1)}, u32[]{:S(2)}, u32[]{:S(2)}) collective-permute-start(bf16[64,3072]{1,0:T(8,128)(2,1)S(1)} %add_convert_fusion.1), channel_id=1, source_target_pairs={{1,0},{2,1},{3,2},{5,4},{6,5},{7,6},{9,8},{10,9},{11,10},{13,12},{... | collective-permute-start | bytes 1179656 | tf_op jit(solution)/shard_map/ppermute | solution.py:43
  90.7 17.3 %copy-start.9 = (bf16[64,3072]{1,0:T(8,128)(2,1)}, bf16[64,3072]{1,0:T(8,128)(2,1)S(1)}, u32[]{:S(2)}) copy-start(bf16[64,3072]{1,0:T(8,128)(2,1)S(1)} %collective-permute-done.11) | copy-start | bytes 1179652
  90.7 6.1 %collective-permute-start.12 = (bf16[64,3072]{1,0:T(8,128)(2,1)S(1)}, bf16[64,3072]{1,0:T(8,128)(2,1)S(1)}, u32[]{:S(2)}, u32[]{:S(2)}) collective-permute-start(bf16[64,3072]{1,0:T(8,128)(2,1)S(1)} %collective-permute-done.11), channel_id=1, source_target_pairs={{1,2},{2,3},{5,6},{6,7},{9,10},{10,11},{13,14},{14,15},{17,18},{18... | collective-permute-start | bytes 1179656 | tf_op jit(solution)/shard_map/ppermute | solution.py:42
  95.5 11.1 %collective-permute-start.15 = (bf16[64,3072]{1,0:T(8,128)(2,1)S(1)}, bf16[64,3072]{1,0:T(8,128)(2,1)S(1)}, u32[]{:S(2)}, u32[]{:S(2)}) collective-permute-start(bf16[64,3072]{1,0:T(8,128)(2,1)S(1)} %collective-permute-done.14), channel_id=1, source_target_pairs={{1,0},{2,1},{5,4},{6,5},{9,8},{10,9},{13,12},{14,13},{17,16},{18,1... | collective-permute-start | bytes 1179656 | tf_op jit(solution)/shard_map/ppermute | solution.py:43
  96.8 11.3 %collective-permute-start.13 = (bf16[64,3072]{1,0:T(8,128)(2,1)S(1)}, bf16[64,3072]{1,0:T(8,128)(2,1)S(1)}, u32[]{:S(2)}, u32[]{:S(2)}) collective-permute-start(bf16[64,3072]{1,0:T(8,128)(2,1)S(1)} %collective-permute-done.12), channel_id=1, source_target_pairs={{2,3},{6,7},{10,11},{14,15},{18,19},{22,23},{26,27},{30,31}} | collective-permute-start | bytes 1179656 | tf_op jit(solution)/shard_map/ppermute | solution.py:42
  106.6 9.7 %collective-permute-start.16 = (bf16[64,3072]{1,0:T(8,128)(2,1)S(1)}, bf16[64,3072]{1,0:T(8,128)(2,1)S(1)}, u32[]{:S(2)}, u32[]{:S(2)}) collective-permute-start(bf16[64,3072]{1,0:T(8,128)(2,1)S(1)} %collective-permute-done.15), channel_id=1, source_target_pairs={{1,0},{5,4},{9,8},{13,12},{17,16},{21,20},{25,24},{29,28}} | collective-permute-start | bytes 1179656 | tf_op jit(solution)/shard_map/ppermute | solution.py:43
  118.4 2.0 collective-permute-start.17
  118.4 3.7 %copy-start.6 = (bf16[136,1536]{1,0:T(8,128)(2,1)S(1)}, bf16[136,1536]{1,0:T(8,128)(2,1)}, u32[]{:S(2)}) copy-start(bf16[136,1536]{1,0:T(8,128)(2,1)} %get-tuple-element.30) | copy-start | bytes 1253380
  118.4 4.6 %copy-start.7 = (bf16[136,1536]{1,0:T(8,128)(2,1)S(1)}, bf16[136,1536]{1,0:T(8,128)(2,1)}, u32[]{:S(2)}) copy-start(bf16[136,1536]{1,0:T(8,128)(2,1)} %get-tuple-element.31) | copy-start | bytes 1253380
  118.4 5.5 %copy-start.8 = (bf16[136,1536]{1,0:T(8,128)(2,1)S(1)}, bf16[136,1536]{1,0:T(8,128)(2,1)}, u32[]{:S(2)}) copy-start(bf16[136,1536]{1,0:T(8,128)(2,1)} %get-tuple-element.32) | copy-start | bytes 1253380
  120.3 4.5 %copy-start.5 = (bf16[136,1536]{1,0:T(8,128)(2,1)}, bf16[136,1536]{1,0:T(8,128)(2,1)S(1)}, u32[]{:S(2)}) copy-start(bf16[136,1536]{1,0:T(8,128)(2,1)S(1)} %collective-permute-done.17) | copy-start | bytes 1253380
  120.6 12.5 %collective-permute-start.18 = (bf16[136,1536]{1,0:T(8,128)(2,1)S(1)}, bf16[136,1536]{1,0:T(8,128)(2,1)S(1)}, u32[]{:S(2)}, u32[]{:S(2)}) collective-permute-start(bf16[136,1536]{1,0:T(8,128)(2,1)S(1)} %get-tuple-element.29), channel_id=1, source_target_pairs={{0,8},{4,12},{8,0},{12,4},{16,24},{20,28},{24,16},{28,20},{1,9},{5... | collective-permute-start | bytes 1253384 | tf_op jit(solution)/shard_map/ppermute | solution.py:203
  122.1 39.8 %collective-permute-start.23 = (bf16[136,1536]{1,0:T(8,128)(2,1)S(1)}, bf16[136,1536]{1,0:T(8,128)(2,1)S(1)}, u32[]{:S(2)}, u32[]{:S(2)}) collective-permute-start(bf16[136,1536]{1,0:T(8,128)(2,1)S(1)} %copy-done.6), channel_id=1, source_target_pairs={{0,28},{4,24},{8,20},{12,16},{16,12},{20,8},{24,4},{28,0},{1,29},{... | collective-permute-start | bytes 1253384 | tf_op jit(solution)/shard_map/ppermute | solution.py:203
  123.0 38.8 %collective-permute-start.21 = (bf16[136,1536]{1,0:T(8,128)(2,1)S(1)}, bf16[136,1536]{1,0:T(8,128)(2,1)S(1)}, u32[]{:S(2)}, u32[]{:S(2)}) collective-permute-start(bf16[136,1536]{1,0:T(8,128)(2,1)S(1)} %copy-done.7), channel_id=1, source_target_pairs={{0,20},{4,16},{8,28},{12,24},{16,4},{20,0},{24,12},{28,8},{1,21},{... | collective-permute-start | bytes 1253384 | tf_op jit(solution)/shard_map/ppermute | solution.py:203
  123.8 26.2 %collective-permute-start.19 = (bf16[136,1536]{1,0:T(8,128)(2,1)S(1)}, bf16[136,1536]{1,0:T(8,128)(2,1)S(1)}, u32[]{:S(2)}, u32[]{:S(2)}) collective-permute-start(bf16[136,1536]{1,0:T(8,128)(2,1)S(1)} %copy-done.8), channel_id=1, source_target_pairs={{0,12},{4,8},{8,4},{12,0},{16,28},{20,24},{24,20},{28,16},{1,13},{... | collective-permute-start | bytes 1253384 | tf_op jit(solution)/shard_map/ppermute | solution.py:203
  124.8 37.1 %collective-permute-start.22 = (bf16[136,1536]{1,0:T(8,128)(2,1)S(1)}, bf16[136,1536]{1,0:T(8,128)(2,1)S(1)}, u32[]{:S(2)}, u32[]{:S(2)}) collective-permute-start(bf16[136,1536]{1,0:T(8,128)(2,1)S(1)} %get-tuple-element.27), channel_id=1, source_target_pairs={{0,24},{4,28},{8,16},{12,20},{16,8},{20,12},{24,0},{28,4},{1,25},{... | collective-permute-start | bytes 1253384 | tf_op jit(solution)/shard_map/ppermute | solution.py:203
  133.1 28.7 %collective-permute-start.20 = (bf16[136,1536]{1,0:T(8,128)(2,1)S(1)}, bf16[136,1536]{1,0:T(8,128)(2,1)S(1)}, u32[]{:S(2)}, u32[]{:S(2)}) collective-permute-start(bf16[136,1536]{1,0:T(8,128)(2,1)S(1)} %get-tuple-element.28), channel_id=1, source_target_pairs={{0,16},{4,20},{8,24},{12,28},{16,0},{20,4},{24,8},{28,12},{1,17},{... | collective-permute-start | bytes 1253384 | tf_op jit(solution)/shard_map/ppermute | solution.py:203
  162.1 6.0 %collective-permute-start.24 = (bf16[1088,1536]{1,0:T(8,128)(2,1)S(1)}, bf16[1088,1536]{1,0:T(8,128)(2,1)S(1)}, u32[]{:S(2)}, u32[]{:S(2)}) collective-permute-start(bf16[1088,1536]{1,0:T(8,128)(2,1)S(1)} %constant_dynamic-update-slice_fusion.14), channel_id=1, source_target_pairs={{0,4},{4,0},{8,12},{12,8},{16,20},{20,16},{24,28},{28,24},{1,5},{5... | collective-permute-start | bytes 10027016 | tf_op jit(solution)/shard_map/ppermute | solution.py:207
  168.5 2.1 copy-start.13
  170.6 5.4 %copy-start.14 = (bf16[1,3072,640]{2,1,0:T(8,128)(2,1)S(1)}, bf16[1,3072,640]{2,1,0:T(8,128)(2,1)}, u32[]{:S(2)}) copy-start(bf16[1,3072,640]{2,1,0:T(8,128)(2,1)} %param.21) | copy-start | bytes 11796484
  176.1 5.9 %copy-start.15 = (bf16[1,640,3072]{2,1,0:T(8,128)(2,1)S(1)}, bf16[1,640,3072]{2,1,0:T(8,128)(2,1)}, u32[]{:S(2)}) copy-start(bf16[1,640,3072]{2,1,0:T(8,128)(2,1)} %param.22) | copy-start | bytes 11796484
  187.7 3.7 %copy-start.2 = (bf16[1088,3072]{1,0:T(8,128)(2,1)}, bf16[1088,3072]{1,0:T(8,128)(2,1)S(1)}, u32[]{:S(2)}) copy-start(bf16[1088,3072]{1,0:T(8,128)(2,1)S(1)} %convolution_convert_fusion) | copy-start | bytes 20054020
  191.4 4.5 %copy-start.12 = (bf16[3072,4]{0,1:T(4,128)(2,1)S(1)}, bf16[3072,4]{0,1:T(4,128)(2,1)}, u32[]{:S(2)}) copy-start(bf16[3072,4]{0,1:T(4,128)(2,1)} %param.19) | copy-start | bytes 73732
  195.4 6.3 %collective-permute-start.25 = (bf16[1088,1536]{1,0:T(8,128)(2,1)}, bf16[1088,1536]{1,0:T(8,128)(2,1)}, u32[]{:S(2)}, u32[]{:S(2)}) collective-permute-start(bf16[1088,1536]{1,0:T(8,128)(2,1)} %bitcast.73), channel_id=1, source_target_pairs={{0,4},{4,0},{8,12},{12,8},{16,20},{20,16},{24,28},{28,24},{1,5},{5... | collective-permute-start | bytes 10027016 | tf_op jit(solution)/shard_map/ppermute | solution.py:223
  205.8 5.0 %collective-permute-start.35 = (bf16[136,1536]{1,0:T(8,128)(2,1)S(1)}, bf16[136,1536]{1,0:T(8,128)(2,1)S(1)}, u32[]{:S(2)}, u32[]{:S(2)}) collective-permute-start(bf16[136,1536]{1,0:T(8,128)(2,1)S(1)} %get-tuple-element.18), channel_id=1, source_target_pairs={{0,4},{4,0},{8,12},{12,8},{16,20},{20,16},{24,28},{28,24},{1,5},{5... | collective-permute-start | bytes 1253384 | tf_op jit(solution)/shard_map/ppermute | solution.py:231
  206.0 11.5 %collective-permute-start.36 = (bf16[136,1536]{1,0:T(8,128)(2,1)S(1)}, bf16[136,1536]{1,0:T(8,128)(2,1)S(1)}, u32[]{:S(2)}, u32[]{:S(2)}) collective-permute-start(bf16[136,1536]{1,0:T(8,128)(2,1)S(1)} %get-tuple-element.17), channel_id=1, source_target_pairs={{0,12},{4,8},{8,4},{12,0},{16,28},{20,24},{24,20},{28,16},{1,13},{... | collective-permute-start | bytes 1253384 | tf_op jit(solution)/shard_map/ppermute | solution.py:231
  206.8 30.5 %collective-permute-start.38 = (bf16[136,1536]{1,0:T(8,128)(2,1)S(1)}, bf16[136,1536]{1,0:T(8,128)(2,1)S(1)}, u32[]{:S(2)}, u32[]{:S(2)}) collective-permute-start(bf16[136,1536]{1,0:T(8,128)(2,1)S(1)} %get-tuple-element.15), channel_id=1, source_target_pairs={{0,28},{4,24},{8,20},{12,16},{16,12},{20,8},{24,4},{28,0},{1,29},{... | collective-permute-start | bytes 1253384 | tf_op jit(solution)/shard_map/ppermute | solution.py:231
  207.8 29.4 %collective-permute-start.37 = (bf16[136,1536]{1,0:T(8,128)(2,1)S(1)}, bf16[136,1536]{1,0:T(8,128)(2,1)S(1)}, u32[]{:S(2)}, u32[]{:S(2)}) collective-permute-start(bf16[136,1536]{1,0:T(8,128)(2,1)S(1)} %get-tuple-element.16), channel_id=1, source_target_pairs={{0,20},{4,16},{8,28},{12,24},{16,4},{20,0},{24,12},{28,8},{1,21},{... | collective-permute-start | bytes 1253384 | tf_op jit(solution)/shard_map/ppermute | solution.py:231
  209.2 32.0 %collective-permute-start.28 = (bf16[136,1536]{1,0:T(8,128)(2,1)S(1)}, bf16[136,1536]{1,0:T(8,128)(2,1)S(1)}, u32[]{:S(2)}, u32[]{:S(2)}) collective-permute-start(bf16[136,1536]{1,0:T(8,128)(2,1)S(1)} %get-tuple-element.19), channel_id=1, source_target_pairs={{0,24},{4,28},{8,16},{12,20},{16,8},{20,12},{24,0},{28,4},{1,25},{... | collective-permute-start | bytes 1253384 | tf_op jit(solution)/shard_map/ppermute | solution.py:231
  210.8 35.9 %collective-permute-start.27 = (bf16[136,1536]{1,0:T(8,128)(2,1)S(1)}, bf16[136,1536]{1,0:T(8,128)(2,1)S(1)}, u32[]{:S(2)}, u32[]{:S(2)}) collective-permute-start(bf16[136,1536]{1,0:T(8,128)(2,1)S(1)} %get-tuple-element.20), channel_id=1, source_target_pairs={{0,16},{4,20},{8,24},{12,28},{16,0},{20,4},{24,8},{28,12},{1,17},{... | collective-permute-start | bytes 1253384 | tf_op jit(solution)/shard_map/ppermute | solution.py:231
  217.5 29.2 %collective-permute-start.26 = (bf16[136,1536]{1,0:T(8,128)(2,1)S(1)}, bf16[136,1536]{1,0:T(8,128)(2,1)S(1)}, u32[]{:S(2)}, u32[]{:S(2)}) collective-permute-start(bf16[136,1536]{1,0:T(8,128)(2,1)S(1)} %get-tuple-element.21), channel_id=1, source_target_pairs={{0,8},{4,12},{8,0},{12,4},{16,24},{20,28},{24,16},{28,20},{1,9},{5... | collective-permute-start | bytes 1253384 | tf_op jit(solution)/shard_map/ppermute | solution.py:231
  239.1 11.6 %collective-permute-start.39 = (bf16[64,1536]{1,0:T(8,128)(2,1)S(1)}, bf16[64,1536]{1,0:T(8,128)(2,1)S(1)}, u32[]{:S(2)}, u32[]{:S(2)}) collective-permute-start(bf16[64,1536]{1,0:T(8,128)(2,1)S(1)} %get-tuple-element.40), channel_id=1, source_target_pairs={{0,1},{4,5},{8,9},{12,13},{16,17},{20,21},{24,25},{28,29}} | collective-permute-start | bytes 589832 | tf_op jit(solution)/shard_map/ppermute | solution.py:27
  240.5 19.2 %collective-permute-start.42 = (bf16[64,1536]{1,0:T(8,128)(2,1)S(1)}, bf16[64,1536]{1,0:T(8,128)(2,1)S(1)}, u32[]{:S(2)}, u32[]{:S(2)}) collective-permute-start(bf16[64,1536]{1,0:T(8,128)(2,1)S(1)} %get-tuple-element.41), channel_id=1, source_target_pairs={{3,2},{7,6},{11,10},{15,14},{19,18},{23,22},{27,26},{31,30}} | collective-permute-start | bytes 589832 | tf_op jit(solution)/shard_map/ppermute | solution.py:28
  248.4 6.8 %collective-permute-start.29 = (bf16[64,1536]{1,0:T(8,128)(2,1)S(1)}, bf16[64,1536]{1,0:T(8,128)(2,1)S(1)}, u32[]{:S(2)}, u32[]{:S(2)}) collective-permute-start(bf16[64,1536]{1,0:T(8,128)(2,1)S(1)} %get-tuple-element.44), channel_id=1, source_target_pairs={{0,1},{4,5},{8,9},{12,13},{16,17},{20,21},{24,25},{28,29}} | collective-permute-start | bytes 589832 | tf_op jit(solution)/shard_map/ppermute | solution.py:27
  249.8 33.7 %copy-start.4 = (bf16[64,3072]{1,0:T(8,128)(2,1)S(1)}, bf16[64,3072]{1,0:T(8,128)(2,1)}, u32[]{:S(2)}) copy-start(bf16[64,3072]{1,0:T(8,128)(2,1)} %copy-done.3) | copy-start | bytes 1179652
  249.8 14.0 %collective-permute-start.32 = (bf16[64,1536]{1,0:T(8,128)(2,1)S(1)}, bf16[64,1536]{1,0:T(8,128)(2,1)S(1)}, u32[]{:S(2)}, u32[]{:S(2)}) collective-permute-start(bf16[64,1536]{1,0:T(8,128)(2,1)S(1)} %get-tuple-element.45), channel_id=1, source_target_pairs={{3,2},{7,6},{11,10},{15,14},{19,18},{23,22},{27,26},{31,30}} | collective-permute-start | bytes 589832 | tf_op jit(solution)/shard_map/ppermute | solution.py:28
  250.7 9.0 %collective-permute-start.40 = (bf16[64,1536]{1,0:T(8,128)(2,1)S(1)}, bf16[64,1536]{1,0:T(8,128)(2,1)S(1)}, u32[]{:S(2)}, u32[]{:S(2)}) collective-permute-start(bf16[64,1536]{1,0:T(8,128)(2,1)S(1)} %add_convert_fusion.9), channel_id=1, source_target_pairs={{0,1},{1,2},{4,5},{5,6},{8,9},{9,10},{12,13},{13,14},{16,17},{17,1... | collective-permute-start | bytes 589832 | tf_op jit(solution)/shard_map/ppermute | solution.py:27
  255.1 29.3 %copy-start.1 = (bf16[256,1024]{1,0:T(8,128)(2,1)S(1)}, bf16[256,1024]{1,0:T(8,128)(2,1)}, u32[]{:S(2)}) copy-start(bf16[256,1024]{1,0:T(8,128)(2,1)} %param.13) | copy-start | bytes 1572868
  255.2 9.0 %collective-permute-start.30 = (bf16[64,1536]{1,0:T(8,128)(2,1)S(1)}, bf16[64,1536]{1,0:T(8,128)(2,1)S(1)}, u32[]{:S(2)}, u32[]{:S(2)}) collective-permute-start(bf16[64,1536]{1,0:T(8,128)(2,1)S(1)} %add_convert_fusion.13), channel_id=1, source_target_pairs={{0,1},{1,2},{4,5},{5,6},{8,9},{9,10},{12,13},{13,14},{16,17},{17,1... | collective-permute-start | bytes 589832 | tf_op jit(solution)/shard_map/ppermute | solution.py:27
  259.9 12.3 %collective-permute-start.41 = (bf16[64,1536]{1,0:T(8,128)(2,1)S(1)}, bf16[64,1536]{1,0:T(8,128)(2,1)S(1)}, u32[]{:S(2)}, u32[]{:S(2)}) collective-permute-start(bf16[64,1536]{1,0:T(8,128)(2,1)S(1)} %get-tuple-element.38), channel_id=1, source_target_pairs={{0,1},{1,2},{2,3},{4,5},{5,6},{6,7},{8,9},{9,10},{10,11},{12,13},{... | collective-permute-start | bytes 589832 | tf_op jit(solution)/shard_map/ppermute | solution.py:27
  263.2 6.2 %collective-permute-start.43 = (bf16[64,1536]{1,0:T(8,128)(2,1)S(1)}, bf16[64,1536]{1,0:T(8,128)(2,1)S(1)}, u32[]{:S(2)}, u32[]{:S(2)}) collective-permute-start(bf16[64,1536]{1,0:T(8,128)(2,1)S(1)} %get-tuple-element.39), channel_id=1, source_target_pairs={{3,2},{2,1},{7,6},{6,5},{11,10},{10,9},{15,14},{14,13},{19,18},{18... | collective-permute-start | bytes 589832 | tf_op jit(solution)/shard_map/ppermute | solution.py:28
  264.3 7.8 %collective-permute-start.31 = (bf16[64,1536]{1,0:T(8,128)(2,1)S(1)}, bf16[64,1536]{1,0:T(8,128)(2,1)S(1)}, u32[]{:S(2)}, u32[]{:S(2)}) collective-permute-start(bf16[64,1536]{1,0:T(8,128)(2,1)S(1)} %get-tuple-element.42), channel_id=1, source_target_pairs={{0,1},{1,2},{2,3},{4,5},{5,6},{6,7},{8,9},{9,10},{10,11},{12,13},{... | collective-permute-start | bytes 589832 | tf_op jit(solution)/shard_map/ppermute | solution.py:27
  268.7 2.1 collective-permute-start.33
  269.4 8.0 %collective-permute-start.44 = (bf16[64,1536]{1,0:T(8,128)(2,1)S(1)}, bf16[64,1536]{1,0:T(8,128)(2,1)S(1)}, u32[]{:S(2)}, u32[]{:S(2)}) collective-permute-start(bf16[64,1536]{1,0:T(8,128)(2,1)S(1)} %add_convert_fusion.6), channel_id=1, source_target_pairs={{3,2},{2,1},{1,0},{7,6},{6,5},{5,4},{11,10},{10,9},{9,8},{15,14},{... | collective-permute-start | bytes 589832 | tf_op jit(solution)/shard_map/ppermute | solution.py:28
  270.8 12.6 %collective-permute-start.34 = (bf16[64,1536]{1,0:T(8,128)(2,1)S(1)}, bf16[64,1536]{1,0:T(8,128)(2,1)S(1)}, u32[]{:S(2)}, u32[]{:S(2)}) collective-permute-start(bf16[64,1536]{1,0:T(8,128)(2,1)S(1)} %add_convert_fusion.10), channel_id=1, source_target_pairs={{3,2},{2,1},{1,0},{7,6},{6,5},{5,4},{11,10},{10,9},{9,8},{15,14},{... | collective-permute-start | bytes 589832 | tf_op jit(solution)/shard_map/ppermute | solution.py:28

commit v2 on v1

--- a/solution.py
+++ b/solution.py
@@ -6,45 +6,18 @@
 EPSILON = 1e-06
 BF = jnp.bfloat16
 F32 = jnp.float32
+CHUNKS = 3
+CHUNKS_BACK = 2
 
 
 def xor_pairs(count, step):
     return [(i, i ^ step) for i in range(count)]
 
 
-def line_scatter(part, rows_each, count, me):
-    def rows(index):
-        return lax.dynamic_slice_in_dim(part, jnp.clip(index, 0, count - 1) * rows_each, rows_each, 0)
-
-    from_left = None
-    from_right = None
-    for step in range(1, count):
-        to_right = rows(me + count - step)
-        to_left = rows(me - count + step)
-        if step > 1:
-            to_right = (to_right.astype(F32) + from_left.astype(F32)).astype(BF)
-            to_left = (to_left.astype(F32) + from_right.astype(F32)).astype(BF)
-        from_left = lax.ppermute(to_right, "exp", [(i, i + 1) for i in range(step)])
-        from_right = lax.ppermute(to_left, "exp", [(count - 1 - i, count - 2 - i) for i in range(step)])
-    total = rows(me).astype(F32)
-    if count > 1:
-        total = total + from_left.astype(F32) + from_right.astype(F32)
-    return total
-
-
-def line_gather(own, count, me):
-    rows_each = own.shape[0]
-    lower = []
-    upper = []
-    left = own
-    right = own
-    for step in range(1, count):
-        left = lax.ppermute(left, "exp", [(i, i + 1) for i in range(step - 1, count - 1)])
-        right = lax.ppermute(right, "exp", [(i + 1, i) for i in range(0, count - step)])
-        lower.append(left)
-        upper.append(right)
-    spread = jnp.concatenate(lower[::-1] + [own] + upper, axis=0)
-    return lax.dynamic_slice_in_dim(spread, (count - 1 - me) * rows_each, count * rows_each, 0)
+def together(values):
+    names = list(values)
+    joined = lax.optimization_barrier(tuple(values[name] for name in names))
+    return dict(zip(names, joined))
 
 
 def body(
@@ -73,7 +46,6 @@
     head_count = rates.shape[0]
     head_size = queries.shape[1] // head_count
     width = out_weight.shape[1]
-    half = width // 2
     experts = seq_count // 2
     capacity = exp_count * max(1, 2 * block_len // experts * 17 // (16 * exp_count))
     own_count = block_len // exp_count
@@ -165,20 +137,8 @@
         .astype(BF)
         .reshape(block_len, head_count * head_size)
     )
-    partial_value = jnp.dot(attention, out_weight, preferred_element_type=F32).astype(BF)
-
-    own_total = line_scatter(partial_value, own_count, exp_count, exp_index)
-    own_residual = lax.dynamic_slice_in_dim(residual_in, exp_index * own_count, own_count, 0)
-    own_hidden = (own_residual.astype(F32) + own_total).astype(BF)
-    hidden = line_gather(own_hidden, exp_count, exp_index)
-    hidden_wide = hidden.astype(F32)
-    row_scale = lax.rsqrt(jnp.mean(hidden_wide * hidden_wide, axis=-1, keepdims=True) + EPSILON)
-    logits = jnp.dot(hidden, router, preferred_element_type=F32) * row_scale
     expert_ids = jnp.arange(experts, dtype=jnp.int32)
     chosen = routes[:, :, None] == expert_ids[None, None, :]
-    route_logits = jnp.sum(jnp.where(chosen, logits[:, None, :], 0.0), axis=2)
-    route_weight = jax.nn.sigmoid(route_logits - route_logits[:, ::-1])
-
     onehot = jnp.sum(chosen.astype(jnp.int32), axis=1)
     before = (local_index[:, None] > local_index[None, :]).astype(BF)
     rank = jnp.dot(before, onehot.astype(BF), preferred_element_type=F32).astype(jnp.int32)
@@ -190,59 +150,152 @@
     pick = [(place[:, k][:, None] == slot_ids[None, :]).astype(BF) for k in range(2)]
     spread = jnp.transpose(pick[0] + pick[1])
 
-    here = lax.dynamic_slice_in_dim(hidden, core * half, half, 1)
-    there = lax.dynamic_slice_in_dim(hidden, (1 - core) * half, half, 1)
-    send_here = jnp.dot(spread, here, preferred_element_type=F32).astype(BF)
-    send_there = jnp.dot(spread, there, preferred_element_type=F32).astype(BF)
-    arrived = []
-    for g in range(chips):
-        rows = slice(g * capacity, (g + 1) * capacity)
-        for b in range(2):
-            block = (send_here if b == 0 else send_there)[rows]
-            if g or b:
-                block = lax.ppermute(block, "seq", xor_pairs(seq_count, 2 * g + b))
-            arrived.append(block)
-    mine = jnp.concatenate(arrived, axis=0)
-    swap = jnp.concatenate([arrived[i ^ 1] for i in range(seq_count)], axis=0)
-    theirs = lax.ppermute(swap, "seq", xor_pairs(seq_count, 1))
-    received = jnp.concatenate(
-        [jnp.where(core == 0, mine, theirs), jnp.where(core == 0, theirs, mine)], axis=1
-    )
-    received_wide = received.astype(F32)
-    in_scale = lax.rsqrt(
-        jnp.mean(received_wide * received_wide, axis=-1, keepdims=True) + EPSILON
-    )
-    gate_act = jnp.dot(received, gate_weight[0], preferred_element_type=F32) * in_scale
-    up_act = jnp.dot(received, up_weight[0], preferred_element_type=F32) * in_scale
-    active = (jax.nn.silu(gate_act) * up_act).astype(BF)
-    partials = jnp.dot(active, down_weight[0], preferred_element_type=F32).astype(BF)
-
-    keep = lax.dynamic_slice_in_dim(partials, core * half, half, 1)
-    give = lax.dynamic_slice_in_dim(partials, (1 - core) * half, half, 1)
-    give = give.reshape(chips, 2, capacity, half)[:, ::-1].reshape(seq_count * capacity, half)
-    got = lax.ppermute(give, "seq", xor_pairs(seq_count, 1))
-    sums = (keep.astype(F32) + got.astype(F32)).astype(BF)
-    tables = [[], []]
-    for g in range(chips):
-        for b in range(2):
-            i = 2 * g + b
-            block = sums[i * capacity : (i + 1) * capacity]
-            if i:
-                block = lax.ppermute(block, "seq", xor_pairs(seq_count, i))
-            tables[b].append(block)
-    mixes = []
-    for b in range(2):
-        table = jnp.concatenate(tables[b], axis=0)
-        mix = sum(
-            jnp.dot(pick[k], table, preferred_element_type=F32) * route_weight[:, k : k + 1]
-            for k in range(2)
-        )
-        mixes.append(line_scatter(mix.astype(BF), own_count, exp_count, exp_index))
-    own_mix = jnp.concatenate(
-        [jnp.where(core == 0, mixes[0], mixes[1]), jnp.where(core == 0, mixes[1], mixes[0])],
-        axis=1,
-    )
-    return (own_hidden.astype(F32) + own_mix).astype(BF)
+    chunks = CHUNKS
+    wide = width // chunks
+    reach = exp_count // 2
+    mirror = jnp.minimum(exp_index, exp_count - 1 - exp_index)
+    stages = 2 * reach - 1
+    hidden = {}
+    total = {}
+    mine = {}
+    theirs = {}
+    gate_act = None
+    up_act = None
+    in_squares = None
+
+    def project(i):
+        cols = slice(i * wide, (i + 1) * wide)
+        return jnp.dot(attention, out_weight[:, cols], preferred_element_type=F32).astype(BF)
+
+    part = {0: project(0)}
+    for r in range(chunks + stages + 2):
+        done = {}
+        for side in range(reach - 1):
+            inner = r - side
+            outer = r - (stages - 1 - side)
+            ins = [(side, side + 1), (exp_count - 1 - side, exp_count - 2 - side)]
+            outs = [(b, a) for a, b in ins]
+            has_in = 0 <= inner < chunks
+            has_out = 0 <= outer < chunks
+            if not (has_in or has_out):
+                continue
+            if has_in and has_out:
+                load = jnp.where(mirror == side, total.get(inner, part[inner]), hidden[outer])
+            else:
+                load = total.get(inner, part[inner]) if has_in else hidden[outer]
+            done["side", side] = lax.ppermute(
+                load, "exp", (ins if has_in else []) + (outs if has_out else [])
+            )
+        middle = r - (reach - 1)
+        if 0 <= middle < chunks:
+            done["middle"] = lax.ppermute(
+                total.get(middle, part[middle]), "exp", [(reach - 1, reach), (reach, reach - 1)]
+            )
+        i = r - stages
+        if 0 <= i < chunks:
+            send = jnp.dot(spread, hidden[i], preferred_element_type=F32).astype(BF)
+            done["group", 0] = send[:capacity]
+            for g in range(1, chips):
+                block = send[g * capacity : (g + 1) * capacity]
+                done["group", g] = lax.ppermute(block, "seq", xor_pairs(seq_count, 2 * g))
+        i = r - stages - 1
+        if 0 <= i < chunks:
+            done["theirs"] = lax.ppermute(mine[i], "seq", xor_pairs(seq_count, 1))
+        i = r - stages - 2
+        if 0 <= i < chunks:
+            rows = jnp.concatenate([mine[i], theirs[i]], axis=0)
+            squares = jnp.sum(jnp.square(rows.astype(F32)), axis=-1, keepdims=True)
+            depth = slice(i * wide, (i + 1) * wide)
+            gate_part = jnp.dot(rows, gate_weight[0, depth], preferred_element_type=F32)
+            up_part = jnp.dot(rows, up_weight[0, depth], preferred_element_type=F32)
+            done["squares"] = squares if i == 0 else in_squares + squares
+            done["gate"] = gate_part if i == 0 else gate_act + gate_part
+            done["up"] = up_part if i == 0 else up_act + up_part
+        if r + 1 < chunks:
+            done["part"] = project(r + 1)
+        done = together(done)
+        if "part" in done:
+            part[r + 1] = done["part"]
+        for side in range(reach - 1):
+            inner = r - side
+            outer = r - (stages - 1 - side)
+            if 0 <= inner < chunks:
+                total[inner] = (part[inner].astype(F32) + done["side", side].astype(F32)).astype(BF)
+            if 0 <= outer < chunks:
+                hidden[outer] = jnp.where(mirror == side, done["side", side], hidden[outer])
+        if 0 <= middle < chunks:
+            residual = residual_in[:, middle * wide : (middle + 1) * wide].astype(F32)
+            whole = total.get(middle, part[middle]).astype(F32) + done["middle"].astype(F32)
+            hidden[middle] = (residual + whole).astype(BF)
+        if ("group", 0) in done:
+            mine[r - stages] = jnp.concatenate([done["group", g] for g in range(chips)], axis=0)
+        if "theirs" in done:
+            theirs[r - stages - 1] = done["theirs"]
+        if "gate" in done:
+            gate_act, up_act, in_squares = done["gate"], done["up"], done["squares"]
+    in_scale = lax.rsqrt(in_squares / width + EPSILON)
+    active = (jax.nn.silu(gate_act * in_scale) * (up_act * in_scale)).astype(BF)
+
+    hidden = jnp.concatenate([hidden[i] for i in range(chunks)], axis=1)
+    squares = jnp.sum(jnp.square(hidden.astype(F32)), axis=-1, keepdims=True)
+    row_scale = lax.rsqrt(squares / width + EPSILON)
+    logits = jnp.dot(hidden, router, preferred_element_type=F32) * row_scale
+    route_logits = jnp.sum(jnp.where(chosen, logits[:, None, :], 0.0), axis=2)
+    route_weight = jax.nn.sigmoid(route_logits - route_logits[:, ::-1])
+    own_hidden = lax.dynamic_slice_in_dim(hidden, exp_index * own_count, own_count, 0)
+
+    chunks = CHUNKS_BACK
+    wide = width // chunks
+    sums = {}
+    mixes = {}
+    own = {}
+
+    def lower(i):
+        cols = slice(i * wide, (i + 1) * wide)
+        return jnp.dot(active, down_weight[0, :, cols], preferred_element_type=F32).astype(BF)
+
+    def own_rows(value, index):
+        return lax.dynamic_slice_in_dim(value, index * own_count, own_count, 0)
+
+    partials = {0: lower(0)}
+    for r in range(chunks + 2):
+        done = {}
+        i = r - 2
+        if 0 <= i < chunks:
+            for step in range(1, exp_count):
+                block = own_rows(mixes[i], jnp.bitwise_xor(exp_index, step))
+                done["own", step] = lax.ppermute(block, "exp", xor_pairs(exp_count, step))
+        i = r - 1
+        if 0 <= i < chunks:
+            for g in range(1, chips):
+                block = sums[i][g * capacity : (g + 1) * capacity]
+                done["table", g] = lax.ppermute(block, "seq", xor_pairs(seq_count, 2 * g))
+        if r < chunks:
+            done["got"] = lax.ppermute(partials[r][slots:], "seq", xor_pairs(seq_count, 1))
+        if r + 1 < chunks:
+            done["partials"] = lower(r + 1)
+        done = together(done)
+        if "partials" in done:
+            partials[r + 1] = done["partials"]
+        if "got" in done:
+            sums[r] = (partials[r][:slots].astype(F32) + done["got"].astype(F32)).astype(BF)
+        i = r - 1
+        if 0 <= i < chunks:
+            table = jnp.concatenate(
+                [sums[i][:capacity]] + [done["table", g] for g in range(1, chips)], axis=0
+            )
+            mixes[i] = sum(
+                jnp.dot(pick[k], table, preferred_element_type=F32) * route_weight[:, k : k + 1]
+                for k in range(2)
+            ).astype(BF)
+        i = r - 2
+        if 0 <= i < chunks:
+            cols = slice(i * wide, (i + 1) * wide)
+            whole = own_hidden[:, cols].astype(F32) + own_rows(mixes[i], exp_index).astype(F32)
+            for step in range(1, exp_count):
+                whole = whole + done["own", step].astype(F32)
+            own[i] = whole.astype(BF)
+    return jnp.concatenate([own[i] for i in range(chunks)], axis=1)
 
 
 def solution(mesh):

time: 285 us -> 234 us (0.82)
  waiting for transfers between devices: 151 us -> 106 us
  starting transfers between devices: 65.1 us -> 53.7 us
  matrix products: 31.4 us -> 36.1 us
    ppermute x40 -> x34, waiting for transfers between devices: 144 us -> 99.4 us  [the longest x6 27.4 us: body(): done['own', step] = lax.ppermute(block, 'exp', xor_pairs(exp_count, step))]
    ppermute x40 -> x34, starting transfers between devices: 60.3 us -> 48.9 us  [the longest x5 14.7 us: body(): lax.ppermute(load, 'exp', (ins if has_in else []) + (outs if has_out else...]
    dot_general x6 -> x14, matrix products: 23.4 us -> 28.1 us  [the longest x2 7.55 us: lower(): jnp.dot(active, down_weight[0, :, cols], preferred_element_type=F32)]
    rev x1 -> x0, local copies, waits for them, and re-layouts: 3.96 us -> none  [body(): give.reshape(chips, 2, capacity, half)[:, ::-1]]
    unnamed x51 -> x46, local copies, waits for them, and re-layouts: 5.64 us -> 7.88 us
    convert_element_type x12 -> x9, other arithmetic: 7.68 us -> 7.7 us  [the longest x2 4.23 us: body(): (partials[r][:slots].astype(F32) + done['got'].astype(F32)).astype(BF)]
  transfers between devices with their start and end apart: 45 -> 39, of which waited for: 25 -> 19; matrix products, arithmetic and copies ran while one was open for 3% -> 10% of each run, Pallas kernels for 0% -> 0%
where the time goes in v2:
time: 234 us; the launch traced here: 233 us
  waiting for transfers between devices  106 us (45%)
  starting transfers between devices  53.7 us (23%)
  matrix products  36.1 us (15%)
  other arithmetic  17.2 us (7%)
  local copies, waits for them, and re-layouts  14.9 us (6%)
  between operations  4.83 us (2%)
    ppermute x6, waiting for transfers between devices, body(): done['own', step] = lax.ppermute(block, 'exp', xor_pairs(exp_count, step))  27.4 us
    ppermute x9, waiting for transfers between devices, body(): done['group', g] = lax.ppermute(block, 'seq', xor_pairs(seq_count, 2 * g))  27 us
    ppermute x5, waiting for transfers between devices, body(): lax.ppermute(load, 'exp', (ins if has_in else []) + (outs if has_out else...  25.8 us
    ppermute x6, waiting for transfers between devices, body(): done['table', g] = lax.ppermute(block, 'seq', xor_pairs(seq_count, 2 * g))  17.6 us
    ppermute x5, starting transfers between devices, body(): lax.ppermute(load, 'exp', (ins if has_in else []) + (outs if has_out else...  14.7 us
    ppermute x6, starting transfers between devices, body(): done['own', step] = lax.ppermute(block, 'exp', xor_pairs(exp_count, step))  13.6 us
    ppermute x9, starting transfers between devices, body(): done['group', g] = lax.ppermute(block, 'seq', xor_pairs(seq_count, 2 * g))  10.7 us
    unnamed x46, local copies, waits for them, and re-layouts  7.88 us
  transfers between devices with their start and end apart: 39, of which 19 were waited for; matrix products, arithmetic and copies ran while one was open for 10% of the time, Pallas kernels for 0%

profile of v2, /device:TPU:0, one launch (start us, length us, event | category | flops | bytes accessed | tf_op | source)
XLA Modules:
  0.0 233.1 jit_solution(871977377632530787)
XLA Ops:
  1.0 1.4 fusion.86
  3.8 1.2 copy.40
  5.0 1.2 compare_convert_fusion.1
  6.3 1.7 convolution_convert_fusion.5
  12.1 3.5 %collective-permute-start.3 = (bf16[4,128,128]{2,1,0:T(8,128)(2,1)S(1)}, bf16[4,128,128]{2,1,0:T(8,128)(2,1)S(1)}, u32[]{:S(2)}, u32[]{:S(2)}) collective-permute-start(bf16[4,128,128]{2,1,0:T(8,128)(2,1)S(1)} %fusion.79), channel_id=1, source_target_pairs={{0,24},{4,28},{8,16},{12,20},{16,8},{20,12},{24,0},{28,4},{1,25},{... | collective-permute-start | bytes 393224 | tf_op jit(solution)/shard_map/ppermute | solution.py:89
  17.0 2.9 %collective-permute-done.3 = bf16[4,128,128]{2,1,0:T(8,128)(2,1)S(1)} collective-permute-done((bf16[4,128,128]{2,1,0:T(8,128)(2,1)S(1)}, bf16[4,128,128]{2,1,0:T(8,128)(2,1)S(1)}, u32[]{:S(2)}, u32[]{:S(2)}) %collective-permute-start.3) | collective-permute-done | bytes 131104 | tf_op jit(solution)/shard_map/ppermute | solution.py:89
  19.9 2.7 %collective-permute-done.2 = bf16[4,128,128]{2,1,0:T(8,128)(2,1)S(1)} collective-permute-done((bf16[4,128,128]{2,1,0:T(8,128)(2,1)S(1)}, bf16[4,128,128]{2,1,0:T(8,128)(2,1)S(1)}, u32[]{:S(2)}, u32[]{:S(2)}) %collective-permute-start.2) | collective-permute-done | bytes 131104 | tf_op jit(solution)/shard_map/ppermute | solution.py:89
  23.3 1.2 collective-permute-done.4
  25.0 2.0 multiply_reduce_fusion.4
  27.2 2.3 fusion.36
  29.5 3.5 %collective-permute-start.5 = (bf16[256,1024]{1,0:T(8,128)(2,1)S(1)}, bf16[256,1024]{1,0:T(8,128)(2,1)S(1)}, u32[]{:S(2)}, u32[]{:S(2)}) collective-permute-start(bf16[256,1024]{1,0:T(8,128)(2,1)S(1)} %fusion.36), channel_id=1, source_target_pairs={{0,1},{3,2},{4,5},{7,6},{8,9},{11,10},{12,13},{15,14},{16,17},{19,... | collective-permute-start | bytes 1572872 | tf_op jit(solution)/shard_map/ppermute | solution.py:186
  33.0 2.3 fusion.39
  35.4 9.1 %collective-permute-done.5 = bf16[256,1024]{1,0:T(8,128)(2,1)S(1)} collective-permute-done((bf16[256,1024]{1,0:T(8,128)(2,1)S(1)}, bf16[256,1024]{1,0:T(8,128)(2,1)S(1)}, u32[]{:S(2)}, u32[]{:S(2)}) %collective-permute-start.5) | collective-permute-done | bytes 524320 | tf_op jit(solution)/shard_map/ppermute | solution.py:186
  44.5 4.4 %collective-permute-start.6 = (bf16[256,1024]{1,0:T(8,128)(2,1)S(1)}, bf16[256,1024]{1,0:T(8,128)(2,1)S(1)}, u32[]{:S(2)}, u32[]{:S(2)}) collective-permute-start(bf16[256,1024]{1,0:T(8,128)(2,1)S(1)} %fusion.39), channel_id=1, source_target_pairs={{0,1},{3,2},{4,5},{7,6},{8,9},{11,10},{12,13},{15,14},{16,17},{19,... | collective-permute-start | bytes 1572872 | tf_op jit(solution)/shard_map/ppermute | solution.py:186
  49.9 2.3 %fusion.42 = bf16[256,1024]{1,0:T(8,128)(2,1)S(1)} fusion(bf16[256,1024]{0,1:T(8,128)(2,1)S(1)} %bitcast.90, bf16[1024,3072]{1,0:T(8,128)(2,1)} %param.18), kind=kOutput, calls=%fused_computation.59 | convolution fusion | flops 537133056 | bytes 3145728 | tf_op jit(solution)/shard_map/dot_general | solution.py:168
  52.3 7.2 %collective-permute-done.6 = bf16[256,1024]{1,0:T(8,128)(2,1)S(1)} collective-permute-done((bf16[256,1024]{1,0:T(8,128)(2,1)S(1)}, bf16[256,1024]{1,0:T(8,128)(2,1)S(1)}, u32[]{:S(2)}, u32[]{:S(2)}) %collective-permute-start.6) | collective-permute-done | bytes 524320 | tf_op jit(solution)/shard_map/ppermute | solution.py:186
  59.9 4.0 %collective-permute-start.8 = (bf16[256,1024]{1,0:T(8,128)(2,1)S(1)}, bf16[256,1024]{1,0:T(8,128)(2,1)S(1)}, u32[]{:S(2)}, u32[]{:S(2)}) collective-permute-start(bf16[256,1024]{1,0:T(8,128)(2,1)S(1)} %broadcast_select_fusion.3), channel_id=1, source_target_pairs={{0,1},{3,2},{1,0},{2,3},{4,5},{7,6},{5,4},{6,7},{8,9},{11,10},{9,8... | collective-permute-start | bytes 1572872 | tf_op jit(solution)/shard_map/ppermute | solution.py:186
  64.9 9.5 %collective-permute-done.8 = bf16[256,1024]{1,0:T(8,128)(2,1)S(1)} collective-permute-done((bf16[256,1024]{1,0:T(8,128)(2,1)S(1)}, bf16[256,1024]{1,0:T(8,128)(2,1)S(1)}, u32[]{:S(2)}, u32[]{:S(2)}) %collective-permute-start.8) | collective-permute-done | bytes 524320 | tf_op jit(solution)/shard_map/ppermute | solution.py:186
  75.3 1.3 collective-permute-start.10
  78.0 1.6 collective-permute-start.12
  80.3 1.3 collective-permute-start.14
  81.5 5.8 %collective-permute-done.12 = bf16[136,1024]{1,0:T(8,128)(2,1)S(1)} collective-permute-done((bf16[136,1024]{1,0:T(8,128)(2,1)S(1)}, bf16[136,1024]{1,0:T(8,128)(2,1)S(1)}, u32[]{:S(2)}, u32[]{:S(2)}) %collective-permute-start.12) | collective-permute-done | bytes 278560 | tf_op jit(solution)/shard_map/ppermute | solution.py:200
  87.4 4.2 %collective-permute-done.13 = bf16[136,1024]{1,0:T(8,128)(2,1)S(1)} collective-permute-done((bf16[136,1024]{1,0:T(8,128)(2,1)S(1)}, bf16[136,1024]{1,0:T(8,128)(2,1)S(1)}, u32[]{:S(2)}, u32[]{:S(2)}) %collective-permute-start.13) | collective-permute-done | bytes 278560 | tf_op jit(solution)/shard_map/ppermute | solution.py:200
  91.9 1.5 collective-permute-start.15
  94.9 1.4 collective-permute-start.17
  96.3 1.5 collective-permute-start.18
  97.9 5.9 %collective-permute-done.16 = bf16[136,1024]{1,0:T(8,128)(2,1)S(1)} collective-permute-done((bf16[136,1024]{1,0:T(8,128)(2,1)S(1)}, bf16[136,1024]{1,0:T(8,128)(2,1)S(1)}, u32[]{:S(2)}, u32[]{:S(2)}) %collective-permute-start.16) | collective-permute-done | bytes 278560 | tf_op jit(solution)/shard_map/ppermute | solution.py:200
  103.8 5.9 %collective-permute-done.17 = bf16[136,1024]{1,0:T(8,128)(2,1)S(1)} collective-permute-done((bf16[136,1024]{1,0:T(8,128)(2,1)S(1)}, bf16[136,1024]{1,0:T(8,128)(2,1)S(1)}, u32[]{:S(2)}, u32[]{:S(2)}) %collective-permute-start.17) | collective-permute-done | bytes 278560 | tf_op jit(solution)/shard_map/ppermute | solution.py:200
  110.5 1.5 collective-permute-start.20
  112.7 1.3 collective-permute-start.22
  114.9 1.4 copy-done.14
  116.3 1.9 fusion.28
  118.4 1.9 fusion.26
  120.4 5.2 %collective-permute-done.21 = bf16[136,1024]{1,0:T(8,128)(2,1)S(1)} collective-permute-done((bf16[136,1024]{1,0:T(8,128)(2,1)S(1)}, bf16[136,1024]{1,0:T(8,128)(2,1)S(1)}, u32[]{:S(2)}, u32[]{:S(2)}) %collective-permute-start.21) | collective-permute-done | bytes 278560 | tf_op jit(solution)/shard_map/ppermute | solution.py:200
  125.7 1.9 fusion.24
  127.6 1.9 fusion.22
  130.9 1.5 collective-permute-done.24
  133.0 2.1 fusion.20
  135.2 1.9 fusion.18
  138.6 1.2 copy-done.16
  139.8 3.0 %convolution_convert_fusion.1 = bf16[1088,1536]{1,0:T(8,128)(2,1)S(1)} fusion(bf16[1088,640]{1,0:T(8,128)(2,1)S(1)} %multiply_convert_fusion, bf16[1,640,3072]{2,1,0:T(8,128)(2,1)S(1)} %copy-done.16), kind=kOutput, calls=%fused_computation.1 | convolution fusion | flops 2140766208 | bytes 6701056 | tf_op jit(solution)/shard_map/dot_general | solution.py:255
  142.9 1.7 copy-done.2
  144.6 1.3 slice.201
  147.4 4.5 %convolution_convert_fusion = bf16[1088,1536]{1,0:T(8,128)(2,1)S(1)} fusion(bf16[1088,640]{1,0:T(8,128)(2,1)S(1)} %copy-done.9, bf16[1,640,3072]{2,1,0:T(8,128)(2,1)} %param.22), kind=kOutput, calls=%fused_computation | convolution fusion | flops 2140766208 | bytes 6701056 | tf_op jit(solution)/shard_map/dot_general | solution.py:255
  151.9 1.7 copy-done.3
  153.7 1.3 slice.177
  155.4 2.4 %add_convert_fusion.1 = bf16[544,1536]{1,0:T(8,128)(2,1)S(1)} fusion(bf16[544,1536]{1,0:T(8,128)(2,1)} %collective-permute-done.25, bf16[1088,1536]{1,0:T(8,128)(2,1)} %copy-done.2), kind=kLoop, calls=%fused_computation.6 | loop fusion | flops 3342336 | bytes 5013504 | tf_op jit(solution)/shard_map/convert_element_type | solution.py:281
  158.8 1.3 collective-permute-start.27
  160.1 1.4 collective-permute-start.28
  161.5 9.0 %collective-permute-done.26 = bf16[136,1536]{1,0:T(8,128)(2,1)S(1)} collective-permute-done((bf16[136,1536]{1,0:T(8,128)(2,1)S(1)}, bf16[136,1536]{1,0:T(8,128)(2,1)S(1)}, u32[]{:S(2)}, u32[]{:S(2)}) %collective-permute-start.26) | collective-permute-done | bytes 417824 | tf_op jit(solution)/shard_map/ppermute | solution.py:272
  170.5 8.7 %collective-permute-done.27 = bf16[136,1536]{1,0:T(8,128)(2,1)S(1)} collective-permute-done((bf16[136,1536]{1,0:T(8,128)(2,1)S(1)}, bf16[136,1536]{1,0:T(8,128)(2,1)S(1)}, u32[]{:S(2)}, u32[]{:S(2)}) %collective-permute-start.27) | collective-permute-done | bytes 417824 | tf_op jit(solution)/shard_map/ppermute | solution.py:272
  179.1 1.9 add_convert_fusion
  181.2 1.3 collective-permute-start.33
  183.1 1.6 collective-permute-start.35
  186.5 6.2 %collective-permute-start.30 = (bf16[64,1536]{1,0:T(8,128)(2,1)S(1)}, bf16[64,1536]{1,0:T(8,128)(2,1)S(1)}, u32[]{:S(2)}, u32[]{:S(2)}) collective-permute-start(bf16[64,1536]{1,0:T(8,128)(2,1)S(1)} %get-tuple-element.140), channel_id=1, source_target_pairs={{0,1},{1,0},{2,3},{3,2},{4,5},{5,4},{6,7},{7,6},{8,9},{9,8},{10,11... | collective-permute-start | bytes 589832 | tf_op jit(solution)/shard_map/ppermute | solution.py:267
  192.7 5.5 %collective-permute-done.30 = bf16[64,1536]{1,0:T(8,128)(2,1)S(1)} collective-permute-done((bf16[64,1536]{1,0:T(8,128)(2,1)S(1)}, bf16[64,1536]{1,0:T(8,128)(2,1)S(1)}, u32[]{:S(2)}, u32[]{:S(2)}) %collective-permute-start.30) | collective-permute-done | bytes 196640 | tf_op jit(solution)/shard_map/ppermute | solution.py:267
  198.1 1.9 collective-permute-start.32
  200.0 8.2 %collective-permute-done.31 = bf16[64,1536]{1,0:T(8,128)(2,1)S(1)} collective-permute-done((bf16[64,1536]{1,0:T(8,128)(2,1)S(1)}, bf16[64,1536]{1,0:T(8,128)(2,1)S(1)}, u32[]{:S(2)}, u32[]{:S(2)}) %collective-permute-start.31) | collective-permute-done | bytes 196640 | tf_op jit(solution)/shard_map/ppermute | solution.py:267
  210.0 0.9 copy-done.10
  211.7 3.1 %collective-permute-start.36 = (bf16[64,1536]{1,0:T(8,128)(2,1)}, bf16[64,1536]{1,0:T(8,128)(2,1)}, u32[]{:S(2)}, u32[]{:S(2)}) collective-permute-start(bf16[64,1536]{1,0:T(8,128)(2,1)} %get-tuple-element.137), channel_id=1, source_target_pairs={{0,1},{1,0},{2,3},{3,2},{4,5},{5,4},{6,7},{7,6},{8,9},{9,8},{10,11... | collective-permute-start | bytes 589832 | tf_op jit(solution)/shard_map/ppermute | solution.py:267
  214.8 2.4 %collective-permute-start.38 = (bf16[64,1536]{1,0:T(8,128)(2,1)}, bf16[64,1536]{1,0:T(8,128)(2,1)}, u32[]{:S(2)}, u32[]{:S(2)}) collective-permute-start(bf16[64,1536]{1,0:T(8,128)(2,1)} %get-tuple-element.135), channel_id=1, source_target_pairs={{0,3},{1,2},{2,1},{3,0},{4,7},{5,6},{6,5},{7,4},{8,11},{9,10},{10,... | collective-permute-start | bytes 589832 | tf_op jit(solution)/shard_map/ppermute | solution.py:267
  217.2 3.5 %collective-permute-done.36 = bf16[64,1536]{1,0:T(8,128)(2,1)} collective-permute-done((bf16[64,1536]{1,0:T(8,128)(2,1)}, bf16[64,1536]{1,0:T(8,128)(2,1)}, u32[]{:S(2)}, u32[]{:S(2)}) %collective-permute-start.36) | collective-permute-done | bytes 196640 | tf_op jit(solution)/shard_map/ppermute | solution.py:267
  220.6 10.2 %collective-permute-done.37 = bf16[64,1536]{1,0:T(8,128)(2,1)} collective-permute-done((bf16[64,1536]{1,0:T(8,128)(2,1)}, bf16[64,1536]{1,0:T(8,128)(2,1)}, u32[]{:S(2)}, u32[]{:S(2)}) %collective-permute-start.37) | collective-permute-done | bytes 196640 | tf_op jit(solution)/shard_map/ppermute | solution.py:267
  230.9 1.5 add_convert_fusion.9
  (156 shorter events, 27.1 us)
Async XLA Ops:
  0.0 24.7 %copy-start = (bf16[256,1024]{1,0:T(8,128)(2,1)S(1)}, bf16[256,1024]{1,0:T(8,128)(2,1)}, u32[]{:S(2)}) copy-start(bf16[256,1024]{1,0:T(8,128)(2,1)} %param.13) | copy-start | bytes 1572868
  0.0 9.3 %copy-start.13 = (f32[8]{0:T(128)S(1)}, f32[8]{0:T(128)}, u32[]{:S(2)}) copy-start(f32[8]{0:T(128)} %param.16) | copy-start | bytes 100
  8.1 3.9 %collective-permute-start = (bf16[8,128,128]{2,1,0:T(8,128)(2,1)S(1)}, bf16[8,128,128]{2,1,0:T(8,128)(2,1)S(1)}, u32[]{:S(2)}, u32[]{:S(2)}) collective-permute-start(bf16[8,128,128]{2,1,0:T(8,128)(2,1)S(1)} %convolution_convert_fusion.5), channel_id=1, source_target_pairs={{0,4},{4,0},{8,12},{12,8},{16,20},{20,16},{24,28},{28,24},{1,5},{5... | collective-permute-start | bytes 786440 | tf_op jit(solution)/shard_map/ppermute | solution.py:71
  12.1 7.8 %collective-permute-start.3 = (bf16[4,128,128]{2,1,0:T(8,128)(2,1)S(1)}, bf16[4,128,128]{2,1,0:T(8,128)(2,1)S(1)}, u32[]{:S(2)}, u32[]{:S(2)}) collective-permute-start(bf16[4,128,128]{2,1,0:T(8,128)(2,1)S(1)} %fusion.79), channel_id=1, source_target_pairs={{0,24},{4,28},{8,16},{12,20},{16,8},{20,12},{24,0},{28,4},{1,25},{... | collective-permute-start | bytes 393224 | tf_op jit(solution)/shard_map/ppermute | solution.py:89
  15.6 6.9 %collective-permute-start.2 = (bf16[4,128,128]{2,1,0:T(8,128)(2,1)S(1)}, bf16[4,128,128]{2,1,0:T(8,128)(2,1)S(1)}, u32[]{:S(2)}, u32[]{:S(2)}) collective-permute-start(bf16[4,128,128]{2,1,0:T(8,128)(2,1)S(1)} %fusion.79), channel_id=1, source_target_pairs={{0,16},{4,20},{8,24},{12,28},{16,0},{20,4},{24,8},{28,12},{1,17},{... | collective-permute-start | bytes 393224 | tf_op jit(solution)/shard_map/ppermute | solution.py:89
  16.1 6.7 %collective-permute-start.1 = (bf16[4,128,128]{2,1,0:T(8,128)(2,1)S(1)}, bf16[4,128,128]{2,1,0:T(8,128)(2,1)S(1)}, u32[]{:S(2)}, u32[]{:S(2)}) collective-permute-start(bf16[4,128,128]{2,1,0:T(8,128)(2,1)S(1)} %fusion.79), channel_id=1, source_target_pairs={{0,8},{4,12},{8,0},{12,4},{16,24},{20,28},{24,16},{28,20},{1,9},{5... | collective-permute-start | bytes 393224 | tf_op jit(solution)/shard_map/ppermute | solution.py:89
  23.0 1.4 collective-permute-start.4
  27.0 6.0 %copy-start.11 = (s32[256,2]{0,1:T(2,128)S(1)}, s32[256,2]{0,1:T(2,128)}, u32[]{:S(2)}) copy-start(s32[256,2]{0,1:T(2,128)} %param.23) | copy-start | bytes 6148
  29.5 15.0 %collective-permute-start.5 = (bf16[256,1024]{1,0:T(8,128)(2,1)S(1)}, bf16[256,1024]{1,0:T(8,128)(2,1)S(1)}, u32[]{:S(2)}, u32[]{:S(2)}) collective-permute-start(bf16[256,1024]{1,0:T(8,128)(2,1)S(1)} %fusion.36), channel_id=1, source_target_pairs={{0,1},{3,2},{4,5},{7,6},{8,9},{11,10},{12,13},{15,14},{16,17},{19,... | collective-permute-start | bytes 1572872 | tf_op jit(solution)/shard_map/ppermute | solution.py:186
  35.4 24.1 %copy-start.5 = (bf16[256,3072]{1,0:T(8,128)(2,1)S(1)}, bf16[256,3072]{1,0:T(8,128)(2,1)}, u32[]{:S(2)}) copy-start(bf16[256,3072]{1,0:T(8,128)(2,1)} %param.12) | copy-start | bytes 4718596
  44.5 15.0 %collective-permute-start.6 = (bf16[256,1024]{1,0:T(8,128)(2,1)S(1)}, bf16[256,1024]{1,0:T(8,128)(2,1)S(1)}, u32[]{:S(2)}, u32[]{:S(2)}) collective-permute-start(bf16[256,1024]{1,0:T(8,128)(2,1)S(1)} %fusion.39), channel_id=1, source_target_pairs={{0,1},{3,2},{4,5},{7,6},{8,9},{11,10},{12,13},{15,14},{16,17},{19,... | collective-permute-start | bytes 1572872 | tf_op jit(solution)/shard_map/ppermute | solution.py:186
  49.1 10.4 %collective-permute-start.7 = (bf16[256,1024]{1,0:T(8,128)(2,1)S(1)}, bf16[256,1024]{1,0:T(8,128)(2,1)S(1)}, u32[]{:S(2)}, u32[]{:S(2)}) collective-permute-start(bf16[256,1024]{1,0:T(8,128)(2,1)S(1)} %add_convert_fusion.7), channel_id=1, source_target_pairs={{1,2},{2,1},{5,6},{6,5},{9,10},{10,9},{13,14},{14,13},{17,18},{18,... | collective-permute-start | bytes 1572872 | tf_op jit(solution)/shard_map/ppermute | solution.py:191
  59.9 14.5 %collective-permute-start.8 = (bf16[256,1024]{1,0:T(8,128)(2,1)S(1)}, bf16[256,1024]{1,0:T(8,128)(2,1)S(1)}, u32[]{:S(2)}, u32[]{:S(2)}) collective-permute-start(bf16[256,1024]{1,0:T(8,128)(2,1)S(1)} %broadcast_select_fusion.3), channel_id=1, source_target_pairs={{0,1},{3,2},{1,0},{2,3},{4,5},{7,6},{5,4},{6,7},{8,9},{11,10},{9,8... | collective-permute-start | bytes 1572872 | tf_op jit(solution)/shard_map/ppermute | solution.py:186
  64.1 10.3 %collective-permute-start.9 = (bf16[256,1024]{1,0:T(8,128)(2,1)S(1)}, bf16[256,1024]{1,0:T(8,128)(2,1)S(1)}, u32[]{:S(2)}, u32[]{:S(2)}) collective-permute-start(bf16[256,1024]{1,0:T(8,128)(2,1)S(1)} %add_convert_fusion.5), channel_id=1, source_target_pairs={{1,2},{2,1},{5,6},{6,5},{9,10},{10,9},{13,14},{14,13},{17,18},{18,... | collective-permute-start | bytes 1572872 | tf_op jit(solution)/shard_map/ppermute | solution.py:191
  75.0 3.0 %copy-start.6 = (bf16[256,1024]{1,0:T(8,128)(2,1)}, bf16[256,1024]{1,0:T(8,128)(2,1)S(1)}, u32[]{:S(2)}) copy-start(bf16[256,1024]{1,0:T(8,128)(2,1)S(1)} %broadcast_select_fusion.2) | copy-start | bytes 1572868
  75.3 16.3 %collective-permute-start.10 = (bf16[256,1024]{1,0:T(8,128)(2,1)S(1)}, bf16[256,1024]{1,0:T(8,128)(2,1)S(1)}, u32[]{:S(2)}, u32[]{:S(2)}) collective-permute-start(bf16[256,1024]{1,0:T(8,128)(2,1)S(1)} %add_convert_fusion.4), channel_id=1, source_target_pairs={{1,0},{2,3},{5,4},{6,7},{9,8},{10,11},{13,12},{14,15},{17,16},{18,... | collective-permute-start | bytes 1572872 | tf_op jit(solution)/shard_map/ppermute | solution.py:186
  76.6 15.0 %collective-permute-start.11 = (bf16[256,1024]{1,0:T(8,128)(2,1)S(1)}, bf16[256,1024]{1,0:T(8,128)(2,1)S(1)}, u32[]{:S(2)}, u32[]{:S(2)}) collective-permute-start(bf16[256,1024]{1,0:T(8,128)(2,1)S(1)} %add_convert_fusion.3), channel_id=1, source_target_pairs={{1,2},{2,1},{5,6},{6,5},{9,10},{10,9},{13,14},{14,13},{17,18},{18,... | collective-permute-start | bytes 1572872 | tf_op jit(solution)/shard_map/ppermute | solution.py:191
  78.0 9.4 %collective-permute-start.12 = (bf16[136,1024]{1,0:T(8,128)(2,1)S(1)}, bf16[136,1024]{1,0:T(8,128)(2,1)S(1)}, u32[]{:S(2)}, u32[]{:S(2)}) collective-permute-start(bf16[136,1024]{1,0:T(8,128)(2,1)S(1)} %get-tuple-element.133), channel_id=1, source_target_pairs={{0,8},{4,12},{8,0},{12,4},{16,24},{20,28},{24,16},{28,20},{1,9},{5... | collective-permute-start | bytes 835592 | tf_op jit(solution)/shard_map/ppermute | solution.py:200
  79.6 12.0 %collective-permute-start.13 = (bf16[136,1024]{1,0:T(8,128)(2,1)S(1)}, bf16[136,1024]{1,0:T(8,128)(2,1)S(1)}, u32[]{:S(2)}, u32[]{:S(2)}) collective-permute-start(bf16[136,1024]{1,0:T(8,128)(2,1)S(1)} %get-tuple-element.132), channel_id=1, source_target_pairs={{0,16},{4,20},{8,24},{12,28},{16,0},{20,4},{24,8},{28,12},{1,17},{... | collective-permute-start | bytes 835592 | tf_op jit(solution)/shard_map/ppermute | solution.py:200
  80.3 11.3 %collective-permute-start.14 = (bf16[136,1024]{1,0:T(8,128)(2,1)S(1)}, bf16[136,1024]{1,0:T(8,128)(2,1)S(1)}, u32[]{:S(2)}, u32[]{:S(2)}) collective-permute-start(bf16[136,1024]{1,0:T(8,128)(2,1)S(1)} %get-tuple-element.131), channel_id=1, source_target_pairs={{0,24},{4,28},{8,16},{12,20},{16,8},{20,12},{24,0},{28,4},{1,25},{... | collective-permute-start | bytes 835592 | tf_op jit(solution)/shard_map/ppermute | solution.py:200
  91.9 17.8 %collective-permute-start.15 = (bf16[256,1024]{1,0:T(8,128)(2,1)S(1)}, bf16[256,1024]{1,0:T(8,128)(2,1)S(1)}, u32[]{:S(2)}, u32[]{:S(2)}) collective-permute-start(bf16[256,1024]{1,0:T(8,128)(2,1)S(1)} %add_convert_fusion.2), channel_id=1, source_target_pairs={{1,0},{2,3},{5,4},{6,7},{9,8},{10,11},{13,12},{14,15},{17,16},{18,... | collective-permute-start | bytes 1572872 | tf_op jit(solution)/shard_map/ppermute | solution.py:186
  93.4 16.3 %collective-permute-start.19 = (bf16[544,1024]{1,0:T(8,128)(2,1)S(1)}, bf16[544,1024]{1,0:T(8,128)(2,1)S(1)}, u32[]{:S(2)}, u32[]{:S(2)}) collective-permute-start(bf16[544,1024]{1,0:T(8,128)(2,1)S(1)} %pad_maximum_fusion.3), channel_id=1, source_target_pairs={{0,4},{4,0},{8,12},{12,8},{16,20},{20,16},{24,28},{28,24},{1,5},{5... | collective-permute-start | bytes 3342344 | tf_op jit(solution)/shard_map/ppermute | solution.py:203
  94.3 9.5 %collective-permute-start.16 = (bf16[136,1024]{1,0:T(8,128)(2,1)S(1)}, bf16[136,1024]{1,0:T(8,128)(2,1)S(1)}, u32[]{:S(2)}, u32[]{:S(2)}) collective-permute-start(bf16[136,1024]{1,0:T(8,128)(2,1)S(1)} %get-tuple-element.129), channel_id=1, source_target_pairs={{0,8},{4,12},{8,0},{12,4},{16,24},{20,28},{24,16},{28,20},{1,9},{5... | collective-permute-start | bytes 835592 | tf_op jit(solution)/shard_map/ppermute | solution.py:200
  94.9 14.7 %collective-permute-start.17 = (bf16[136,1024]{1,0:T(8,128)(2,1)S(1)}, bf16[136,1024]{1,0:T(8,128)(2,1)S(1)}, u32[]{:S(2)}, u32[]{:S(2)}) collective-permute-start(bf16[136,1024]{1,0:T(8,128)(2,1)S(1)} %get-tuple-element.128), channel_id=1, source_target_pairs={{0,16},{4,20},{8,24},{12,28},{16,0},{20,4},{24,8},{28,12},{1,17},{... | collective-permute-start | bytes 835592 | tf_op jit(solution)/shard_map/ppermute | solution.py:200
  96.3 13.4 %collective-permute-start.18 = (bf16[136,1024]{1,0:T(8,128)(2,1)S(1)}, bf16[136,1024]{1,0:T(8,128)(2,1)S(1)}, u32[]{:S(2)}, u32[]{:S(2)}) collective-permute-start(bf16[136,1024]{1,0:T(8,128)(2,1)S(1)} %get-tuple-element.127), channel_id=1, source_target_pairs={{0,24},{4,28},{8,16},{12,20},{16,8},{20,12},{24,0},{28,4},{1,25},{... | collective-permute-start | bytes 835592 | tf_op jit(solution)/shard_map/ppermute | solution.py:200
  110.5 9.9 %collective-permute-start.20 = (bf16[136,1024]{1,0:T(8,128)(2,1)S(1)}, bf16[136,1024]{1,0:T(8,128)(2,1)S(1)}, u32[]{:S(2)}, u32[]{:S(2)}) collective-permute-start(bf16[136,1024]{1,0:T(8,128)(2,1)S(1)} %get-tuple-element.125), channel_id=1, source_target_pairs={{0,8},{4,12},{8,0},{12,4},{16,24},{20,28},{24,16},{28,20},{1,9},{5... | collective-permute-start | bytes 835592 | tf_op jit(solution)/shard_map/ppermute | solution.py:200
  112.0 13.6 %collective-permute-start.21 = (bf16[136,1024]{1,0:T(8,128)(2,1)S(1)}, bf16[136,1024]{1,0:T(8,128)(2,1)S(1)}, u32[]{:S(2)}, u32[]{:S(2)}) collective-permute-start(bf16[136,1024]{1,0:T(8,128)(2,1)S(1)} %get-tuple-element.124), channel_id=1, source_target_pairs={{0,16},{4,20},{8,24},{12,28},{16,0},{20,4},{24,8},{28,12},{1,17},{... | collective-permute-start | bytes 835592 | tf_op jit(solution)/shard_map/ppermute | solution.py:200
  112.7 12.9 %collective-permute-start.22 = (bf16[136,1024]{1,0:T(8,128)(2,1)S(1)}, bf16[136,1024]{1,0:T(8,128)(2,1)S(1)}, u32[]{:S(2)}, u32[]{:S(2)}) collective-permute-start(bf16[136,1024]{1,0:T(8,128)(2,1)S(1)} %get-tuple-element.123), channel_id=1, source_target_pairs={{0,24},{4,28},{8,16},{12,20},{16,8},{20,12},{24,0},{28,4},{1,25},{... | collective-permute-start | bytes 835592 | tf_op jit(solution)/shard_map/ppermute | solution.py:200
  114.1 11.5 %collective-permute-start.23 = (bf16[544,1024]{1,0:T(8,128)(2,1)S(1)}, bf16[544,1024]{1,0:T(8,128)(2,1)S(1)}, u32[]{:S(2)}, u32[]{:S(2)}) collective-permute-start(bf16[544,1024]{1,0:T(8,128)(2,1)S(1)} %pad_maximum_fusion.4), channel_id=1, source_target_pairs={{0,4},{4,0},{8,12},{12,8},{16,20},{20,16},{24,28},{28,24},{1,5},{5... | collective-permute-start | bytes 3342344 | tf_op jit(solution)/shard_map/ppermute | solution.py:203
  114.2 2.1 copy-start.14
  116.3 2.1 copy-start.15
  129.6 2.8 %collective-permute-start.24 = (bf16[544,1024]{1,0:T(8,128)(2,1)S(1)}, bf16[544,1024]{1,0:T(8,128)(2,1)S(1)}, u32[]{:S(2)}, u32[]{:S(2)}) collective-permute-start(bf16[544,1024]{1,0:T(8,128)(2,1)S(1)} %pad_maximum_fusion.5), channel_id=1, source_target_pairs={{0,4},{4,0},{8,12},{12,8},{16,20},{20,16},{24,28},{28,24},{1,5},{5... | collective-permute-start | bytes 3342344 | tf_op jit(solution)/shard_map/ppermute | solution.py:203
  137.7 2.1 copy-start.16
  139.8 3.0 %copy-start.8 = (bf16[1088,640]{1,0:T(8,128)(2,1)}, bf16[1088,640]{1,0:T(8,128)(2,1)S(1)}, u32[]{:S(2)}) copy-start(bf16[1088,640]{1,0:T(8,128)(2,1)S(1)} %multiply_convert_fusion) | copy-start | bytes 4177924
  142.8 1.7 copy-start.2
  144.6 1.5 copy-start.7
  145.9 0.7 copy-start.12
  145.9 6.1 %collective-permute-start.25 = (bf16[544,1536]{1,0:T(8,128)(2,1)}, bf16[544,1536]{1,0:T(8,128)(2,1)}, u32[]{:S(2)}, u32[]{:S(2)}) collective-permute-start(bf16[544,1536]{1,0:T(8,128)(2,1)} %slice.201), channel_id=1, source_target_pairs={{0,4},{4,0},{8,12},{12,8},{16,20},{20,16},{24,28},{28,24},{1,5},{5... | collective-permute-start | bytes 5013512 | tf_op jit(solution)/shard_map/ppermute | solution.py:274
  146.0 1.3 copy-start.9
  151.9 1.7 copy-start.3
  154.9 24.2 %collective-permute-start.29 = (bf16[544,1536]{1,0:T(8,128)(2,1)}, bf16[544,1536]{1,0:T(8,128)(2,1)}, u32[]{:S(2)}, u32[]{:S(2)}) collective-permute-start(bf16[544,1536]{1,0:T(8,128)(2,1)} %slice.177), channel_id=1, source_target_pairs={{0,4},{4,0},{8,12},{12,8},{16,20},{20,16},{24,28},{28,24},{1,5},{5... | collective-permute-start | bytes 5013512 | tf_op jit(solution)/shard_map/ppermute | solution.py:274
  157.8 21.3 %copy-start.4 = (bf16[1088,1536]{1,0:T(8,128)(2,1)S(1)}, bf16[1088,1536]{1,0:T(8,128)(2,1)}, u32[]{:S(2)}) copy-start(bf16[1088,1536]{1,0:T(8,128)(2,1)} %copy-done.3) | copy-start | bytes 10027012
  157.9 12.6 %collective-permute-start.26 = (bf16[136,1536]{1,0:T(8,128)(2,1)S(1)}, bf16[136,1536]{1,0:T(8,128)(2,1)S(1)}, u32[]{:S(2)}, u32[]{:S(2)}) collective-permute-start(bf16[136,1536]{1,0:T(8,128)(2,1)S(1)} %get-tuple-element.120), channel_id=1, source_target_pairs={{0,8},{4,12},{8,0},{12,4},{16,24},{20,28},{24,16},{28,20},{1,9},{5... | collective-permute-start | bytes 1253384 | tf_op jit(solution)/shard_map/ppermute | solution.py:272
  158.8 20.4 %collective-permute-start.27 = (bf16[136,1536]{1,0:T(8,128)(2,1)S(1)}, bf16[136,1536]{1,0:T(8,128)(2,1)S(1)}, u32[]{:S(2)}, u32[]{:S(2)}) collective-permute-start(bf16[136,1536]{1,0:T(8,128)(2,1)S(1)} %get-tuple-element.119), channel_id=1, source_target_pairs={{0,16},{4,20},{8,24},{12,28},{16,0},{20,4},{24,8},{28,12},{1,17},{... | collective-permute-start | bytes 1253384 | tf_op jit(solution)/shard_map/ppermute | solution.py:272
  160.1 19.1 %collective-permute-start.28 = (bf16[136,1536]{1,0:T(8,128)(2,1)S(1)}, bf16[136,1536]{1,0:T(8,128)(2,1)S(1)}, u32[]{:S(2)}, u32[]{:S(2)}) collective-permute-start(bf16[136,1536]{1,0:T(8,128)(2,1)S(1)} %get-tuple-element.118), channel_id=1, source_target_pairs={{0,24},{4,28},{8,16},{12,20},{16,8},{20,12},{24,0},{28,4},{1,25},{... | collective-permute-start | bytes 1253384 | tf_op jit(solution)/shard_map/ppermute | solution.py:272
  181.2 27.1 %collective-permute-start.33 = (bf16[136,1536]{1,0:T(8,128)(2,1)S(1)}, bf16[136,1536]{1,0:T(8,128)(2,1)S(1)}, u32[]{:S(2)}, u32[]{:S(2)}) collective-permute-start(bf16[136,1536]{1,0:T(8,128)(2,1)S(1)} %get-tuple-element.116), channel_id=1, source_target_pairs={{0,8},{4,12},{8,0},{12,4},{16,24},{20,28},{24,16},{28,20},{1,9},{5... | collective-permute-start | bytes 1253384 | tf_op jit(solution)/shard_map/ppermute | solution.py:272
  182.5 25.8 %collective-permute-start.34 = (bf16[136,1536]{1,0:T(8,128)(2,1)S(1)}, bf16[136,1536]{1,0:T(8,128)(2,1)S(1)}, u32[]{:S(2)}, u32[]{:S(2)}) collective-permute-start(bf16[136,1536]{1,0:T(8,128)(2,1)S(1)} %get-tuple-element.115), channel_id=1, source_target_pairs={{0,16},{4,20},{8,24},{12,28},{16,0},{20,4},{24,8},{28,12},{1,17},{... | collective-permute-start | bytes 1253384 | tf_op jit(solution)/shard_map/ppermute | solution.py:272
  183.1 25.1 %collective-permute-start.35 = (bf16[136,1536]{1,0:T(8,128)(2,1)S(1)}, bf16[136,1536]{1,0:T(8,128)(2,1)S(1)}, u32[]{:S(2)}, u32[]{:S(2)}) collective-permute-start(bf16[136,1536]{1,0:T(8,128)(2,1)S(1)} %get-tuple-element.114), channel_id=1, source_target_pairs={{0,24},{4,28},{8,16},{12,20},{16,8},{20,12},{24,0},{28,4},{1,25},{... | collective-permute-start | bytes 1253384 | tf_op jit(solution)/shard_map/ppermute | solution.py:272
  186.5 11.7 %collective-permute-start.30 = (bf16[64,1536]{1,0:T(8,128)(2,1)S(1)}, bf16[64,1536]{1,0:T(8,128)(2,1)S(1)}, u32[]{:S(2)}, u32[]{:S(2)}) collective-permute-start(bf16[64,1536]{1,0:T(8,128)(2,1)S(1)} %get-tuple-element.140), channel_id=1, source_target_pairs={{0,1},{1,0},{2,3},{3,2},{4,5},{5,4},{6,7},{7,6},{8,9},{9,8},{10,11... | collective-permute-start | bytes 589832 | tf_op jit(solution)/shard_map/ppermute | solution.py:267
  192.7 15.6 %collective-permute-start.31 = (bf16[64,1536]{1,0:T(8,128)(2,1)S(1)}, bf16[64,1536]{1,0:T(8,128)(2,1)S(1)}, u32[]{:S(2)}, u32[]{:S(2)}) collective-permute-start(bf16[64,1536]{1,0:T(8,128)(2,1)S(1)} %get-tuple-element.139), channel_id=1, source_target_pairs={{0,2},{1,3},{2,0},{3,1},{4,6},{5,7},{6,4},{7,5},{8,10},{9,11},{10,... | collective-permute-start | bytes 589832 | tf_op jit(solution)/shard_map/ppermute | solution.py:267
  198.1 10.1 %collective-permute-start.32 = (bf16[64,1536]{1,0:T(8,128)(2,1)S(1)}, bf16[64,1536]{1,0:T(8,128)(2,1)S(1)}, u32[]{:S(2)}, u32[]{:S(2)}) collective-permute-start(bf16[64,1536]{1,0:T(8,128)(2,1)S(1)} %get-tuple-element.138), channel_id=1, source_target_pairs={{0,3},{1,2},{2,1},{3,0},{4,7},{5,6},{6,5},{7,4},{8,11},{9,10},{10,... | collective-permute-start | bytes 589832 | tf_op jit(solution)/shard_map/ppermute | solution.py:267
  209.1 24.0 %copy-start.1 = (bf16[256,1024]{1,0:T(8,128)(2,1)S(1)}, bf16[256,1024]{1,0:T(8,128)(2,1)}, u32[]{:S(2)}) copy-start(bf16[256,1024]{1,0:T(8,128)(2,1)} %param.13) | copy-start | bytes 1572868
  209.9 0.9 copy-start.10
  211.7 9.0 %collective-permute-start.36 = (bf16[64,1536]{1,0:T(8,128)(2,1)}, bf16[64,1536]{1,0:T(8,128)(2,1)}, u32[]{:S(2)}, u32[]{:S(2)}) collective-permute-start(bf16[64,1536]{1,0:T(8,128)(2,1)} %get-tuple-element.137), channel_id=1, source_target_pairs={{0,1},{1,0},{2,3},{3,2},{4,5},{5,4},{6,7},{7,6},{8,9},{9,8},{10,11... | collective-permute-start | bytes 589832 | tf_op jit(solution)/shard_map/ppermute | solution.py:267
  214.8 16.0 %collective-permute-start.37 = (bf16[64,1536]{1,0:T(8,128)(2,1)}, bf16[64,1536]{1,0:T(8,128)(2,1)}, u32[]{:S(2)}, u32[]{:S(2)}) collective-permute-start(bf16[64,1536]{1,0:T(8,128)(2,1)} %get-tuple-element.136), channel_id=1, source_target_pairs={{0,2},{1,3},{2,0},{3,1},{4,6},{5,7},{6,4},{7,5},{8,10},{9,11},{10,... | collective-permute-start | bytes 589832 | tf_op jit(solution)/shard_map/ppermute | solution.py:267
  214.8 16.0 %collective-permute-start.38 = (bf16[64,1536]{1,0:T(8,128)(2,1)}, bf16[64,1536]{1,0:T(8,128)(2,1)}, u32[]{:S(2)}, u32[]{:S(2)}) collective-permute-start(bf16[64,1536]{1,0:T(8,128)(2,1)} %get-tuple-element.135), channel_id=1, source_target_pairs={{0,3},{1,2},{2,1},{3,0},{4,7},{5,6},{6,5},{7,4},{8,11},{9,10},{10,... | collective-permute-start | bytes 589832 | tf_op jit(solution)/shard_map/ppermute | solution.py:267

commit v3 on v2

--- a/solution.py
+++ b/solution.py
@@ -1,17 +1,165 @@
+import functools
+
 import jax
 import jax.numpy as jnp
 from jax import lax
+from jax.experimental import pallas as pl
+from jax.experimental.pallas import tpu as pltpu
 from jax.sharding import PartitionSpec as P
 
 EPSILON = 1e-06
 BF = jnp.bfloat16
 F32 = jnp.float32
 CHUNKS = 3
-CHUNKS_BACK = 2
+CHUNKS_BACK = 3
 
 
 def xor_pairs(count, step):
     return [(i, i ^ step) for i in range(count)]
+
+
+def dot(a, b):
+    return jnp.dot(a, b, preferred_element_type=F32)
+
+
+def gate_up_kernel(parts, *refs):
+    rows = refs[:parts]
+    gate_hbm, up_hbm, gate_out, up_out, squares_out, gate_w, up_w, sems = refs[parts:]
+    depth = gate_w.shape[0]
+    wide = depth // parts
+    copies = [
+        pltpu.make_async_copy(hbm.at[0, pl.ds(0, depth)], vmem, sems.at[k])
+        for k, (hbm, vmem) in enumerate(((gate_hbm, gate_w), (up_hbm, up_w)))
+    ]
+    for copy in copies:
+        copy.start()
+    for copy in copies:
+        copy.wait()
+    tile = rows[0].shape[0] // 2
+
+    def step(t, carry):
+        at = pl.ds(pl.multiple_of(t * tile, 16), tile)
+        gate = up = squares = None
+        for p in range(parts):
+            x = rows[p][at, :]
+            x_wide = x.astype(F32)
+            depths = slice(p * wide, (p + 1) * wide)
+            new = (
+                dot(x, gate_w[depths, :]),
+                dot(x, up_w[depths, :]),
+                jnp.sum(x_wide * x_wide, axis=-1, keepdims=True),
+            )
+            gate, up, squares = new if p == 0 else (gate + new[0], up + new[1], squares + new[2])
+        gate_out[at, :] = gate
+        up_out[at, :] = up
+        squares_out[at, :] = jnp.broadcast_to(squares, (tile, squares_out.shape[1]))
+        return carry
+
+    lax.fori_loop(0, 2, step, 0)
+
+
+def expert_kernel(
+    width, rows, gate_in, up_in, squares_in, gate_hbm, up_hbm, down_hbm, *refs
+):
+    outs = refs[:-5]
+    gate_w, up_w, down_w, act, sems = refs[-5:]
+    slots, wide = rows.shape
+    copies = [
+        pltpu.make_async_copy(hbm, vmem, sems.at[k])
+        for k, (hbm, vmem) in enumerate(
+            (
+                (gate_hbm.at[0, pl.ds(width - wide, wide)], gate_w),
+                (up_hbm.at[0, pl.ds(width - wide, wide)], up_w),
+                (down_hbm.at[0], down_w),
+            )
+        )
+    ]
+    for copy in copies:
+        copy.start()
+    copies[0].wait()
+    copies[1].wait()
+    tile = slots // 2
+
+    def step(t, carry):
+        at = pl.ds(pl.multiple_of(t * tile, 16), tile)
+        x = rows[at, :]
+        x_wide = x.astype(F32)
+        squares = squares_in[at, :1] + jnp.sum(x_wide * x_wide, axis=-1, keepdims=True)
+        scale = lax.rsqrt(squares / width + EPSILON)
+        gate = (gate_in[at, :] + dot(x, gate_w[...])) * scale
+        up = (up_in[at, :] + dot(x, up_w[...])) * scale
+        act[at, :] = (gate * (1.0 / (1.0 + jnp.exp(-gate))) * up).astype(BF)
+        return carry
+
+    lax.fori_loop(0, 2, step, 0)
+    copies[2].wait()
+    left = 0
+    for out in outs:
+        cols = slice(left, left + out.shape[1])
+        left += out.shape[1]
+
+        def lower(t, carry, out=out, cols=cols):
+            at = pl.ds(pl.multiple_of(t * tile, 16), tile)
+            out[at, :] = dot(act[at, :], down_w[:, cols]).astype(BF)
+            return carry
+
+        lax.fori_loop(0, 2, lower, 0)
+
+
+VMEM = pl.BlockSpec(memory_space=pltpu.VMEM)
+ANY = pl.BlockSpec(memory_space=pl.ANY)
+VMEM_LIMIT = 40 * 1024 * 1024
+
+
+def gate_up_first(rows, gate_weight, up_weight):
+    slots, wide = rows[0].shape
+    units = gate_weight.shape[2]
+    depth = wide * len(rows)
+    return pl.pallas_call(
+        functools.partial(gate_up_kernel, len(rows)),
+        out_shape=(
+            jax.ShapeDtypeStruct((slots, units), F32),
+            jax.ShapeDtypeStruct((slots, units), F32),
+            jax.ShapeDtypeStruct((slots, 128), F32),
+        ),
+        in_specs=[VMEM] * len(rows) + [ANY] * 2,
+        out_specs=(VMEM,) * 3,
+        scratch_shapes=[
+            pltpu.VMEM((depth, units), BF),
+            pltpu.VMEM((depth, units), BF),
+            pltpu.SemaphoreType.DMA((2,)),
+        ],
+        compiler_params=pltpu.CompilerParams(vmem_limit_bytes=VMEM_LIMIT),
+        cost_estimate=pl.CostEstimate(
+            flops=4 * slots * depth * units,
+            bytes_accessed=4 * depth * units + 2 * slots * depth + 8 * slots * units,
+            transcendentals=0,
+        ),
+    )(*rows, gate_weight, up_weight)
+
+
+def expert_last(rows, first, gate_weight, up_weight, down_weight, chunks):
+    slots, wide = rows.shape
+    units, width = down_weight.shape[1:]
+    return pl.pallas_call(
+        functools.partial(expert_kernel, width),
+        out_shape=tuple(jax.ShapeDtypeStruct((slots, width // chunks), BF) for _ in range(chunks)),
+        in_specs=[VMEM] * 4 + [ANY] * 3,
+        out_specs=(VMEM,) * chunks,
+        scratch_shapes=[
+            pltpu.VMEM((wide, units), BF),
+            pltpu.VMEM((wide, units), BF),
+            pltpu.VMEM((units, width), BF),
+            pltpu.VMEM((slots, units), BF),
+            pltpu.SemaphoreType.DMA((3,)),
+        ],
+        compiler_params=pltpu.CompilerParams(vmem_limit_bytes=VMEM_LIMIT),
+        cost_estimate=pl.CostEstimate(
+            flops=4 * slots * wide * units + 2 * slots * units * width,
+            bytes_accessed=2 * units * (2 * wide + width) + 2 * slots * (wide + width) + 8 * slots * units,
+            transcendentals=slots * units,
+        ),
+    )(rows, *first, gate_weight, up_weight, down_weight)
 
 
 def together(values):
@@ -159,16 +307,13 @@
     total = {}
     mine = {}
     theirs = {}
-    gate_act = None
-    up_act = None
-    in_squares = None
 
     def project(i):
         cols = slice(i * wide, (i + 1) * wide)
         return jnp.dot(attention, out_weight[:, cols], preferred_element_type=F32).astype(BF)
 
     part = {0: project(0)}
-    for r in range(chunks + stages + 2):
+    for r in range(chunks + stages + 1):
         done = {}
         for side in range(reach - 1):
             inner = r - side
@@ -201,16 +346,21 @@
         i = r - stages - 1
         if 0 <= i < chunks:
             done["theirs"] = lax.ppermute(mine[i], "seq", xor_pairs(seq_count, 1))
-        i = r - stages - 2
-        if 0 <= i < chunks:
-            rows = jnp.concatenate([mine[i], theirs[i]], axis=0)
-            squares = jnp.sum(jnp.square(rows.astype(F32)), axis=-1, keepdims=True)
-            depth = slice(i * wide, (i + 1) * wide)
-            gate_part = jnp.dot(rows, gate_weight[0, depth], preferred_element_type=F32)
-            up_part = jnp.dot(rows, up_weight[0, depth], preferred_element_type=F32)
-            done["squares"] = squares if i == 0 else in_squares + squares
-            done["gate"] = gate_part if i == 0 else gate_act + gate_part
-            done["up"] = up_part if i == 0 else up_act + up_part
+        if r == stages + chunks - 1:
+            theirs[chunks - 2] = done["theirs"]
+            firsts = {
+                "mine": gate_up_first([mine[i] for i in range(chunks - 1)], gate_weight, up_weight),
+                "theirs": gate_up_first(
+                    [theirs[i] for i in range(chunks - 1)], gate_weight, up_weight
+                ),
+            }
+            for side in firsts:
+                for k in range(3):
+                    done["first", side, k] = firsts[side][k]
+        if r == stages + chunks:
+            done["lowered"] = expert_last(
+                mine[chunks - 1], firsts["mine"], gate_weight, up_weight, down_weight, CHUNKS_BACK
+            )
         if r + 1 < chunks:
             done["part"] = project(r + 1)
         done = together(done)
@@ -231,10 +381,14 @@
             mine[r - stages] = jnp.concatenate([done["group", g] for g in range(chips)], axis=0)
         if "theirs" in done:
             theirs[r - stages - 1] = done["theirs"]
-        if "gate" in done:
-            gate_act, up_act, in_squares = done["gate"], done["up"], done["squares"]
-    in_scale = lax.rsqrt(in_squares / width + EPSILON)
-    active = (jax.nn.silu(gate_act * in_scale) * (up_act * in_scale)).astype(BF)
+        if ("first", "mine", 0) in done:
+            firsts = {
+                side: [done["first", side, k] for k in range(3)] for side in ("mine", "theirs")
+            }
+    kept = done["lowered"]
+    partials = expert_last(
+        theirs[chunks - 1], firsts["theirs"], gate_weight, up_weight, down_weight, CHUNKS_BACK
+    )
 
     hidden = jnp.concatenate([hidden[i] for i in range(chunks)], axis=1)
     squares = jnp.sum(jnp.square(hidden.astype(F32)), axis=-1, keepdims=True)
@@ -250,35 +404,30 @@
     mixes = {}
     own = {}
 
-    def lower(i):
-        cols = slice(i * wide, (i + 1) * wide)
-        return jnp.dot(active, down_weight[0, :, cols], preferred_element_type=F32).astype(BF)
-
     def own_rows(value, index):
         return lax.dynamic_slice_in_dim(value, index * own_count, own_count, 0)
 
-    partials = {0: lower(0)}
     for r in range(chunks + 2):
         done = {}
-        i = r - 2
-        if 0 <= i < chunks:
-            for step in range(1, exp_count):
-                block = own_rows(mixes[i], jnp.bitwise_xor(exp_index, step))
-                done["own", step] = lax.ppermute(block, "exp", xor_pairs(exp_count, step))
         i = r - 1
         if 0 <= i < chunks:
             for g in range(1, chips):
                 block = sums[i][g * capacity : (g + 1) * capacity]
                 done["table", g] = lax.ppermute(block, "seq", xor_pairs(seq_count, 2 * g))
-        if r < chunks:
-            done["got"] = lax.ppermute(partials[r][slots:], "seq", xor_pairs(seq_count, 1))
-        if r + 1 < chunks:
-            done["partials"] = lower(r + 1)
+        i = r - 2
+        if 0 <= i < chunks:
+            for step in range(exp_count - 1, 0, -1):
+                block = own_rows(mixes[i], jnp.bitwise_xor(exp_index, step))
+                done["own", step] = lax.ppermute(block, "exp", xor_pairs(exp_count, step))
+        for i in range(chunks):
+            if r == min(i, 1):
+                done["got", i] = lax.ppermute(partials[i], "seq", xor_pairs(seq_count, 1))
         done = together(done)
-        if "partials" in done:
-            partials[r + 1] = done["partials"]
-        if "got" in done:
-            sums[r] = (partials[r][:slots].astype(F32) + done["got"].astype(F32)).astype(BF)
+        for i in range(chunks):
+            if ("got", i) in done:
+                sums[i] = (
+                    kept[i].astype(F32) + done["got", i].astype(F32)
+                ).astype(BF)
         i = r - 1
         if 0 <= i < chunks:
             table = jnp.concatenate(

time: 234 us -> 220 us (0.940)
  Pallas kernels: 0 us -> 24.2 us
  matrix products: 36.1 us -> 16.4 us
  waiting for transfers between devices: 106 us -> 91.5 us
  local copies, waits for them, and re-layouts: 14.9 us -> 6.24 us
  starting transfers between devices: 53.7 us -> 60.5 us
    pallas_call x0 -> x4, Pallas kernels: none -> 24.2 us  [the longest x2 15.8 us: expert_last(): pl.pallas_call(functools.partial(expert_kernel, width), out_shape=tuple((...]
    dot_general x8 -> x0, matrix products: 19.2 us -> none  [the longest x2 7.55 us: lower(): jnp.dot(active, down_weight[0, :, cols], preferred_element_type=F32)]
    ppermute x6 -> x9, waiting for transfers between devices: 27.4 us -> 11 us  [body(): done['own', step] = lax.ppermute(block, 'exp', xor_pairs(exp_count, step))]
    unnamed x46 -> x41, local copies, waits for them, and re-layouts: 7.88 us -> 2.51 us
    ppermute x6 -> x9, starting transfers between devices: 7.11 us -> 11.3 us  [body(): done['table', g] = lax.ppermute(block, 'seq', xor_pairs(seq_count, 2 * g))]
    ppermute x6 -> x9, waiting for transfers between devices: 17.6 us -> 21 us  [body(): done['table', g] = lax.ppermute(block, 'seq', xor_pairs(seq_count, 2 * g))]
    ppermute x5, starting transfers between devices: 14.7 us -> 17.7 us  [body(): lax.ppermute(load, 'exp', (ins if has_in else []) + (outs if has_out else...]
    slice x2 -> x0, local copies, waits for them, and re-layouts: 2.61 us -> none  [body(): partials[r][slots:]]
  transfers between devices with their start and end apart: 39 -> 46, of which waited for: 19 -> 23; matrix products, arithmetic and copies ran while one was open for 10% -> 8% of each run, Pallas kernels for 0% -> 7%
where the time goes in v3:
time: 220 us; the launch traced here: 219 us
  waiting for transfers between devices  91.5 us (42%)
  starting transfers between devices  60.5 us (28%)
  Pallas kernels  24.2 us (11%)
  matrix products  16.4 us (7%)
  other arithmetic  15.5 us (7%)
  local copies, waits for them, and re-layouts  6.24 us (3%)
  between operations  4.69 us (2%)
    ppermute x5, waiting for transfers between devices, body(): lax.ppermute(load, 'exp', (ins if has_in else []) + (outs if has_out else...  26.8 us
    ppermute x9, waiting for transfers between devices, body(): done['group', g] = lax.ppermute(block, 'seq', xor_pairs(seq_count, 2 * g))  25.4 us
    ppermute x9, waiting for transfers between devices, body(): done['table', g] = lax.ppermute(block, 'seq', xor_pairs(seq_count, 2 * g))  21 us
    ppermute x5, starting transfers between devices, body(): lax.ppermute(load, 'exp', (ins if has_in else []) + (outs if has_out else...  17.7 us
    pallas_call x2, Pallas kernels, expert_last(): pl.pallas_call(functools.partial(expert_kernel, width), out_shape=tuple((...  15.8 us
    ppermute x9, starting transfers between devices, body(): done['own', step] = lax.ppermute(block, 'exp', xor_pairs(exp_count, step))  12.8 us
    ppermute x9, starting transfers between devices, body(): done['table', g] = lax.ppermute(block, 'seq', xor_pairs(seq_count, 2 * g))  11.3 us
    ppermute x9, waiting for transfers between devices, body(): done['own', step] = lax.ppermute(block, 'exp', xor_pairs(exp_count, step))  11 us
  transfers between devices with their start and end apart: 46, of which 23 were waited for; matrix products, arithmetic and copies ran while one was open for 8% of the time, Pallas kernels for 7%

profile of v3, /device:TPU:0, one launch (start us, length us, event | category | flops | bytes accessed | tf_op | source)
XLA Modules:
  0.0 219.0 jit_solution(3797578944168877263)
XLA Ops:
  1.0 1.4 fusion.68
  3.8 1.3 copy.40
  5.1 1.3 compare_convert_fusion.1
  11.1 2.6 %collective-permute-start.1 = (bf16[4,128,128]{2,1,0:T(8,128)(2,1)S(1)}, bf16[4,128,128]{2,1,0:T(8,128)(2,1)S(1)}, u32[]{:S(2)}, u32[]{:S(2)}) collective-permute-start(bf16[4,128,128]{2,1,0:T(8,128)(2,1)S(1)} %fusion.61), channel_id=1, source_target_pairs={{0,8},{4,12},{8,0},{12,4},{16,24},{20,28},{24,16},{28,20},{1,9},{5... | collective-permute-start | bytes 393224 | tf_op jit(solution)/shard_map/ppermute | solution.py:237
  13.7 1.5 collective-permute-start.2
  15.9 2.1 collective-permute-done.1
  17.9 4.2 %collective-permute-done.2 = bf16[4,128,128]{2,1,0:T(8,128)(2,1)S(1)} collective-permute-done((bf16[4,128,128]{2,1,0:T(8,128)(2,1)S(1)}, bf16[4,128,128]{2,1,0:T(8,128)(2,1)S(1)}, u32[]{:S(2)}, u32[]{:S(2)}) %collective-permute-start.2) | collective-permute-done | bytes 131104 | tf_op jit(solution)/shard_map/ppermute | solution.py:237
  22.5 1.2 collective-permute-done.4
  24.3 2.0 multiply_reduce_fusion.1
  26.4 2.3 %fusion.16 = bf16[256,1024]{1,0:T(8,128)(2,1)S(1)} fusion(bf16[256,1024]{0,1:T(8,128)(2,1)S(1)} %bitcast.56, bf16[1024,3072]{1,0:T(8,128)(2,1)} %param.18), kind=kOutput, calls=%fused_computation.32 | convolution fusion | flops 537133056 | bytes 3145728 | tf_op jit(solution)/shard_map/dot_general | solution.py:313
  28.8 3.5 %collective-permute-start.5 = (bf16[256,1024]{1,0:T(8,128)(2,1)S(1)}, bf16[256,1024]{1,0:T(8,128)(2,1)S(1)}, u32[]{:S(2)}, u32[]{:S(2)}) collective-permute-start(bf16[256,1024]{1,0:T(8,128)(2,1)S(1)} %fusion.16), channel_id=1, source_target_pairs={{0,1},{3,2},{4,5},{7,6},{8,9},{11,10},{12,13},{15,14},{16,17},{19,... | collective-permute-start | bytes 1572872 | tf_op jit(solution)/shard_map/ppermute | solution.py:331
  32.3 2.3 %fusion.19 = bf16[256,1024]{1,0:T(8,128)(2,1)S(1)} fusion(bf16[256,1024]{0,1:T(8,128)(2,1)S(1)} %bitcast.57, bf16[1024,3072]{1,0:T(8,128)(2,1)} %param.18), kind=kOutput, calls=%fused_computation.33 | convolution fusion | flops 537133056 | bytes 3145728 | tf_op jit(solution)/shard_map/dot_general | solution.py:313
  34.6 9.1 %collective-permute-done.5 = bf16[256,1024]{1,0:T(8,128)(2,1)S(1)} collective-permute-done((bf16[256,1024]{1,0:T(8,128)(2,1)S(1)}, bf16[256,1024]{1,0:T(8,128)(2,1)S(1)}, u32[]{:S(2)}, u32[]{:S(2)}) %collective-permute-start.5) | collective-permute-done | bytes 524320 | tf_op jit(solution)/shard_map/ppermute | solution.py:331
  44.6 7.2 %collective-permute-start.6 = (bf16[256,1024]{1,0:T(8,128)(2,1)S(1)}, bf16[256,1024]{1,0:T(8,128)(2,1)S(1)}, u32[]{:S(2)}, u32[]{:S(2)}) collective-permute-start(bf16[256,1024]{1,0:T(8,128)(2,1)S(1)} %fusion.19), channel_id=1, source_target_pairs={{0,1},{3,2},{4,5},{7,6},{8,9},{11,10},{12,13},{15,14},{16,17},{19,... | collective-permute-start | bytes 1572872 | tf_op jit(solution)/shard_map/ppermute | solution.py:331
  52.0 2.4 %fusion.22 = bf16[256,1024]{1,0:T(8,128)(2,1)S(1)} fusion(bf16[256,1024]{0,1:T(8,128)(2,1)S(1)} %bitcast.58, bf16[1024,3072]{1,0:T(8,128)(2,1)} %param.18), kind=kOutput, calls=%fused_computation.34 | convolution fusion | flops 537133056 | bytes 3145728 | tf_op jit(solution)/shard_map/dot_general | solution.py:313
  54.4 7.8 %collective-permute-done.6 = bf16[256,1024]{1,0:T(8,128)(2,1)S(1)} collective-permute-done((bf16[256,1024]{1,0:T(8,128)(2,1)S(1)}, bf16[256,1024]{1,0:T(8,128)(2,1)S(1)}, u32[]{:S(2)}, u32[]{:S(2)}) %collective-permute-start.6) | collective-permute-done | bytes 524320 | tf_op jit(solution)/shard_map/ppermute | solution.py:331
  63.5 4.2 %collective-permute-start.8 = (bf16[256,1024]{1,0:T(8,128)(2,1)S(1)}, bf16[256,1024]{1,0:T(8,128)(2,1)S(1)}, u32[]{:S(2)}, u32[]{:S(2)}) collective-permute-start(bf16[256,1024]{1,0:T(8,128)(2,1)S(1)} %broadcast_select_fusion.3), channel_id=1, source_target_pairs={{0,1},{3,2},{1,0},{2,3},{4,5},{7,6},{5,4},{6,7},{8,9},{11,10},{9,8... | collective-permute-start | bytes 1572872 | tf_op jit(solution)/shard_map/ppermute | solution.py:331
  67.7 9.9 %collective-permute-done.8 = bf16[256,1024]{1,0:T(8,128)(2,1)S(1)} collective-permute-done((bf16[256,1024]{1,0:T(8,128)(2,1)S(1)}, bf16[256,1024]{1,0:T(8,128)(2,1)S(1)}, u32[]{:S(2)}, u32[]{:S(2)}) %collective-permute-start.8) | collective-permute-done | bytes 524320 | tf_op jit(solution)/shard_map/ppermute | solution.py:331
  79.2 1.3 collective-permute-start.10
  81.2 1.3 collective-permute-start.12
  83.3 1.4 collective-permute-start.14
  84.8 5.3 %collective-permute-done.12 = bf16[136,1024]{1,0:T(8,128)(2,1)S(1)} collective-permute-done((bf16[136,1024]{1,0:T(8,128)(2,1)S(1)}, bf16[136,1024]{1,0:T(8,128)(2,1)S(1)}, u32[]{:S(2)}, u32[]{:S(2)}) %collective-permute-start.12) | collective-permute-done | bytes 278560 | tf_op jit(solution)/shard_map/ppermute | solution.py:345
  90.0 4.0 %collective-permute-done.13 = bf16[136,1024]{1,0:T(8,128)(2,1)S(1)} collective-permute-done((bf16[136,1024]{1,0:T(8,128)(2,1)S(1)}, bf16[136,1024]{1,0:T(8,128)(2,1)S(1)}, u32[]{:S(2)}, u32[]{:S(2)}) %collective-permute-start.13) | collective-permute-done | bytes 278560 | tf_op jit(solution)/shard_map/ppermute | solution.py:345
  94.5 1.5 collective-permute-start.15
  97.7 1.4 collective-permute-start.17
  99.1 1.3 collective-permute-start.18
  100.4 6.0 %collective-permute-done.16 = bf16[136,1024]{1,0:T(8,128)(2,1)S(1)} collective-permute-done((bf16[136,1024]{1,0:T(8,128)(2,1)S(1)}, bf16[136,1024]{1,0:T(8,128)(2,1)S(1)}, u32[]{:S(2)}, u32[]{:S(2)}) %collective-permute-start.16) | collective-permute-done | bytes 278560 | tf_op jit(solution)/shard_map/ppermute | solution.py:345
  106.3 5.0 %collective-permute-done.17 = bf16[136,1024]{1,0:T(8,128)(2,1)S(1)} collective-permute-done((bf16[136,1024]{1,0:T(8,128)(2,1)S(1)}, bf16[136,1024]{1,0:T(8,128)(2,1)S(1)}, u32[]{:S(2)}, u32[]{:S(2)}) %collective-permute-start.17) | collective-permute-done | bytes 278560 | tf_op jit(solution)/shard_map/ppermute | solution.py:345
  113.5 1.2 collective-permute-start.20
  114.7 1.1 collective-permute-start.21
  115.9 1.2 collective-permute-start.22
  117.0 4.2 %shard_map.118 = (f32[544,640]{1,0:T(8,128)S(1)}, f32[544,640]{1,0:T(8,128)S(1)}, f32[544,128]{1,0:T(8,128)S(1)}) custom-call(bf16[544,1024]{1,0:T(8,128)(2,1)S(1)} %constant_dynamic-update-slice_fusion.refs_0_, bf16[544,1024]{1,0:T(8,128)(2,1)S(1)} %constant_dynamic-update-slice_fusion.4.refs_1_, bf16[1,3072,640]{2,1,0:T(8,128)(2,1)S(1)} %copy-done.2, ...), custom_call_target="tpu_custom_call" | custom-call | flops 2852126720 | bytes 10256384 | tf_op jit(solution)/shard_map/pallas_call | solution.py:118
  121.3 4.2 %shard_map.119 = (f32[544,640]{1,0:T(8,128)S(1)}, f32[544,640]{1,0:T(8,128)S(1)}, f32[544,128]{1,0:T(8,128)S(1)}) custom-call(bf16[544,1024]{1,0:T(8,128)(2,1)S(1)} %collective-permute-done.19.refs_0_, bf16[544,1024]{1,0:T(8,128)(2,1)S(1)} %collective-permute-done.23.refs_1_, bf16[1,3072,640]{2,1,0:T(8,128)(2,1)S(1)} %copy-done.2, ...), custom_call_target="tpu_custom_call" | custom-call | flops 2852126720 | bytes 10256384 | tf_op jit(solution)/shard_map/pallas_call | solution.py:118
  125.5 4.0 %collective-permute-done.21 = bf16[136,1024]{1,0:T(8,128)(2,1)S(1)} collective-permute-done((bf16[136,1024]{1,0:T(8,128)(2,1)S(1)}, bf16[136,1024]{1,0:T(8,128)(2,1)S(1)}, u32[]{:S(2)}, u32[]{:S(2)}) %collective-permute-start.21) | collective-permute-done | bytes 278560 | tf_op jit(solution)/shard_map/ppermute | solution.py:345
  129.7 7.3 %shard_map.120 = (bf16[544,1024]{1,0:T(8,128)(2,1)S(1)}, bf16[544,1024]{1,0:T(8,128)(2,1)S(1)}, bf16[544,1024]{1,0:T(8,128)(2,1)S(1)}) custom-call(bf16[544,1024]{1,0:T(8,128)(2,1)S(1)} %constant_dynamic-update-slice_fusion.8.rows, f32[544,640]{1,0:T(8,128)S(1)} %get-tuple-element.99.gate_in, f32[544,640]{1,0:T(8,128)S(1)} %get-tuple-element.100.up_in, ...), custom_call_target="tpu_custom_call" | custom-call | flops 3565158400 | bytes 13795328 | tf_op jit(solution)/shard_map/pallas_call | solution.py:144
  138.1 8.5 %shard_map.121 = (bf16[544,1024]{1,0:T(8,128)(2,1)}, bf16[544,1024]{1,0:T(8,128)(2,1)}, bf16[544,1024]{1,0:T(8,128)(2,1)}) custom-call(bf16[544,1024]{1,0:T(8,128)(2,1)S(1)} %collective-permute-done.24.rows, f32[544,640]{1,0:T(8,128)S(1)} %get-tuple-element.107.gate_in, f32[544,640]{1,0:T(8,128)S(1)} %get-tuple-element.108.up_in, ...), custom_call_target="tpu_custom_call" | custom-call | flops 3565158400 | bytes 13795328 | tf_op jit(solution)/shard_map/pallas_call | solution.py:144
  147.1 1.4 multiply_reduce_fusion
  148.6 1.2 copy-done.5
  151.1 2.0 add_convert_fusion.2
  154.1 1.4 collective-permute-start.27
  155.5 1.3 collective-permute-start.28
  156.8 6.0 %collective-permute-done.26 = bf16[136,1024]{1,0:T(8,128)(2,1)S(1)} collective-permute-done((bf16[136,1024]{1,0:T(8,128)(2,1)S(1)}, bf16[136,1024]{1,0:T(8,128)(2,1)S(1)}, u32[]{:S(2)}, u32[]{:S(2)}) %collective-permute-start.26) | collective-permute-done | bytes 278560 | tf_op jit(solution)/shard_map/ppermute | solution.py:416
  162.8 4.5 %collective-permute-done.27 = bf16[136,1024]{1,0:T(8,128)(2,1)S(1)} collective-permute-done((bf16[136,1024]{1,0:T(8,128)(2,1)S(1)}, bf16[136,1024]{1,0:T(8,128)(2,1)S(1)}, u32[]{:S(2)}, u32[]{:S(2)}) %collective-permute-start.27) | collective-permute-done | bytes 278560 | tf_op jit(solution)/shard_map/ppermute | solution.py:416
  169.8 2.4 %collective-permute-start.34 = (bf16[64,1024]{1,0:T(8,128)(2,1)S(1)}, bf16[64,1024]{1,0:T(8,128)(2,1)S(1)}, u32[]{:S(2)}, u32[]{:S(2)}) collective-permute-start(bf16[64,1024]{1,0:T(8,128)(2,1)S(1)} %get-tuple-element.180), channel_id=1, source_target_pairs={{0,3},{1,2},{2,1},{3,0},{4,7},{5,6},{6,5},{7,4},{8,11},{9,10},{10,... | collective-permute-start | bytes 393224 | tf_op jit(solution)/shard_map/ppermute | solution.py:421
  172.2 3.0 %collective-permute-start.35 = (bf16[64,1024]{1,0:T(8,128)(2,1)S(1)}, bf16[64,1024]{1,0:T(8,128)(2,1)S(1)}, u32[]{:S(2)}, u32[]{:S(2)}) collective-permute-start(bf16[64,1024]{1,0:T(8,128)(2,1)S(1)} %get-tuple-element.179), channel_id=1, source_target_pairs={{0,2},{1,3},{2,0},{3,1},{4,6},{5,7},{6,4},{7,5},{8,10},{9,11},{10,... | collective-permute-start | bytes 393224 | tf_op jit(solution)/shard_map/ppermute | solution.py:421
  175.2 1.7 add_convert_fusion.1
  177.0 1.4 collective-permute-start.31
  179.1 1.4 collective-permute-start.33
  180.5 1.7 add_convert_fusion
  183.0 1.8 collective-permute-done.35
  184.8 1.3 collective-permute-start.37
  186.1 1.4 collective-permute-done.36
  187.5 1.3 collective-permute-start.38
  188.7 1.5 collective-permute-start.39
  190.3 3.2 %collective-permute-done.33 = bf16[136,1024]{1,0:T(8,128)(2,1)S(1)} collective-permute-done((bf16[136,1024]{1,0:T(8,128)(2,1)S(1)}, bf16[136,1024]{1,0:T(8,128)(2,1)S(1)}, u32[]{:S(2)}, u32[]{:S(2)}) %collective-permute-start.33) | collective-permute-done | bytes 278560 | tf_op jit(solution)/shard_map/ppermute | solution.py:416
  194.9 1.4 collective-permute-start.40
  196.3 2.3 %collective-permute-done.37 = bf16[136,1024]{1,0:T(8,128)(2,1)S(1)} collective-permute-done((bf16[136,1024]{1,0:T(8,128)(2,1)S(1)}, bf16[136,1024]{1,0:T(8,128)(2,1)S(1)}, u32[]{:S(2)}, u32[]{:S(2)}) %collective-permute-start.37) | collective-permute-done | bytes 278560 | tf_op jit(solution)/shard_map/ppermute | solution.py:416
  199.3 3.9 %collective-permute-done.38 = bf16[136,1024]{1,0:T(8,128)(2,1)S(1)} collective-permute-done((bf16[136,1024]{1,0:T(8,128)(2,1)S(1)}, bf16[136,1024]{1,0:T(8,128)(2,1)S(1)}, u32[]{:S(2)}, u32[]{:S(2)}) %collective-permute-start.38) | collective-permute-done | bytes 278560 | tf_op jit(solution)/shard_map/ppermute | solution.py:416
  203.2 2.0 collective-permute-done.41
  206.6 3.2 %collective-permute-start.43 = (bf16[64,1024]{1,0:T(8,128)(2,1)S(1)}, bf16[64,1024]{1,0:T(8,128)(2,1)S(1)}, u32[]{:S(2)}, u32[]{:S(2)}) collective-permute-start(bf16[64,1024]{1,0:T(8,128)(2,1)S(1)} %get-tuple-element.174), channel_id=1, source_target_pairs={{0,3},{1,2},{2,1},{3,0},{4,7},{5,6},{6,5},{7,4},{8,11},{9,10},{10,... | collective-permute-start | bytes 393224 | tf_op jit(solution)/shard_map/ppermute | solution.py:421
  209.8 1.2 collective-permute-start.45
  211.0 2.5 %collective-permute-done.43 = bf16[64,1024]{1,0:T(8,128)(2,1)S(1)} collective-permute-done((bf16[64,1024]{1,0:T(8,128)(2,1)S(1)}, bf16[64,1024]{1,0:T(8,128)(2,1)S(1)}, u32[]{:S(2)}, u32[]{:S(2)}) %collective-permute-start.43) | collective-permute-done | bytes 131104 | tf_op jit(solution)/shard_map/ppermute | solution.py:421
  213.5 3.3 %collective-permute-done.44 = bf16[64,1024]{1,0:T(8,128)(2,1)S(1)} collective-permute-done((bf16[64,1024]{1,0:T(8,128)(2,1)S(1)}, bf16[64,1024]{1,0:T(8,128)(2,1)S(1)}, u32[]{:S(2)}, u32[]{:S(2)}) %collective-permute-start.44) | collective-permute-done | bytes 131104 | tf_op jit(solution)/shard_map/ppermute | solution.py:421
  216.8 1.4 add_convert_fusion.11
  (149 shorter events, 27.0 us)
Async XLA Ops:
  0.0 23.9 %copy-start = (bf16[256,1024]{1,0:T(8,128)(2,1)S(1)}, bf16[256,1024]{1,0:T(8,128)(2,1)}, u32[]{:S(2)}) copy-start(bf16[256,1024]{1,0:T(8,128)(2,1)} %param.13) | copy-start | bytes 1572868
  0.0 6.4 %copy-start.15 = (bf16[256,1024]{1,0:T(8,128)(2,1)S(1)}, bf16[256,1024]{1,0:T(8,128)(2,1)}, u32[]{:S(2)}) copy-start(bf16[256,1024]{1,0:T(8,128)(2,1)} %param.15) | copy-start | bytes 1572868
  3.8 4.5 %copy-start.14 = (f32[8]{0:T(128)S(1)}, f32[8]{0:T(128)}, u32[]{:S(2)}) copy-start(f32[8]{0:T(128)} %param.16) | copy-start | bytes 100
  7.1 3.9 %collective-permute-start = (bf16[8,128,128]{2,1,0:T(8,128)(2,1)S(1)}, bf16[8,128,128]{2,1,0:T(8,128)(2,1)S(1)}, u32[]{:S(2)}, u32[]{:S(2)}) collective-permute-start(bf16[8,128,128]{2,1,0:T(8,128)(2,1)S(1)} %convolution_convert_fusion.3), channel_id=1, source_target_pairs={{0,4},{4,0},{8,12},{12,8},{16,20},{20,16},{24,28},{28,24},{1,5},{5... | collective-permute-start | bytes 786440 | tf_op jit(solution)/shard_map/ppermute | solution.py:219
  11.1 6.8 %collective-permute-start.1 = (bf16[4,128,128]{2,1,0:T(8,128)(2,1)S(1)}, bf16[4,128,128]{2,1,0:T(8,128)(2,1)S(1)}, u32[]{:S(2)}, u32[]{:S(2)}) collective-permute-start(bf16[4,128,128]{2,1,0:T(8,128)(2,1)S(1)} %fusion.61), channel_id=1, source_target_pairs={{0,8},{4,12},{8,0},{12,4},{16,24},{20,28},{24,16},{28,20},{1,9},{5... | collective-permute-start | bytes 393224 | tf_op jit(solution)/shard_map/ppermute | solution.py:237
  13.7 8.4 %collective-permute-start.2 = (bf16[4,128,128]{2,1,0:T(8,128)(2,1)S(1)}, bf16[4,128,128]{2,1,0:T(8,128)(2,1)S(1)}, u32[]{:S(2)}, u32[]{:S(2)}) collective-permute-start(bf16[4,128,128]{2,1,0:T(8,128)(2,1)S(1)} %fusion.61), channel_id=1, source_target_pairs={{0,16},{4,20},{8,24},{12,28},{16,0},{20,4},{24,8},{28,12},{1,17},{... | collective-permute-start | bytes 393224 | tf_op jit(solution)/shard_map/ppermute | solution.py:237
  15.2 6.9 %collective-permute-start.3 = (bf16[4,128,128]{2,1,0:T(8,128)(2,1)S(1)}, bf16[4,128,128]{2,1,0:T(8,128)(2,1)S(1)}, u32[]{:S(2)}, u32[]{:S(2)}) collective-permute-start(bf16[4,128,128]{2,1,0:T(8,128)(2,1)S(1)} %fusion.61), channel_id=1, source_target_pairs={{0,24},{4,28},{8,16},{12,20},{16,8},{20,12},{24,0},{28,4},{1,25},{... | collective-permute-start | bytes 393224 | tf_op jit(solution)/shard_map/ppermute | solution.py:237
  22.3 1.4 collective-permute-start.4
  26.4 5.9 %copy-start.12 = (s32[256,2]{0,1:T(2,128)S(1)}, s32[256,2]{0,1:T(2,128)}, u32[]{:S(2)}) copy-start(s32[256,2]{0,1:T(2,128)} %param.23) | copy-start | bytes 6148
  28.8 15.0 %collective-permute-start.5 = (bf16[256,1024]{1,0:T(8,128)(2,1)S(1)}, bf16[256,1024]{1,0:T(8,128)(2,1)S(1)}, u32[]{:S(2)}, u32[]{:S(2)}) collective-permute-start(bf16[256,1024]{1,0:T(8,128)(2,1)S(1)} %fusion.16), channel_id=1, source_target_pairs={{0,1},{3,2},{4,5},{7,6},{8,9},{11,10},{12,13},{15,14},{16,17},{19,... | collective-permute-start | bytes 1572872 | tf_op jit(solution)/shard_map/ppermute | solution.py:331
  43.9 10.5 %collective-permute-start.7 = (bf16[256,1024]{1,0:T(8,128)(2,1)S(1)}, bf16[256,1024]{1,0:T(8,128)(2,1)S(1)}, u32[]{:S(2)}, u32[]{:S(2)}) collective-permute-start(bf16[256,1024]{1,0:T(8,128)(2,1)S(1)} %add_convert_fusion.8), channel_id=1, source_target_pairs={{1,2},{2,1},{5,6},{6,5},{9,10},{10,9},{13,14},{14,13},{17,18},{18,... | collective-permute-start | bytes 1572872 | tf_op jit(solution)/shard_map/ppermute | solution.py:336
  44.6 17.6 %collective-permute-start.6 = (bf16[256,1024]{1,0:T(8,128)(2,1)S(1)}, bf16[256,1024]{1,0:T(8,128)(2,1)S(1)}, u32[]{:S(2)}, u32[]{:S(2)}) collective-permute-start(bf16[256,1024]{1,0:T(8,128)(2,1)S(1)} %fusion.19), channel_id=1, source_target_pairs={{0,1},{3,2},{4,5},{7,6},{8,9},{11,10},{12,13},{15,14},{16,17},{19,... | collective-permute-start | bytes 1572872 | tf_op jit(solution)/shard_map/ppermute | solution.py:331
  54.4 8.7 %copy-start.6 = (bf16[256,3072]{1,0:T(8,128)(2,1)S(1)}, bf16[256,3072]{1,0:T(8,128)(2,1)}, u32[]{:S(2)}) copy-start(bf16[256,3072]{1,0:T(8,128)(2,1)} %param.12) | copy-start | bytes 4718596
  62.4 5.3 %collective-permute-start.9 = (bf16[256,1024]{1,0:T(8,128)(2,1)S(1)}, bf16[256,1024]{1,0:T(8,128)(2,1)S(1)}, u32[]{:S(2)}, u32[]{:S(2)}) collective-permute-start(bf16[256,1024]{1,0:T(8,128)(2,1)S(1)} %add_convert_fusion.6), channel_id=1, source_target_pairs={{1,2},{2,1},{5,6},{6,5},{9,10},{10,9},{13,14},{14,13},{17,18},{18,... | collective-permute-start | bytes 1572872 | tf_op jit(solution)/shard_map/ppermute | solution.py:336
  63.5 14.1 %collective-permute-start.8 = (bf16[256,1024]{1,0:T(8,128)(2,1)S(1)}, bf16[256,1024]{1,0:T(8,128)(2,1)S(1)}, u32[]{:S(2)}, u32[]{:S(2)}) collective-permute-start(bf16[256,1024]{1,0:T(8,128)(2,1)S(1)} %broadcast_select_fusion.3), channel_id=1, source_target_pairs={{0,1},{3,2},{1,0},{2,3},{4,5},{7,6},{5,4},{6,7},{8,9},{11,10},{9,8... | collective-permute-start | bytes 1572872 | tf_op jit(solution)/shard_map/ppermute | solution.py:331
  78.0 2.5 %copy-start.9 = (bf16[256,1024]{1,0:T(8,128)(2,1)}, bf16[256,1024]{1,0:T(8,128)(2,1)S(1)}, u32[]{:S(2)}) copy-start(bf16[256,1024]{1,0:T(8,128)(2,1)S(1)} %broadcast_select_fusion.2) | copy-start | bytes 1572868
  78.2 15.9 %collective-permute-start.11 = (bf16[256,1024]{1,0:T(8,128)(2,1)S(1)}, bf16[256,1024]{1,0:T(8,128)(2,1)S(1)}, u32[]{:S(2)}, u32[]{:S(2)}) collective-permute-start(bf16[256,1024]{1,0:T(8,128)(2,1)S(1)} %add_convert_fusion.4), channel_id=1, source_target_pairs={{1,2},{2,1},{5,6},{6,5},{9,10},{10,9},{13,14},{14,13},{17,18},{18,... | collective-permute-start | bytes 1572872 | tf_op jit(solution)/shard_map/ppermute | solution.py:336
  79.2 14.9 %collective-permute-start.10 = (bf16[256,1024]{1,0:T(8,128)(2,1)S(1)}, bf16[256,1024]{1,0:T(8,128)(2,1)S(1)}, u32[]{:S(2)}, u32[]{:S(2)}) collective-permute-start(bf16[256,1024]{1,0:T(8,128)(2,1)S(1)} %add_convert_fusion.5), channel_id=1, source_target_pairs={{1,0},{2,3},{5,4},{6,7},{9,8},{10,11},{13,12},{14,15},{17,16},{18,... | collective-permute-start | bytes 1572872 | tf_op jit(solution)/shard_map/ppermute | solution.py:331
  81.2 8.8 %collective-permute-start.12 = (bf16[136,1024]{1,0:T(8,128)(2,1)S(1)}, bf16[136,1024]{1,0:T(8,128)(2,1)S(1)}, u32[]{:S(2)}, u32[]{:S(2)}) collective-permute-start(bf16[136,1024]{1,0:T(8,128)(2,1)S(1)} %get-tuple-element.170), channel_id=1, source_target_pairs={{0,8},{4,12},{8,0},{12,4},{16,24},{20,28},{24,16},{28,20},{1,9},{5... | collective-permute-start | bytes 835592 | tf_op jit(solution)/shard_map/ppermute | solution.py:345
  82.5 11.6 %collective-permute-start.13 = (bf16[136,1024]{1,0:T(8,128)(2,1)S(1)}, bf16[136,1024]{1,0:T(8,128)(2,1)S(1)}, u32[]{:S(2)}, u32[]{:S(2)}) collective-permute-start(bf16[136,1024]{1,0:T(8,128)(2,1)S(1)} %get-tuple-element.169), channel_id=1, source_target_pairs={{0,16},{4,20},{8,24},{12,28},{16,0},{20,4},{24,8},{28,12},{1,17},{... | collective-permute-start | bytes 835592 | tf_op jit(solution)/shard_map/ppermute | solution.py:345
  83.3 10.7 %collective-permute-start.14 = (bf16[136,1024]{1,0:T(8,128)(2,1)S(1)}, bf16[136,1024]{1,0:T(8,128)(2,1)S(1)}, u32[]{:S(2)}, u32[]{:S(2)}) collective-permute-start(bf16[136,1024]{1,0:T(8,128)(2,1)S(1)} %get-tuple-element.168), channel_id=1, source_target_pairs={{0,24},{4,28},{8,16},{12,20},{16,8},{20,12},{24,0},{28,4},{1,25},{... | collective-permute-start | bytes 835592 | tf_op jit(solution)/shard_map/ppermute | solution.py:345
  94.2 18.3 %collective-permute-start.19 = (bf16[544,1024]{1,0:T(8,128)(2,1)S(1)}, bf16[544,1024]{1,0:T(8,128)(2,1)S(1)}, u32[]{:S(2)}, u32[]{:S(2)}) collective-permute-start(bf16[544,1024]{1,0:T(8,128)(2,1)S(1)} %constant_dynamic-update-slice_fusion.refs_0_), channel_id=1, source_target_pairs={{0,4},{4,0},{8,12},{12,8},{16,20},{20,16},{24,28},{28,24},{1,5},{5... | collective-permute-start | bytes 3342344 | tf_op jit(solution)/shard_map/ppermute | solution.py:348
  94.5 17.9 %collective-permute-start.15 = (bf16[256,1024]{1,0:T(8,128)(2,1)S(1)}, bf16[256,1024]{1,0:T(8,128)(2,1)S(1)}, u32[]{:S(2)}, u32[]{:S(2)}) collective-permute-start(bf16[256,1024]{1,0:T(8,128)(2,1)S(1)} %add_convert_fusion.3), channel_id=1, source_target_pairs={{1,0},{2,3},{5,4},{6,7},{9,8},{10,11},{13,12},{14,15},{17,16},{18,... | collective-permute-start | bytes 1572872 | tf_op jit(solution)/shard_map/ppermute | solution.py:331
  96.7 20.3 %copy-start.3 = (bf16[1,3072,640]{2,1,0:T(8,128)(2,1)S(1)}, bf16[1,3072,640]{2,1,0:T(8,128)(2,1)}, u32[]{:S(2)}) copy-start(bf16[1,3072,640]{2,1,0:T(8,128)(2,1)} %up_hbm.3) | copy-start | bytes 11796484
  96.8 9.5 %collective-permute-start.16 = (bf16[136,1024]{1,0:T(8,128)(2,1)S(1)}, bf16[136,1024]{1,0:T(8,128)(2,1)S(1)}, u32[]{:S(2)}, u32[]{:S(2)}) collective-permute-start(bf16[136,1024]{1,0:T(8,128)(2,1)S(1)} %get-tuple-element.166), channel_id=1, source_target_pairs={{0,8},{4,12},{8,0},{12,4},{16,24},{20,28},{24,16},{28,20},{1,9},{5... | collective-permute-start | bytes 835592 | tf_op jit(solution)/shard_map/ppermute | solution.py:345
  97.7 13.7 %collective-permute-start.17 = (bf16[136,1024]{1,0:T(8,128)(2,1)S(1)}, bf16[136,1024]{1,0:T(8,128)(2,1)S(1)}, u32[]{:S(2)}, u32[]{:S(2)}) collective-permute-start(bf16[136,1024]{1,0:T(8,128)(2,1)S(1)} %get-tuple-element.165), channel_id=1, source_target_pairs={{0,16},{4,20},{8,24},{12,28},{16,0},{20,4},{24,8},{28,12},{1,17},{... | collective-permute-start | bytes 835592 | tf_op jit(solution)/shard_map/ppermute | solution.py:345
  99.1 13.4 %collective-permute-start.18 = (bf16[136,1024]{1,0:T(8,128)(2,1)S(1)}, bf16[136,1024]{1,0:T(8,128)(2,1)S(1)}, u32[]{:S(2)}, u32[]{:S(2)}) collective-permute-start(bf16[136,1024]{1,0:T(8,128)(2,1)S(1)} %get-tuple-element.164), channel_id=1, source_target_pairs={{0,24},{4,28},{8,16},{12,20},{16,8},{20,12},{24,0},{28,4},{1,25},{... | collective-permute-start | bytes 835592 | tf_op jit(solution)/shard_map/ppermute | solution.py:345
  112.6 8.7 %collective-permute-start.23 = (bf16[544,1024]{1,0:T(8,128)(2,1)S(1)}, bf16[544,1024]{1,0:T(8,128)(2,1)S(1)}, u32[]{:S(2)}, u32[]{:S(2)}) collective-permute-start(bf16[544,1024]{1,0:T(8,128)(2,1)S(1)} %constant_dynamic-update-slice_fusion.4.refs_1_), channel_id=1, source_target_pairs={{0,4},{4,0},{8,12},{12,8},{16,20},{20,16},{24,28},{28,24},{1,5},{5... | collective-permute-start | bytes 3342344 | tf_op jit(solution)/shard_map/ppermute | solution.py:348
  112.7 0.8 copy-start.7
  112.8 4.3 %copy-start.2 = (bf16[1,3072,640]{2,1,0:T(8,128)(2,1)S(1)}, bf16[1,3072,640]{2,1,0:T(8,128)(2,1)}, u32[]{:S(2)}) copy-start(bf16[1,3072,640]{2,1,0:T(8,128)(2,1)} %gate_hbm.3) | copy-start | bytes 11796484
  113.5 11.9 %collective-permute-start.20 = (bf16[136,1024]{1,0:T(8,128)(2,1)S(1)}, bf16[136,1024]{1,0:T(8,128)(2,1)S(1)}, u32[]{:S(2)}, u32[]{:S(2)}) collective-permute-start(bf16[136,1024]{1,0:T(8,128)(2,1)S(1)} %get-tuple-element.162), channel_id=1, source_target_pairs={{0,8},{4,12},{8,0},{12,4},{16,24},{20,28},{24,16},{28,20},{1,9},{5... | collective-permute-start | bytes 835592 | tf_op jit(solution)/shard_map/ppermute | solution.py:345
  114.7 14.7 %collective-permute-start.21 = (bf16[136,1024]{1,0:T(8,128)(2,1)S(1)}, bf16[136,1024]{1,0:T(8,128)(2,1)S(1)}, u32[]{:S(2)}, u32[]{:S(2)}) collective-permute-start(bf16[136,1024]{1,0:T(8,128)(2,1)S(1)} %get-tuple-element.161), channel_id=1, source_target_pairs={{0,16},{4,20},{8,24},{12,28},{16,0},{20,4},{24,8},{28,12},{1,17},{... | collective-permute-start | bytes 835592 | tf_op jit(solution)/shard_map/ppermute | solution.py:345
  115.9 13.6 %collective-permute-start.22 = (bf16[136,1024]{1,0:T(8,128)(2,1)S(1)}, bf16[136,1024]{1,0:T(8,128)(2,1)S(1)}, u32[]{:S(2)}, u32[]{:S(2)}) collective-permute-start(bf16[136,1024]{1,0:T(8,128)(2,1)S(1)} %get-tuple-element.160), channel_id=1, source_target_pairs={{0,24},{4,28},{8,16},{12,20},{16,8},{20,12},{24,0},{28,4},{1,25},{... | collective-permute-start | bytes 835592 | tf_op jit(solution)/shard_map/ppermute | solution.py:345
  129.6 8.5 %collective-permute-start.24 = (bf16[544,1024]{1,0:T(8,128)(2,1)S(1)}, bf16[544,1024]{1,0:T(8,128)(2,1)S(1)}, u32[]{:S(2)}, u32[]{:S(2)}) collective-permute-start(bf16[544,1024]{1,0:T(8,128)(2,1)S(1)} %constant_dynamic-update-slice_fusion.8.rows), channel_id=1, source_target_pairs={{0,4},{4,0},{8,12},{12,8},{16,20},{20,16},{24,28},{28,24},{1,5},{5... | collective-permute-start | bytes 3342344 | tf_op jit(solution)/shard_map/ppermute | solution.py:348
  137.0 1.1 copy-start.4
  138.1 9.0 %copy-start.8 = (bf16[256,1024]{1,0:T(8,128)(2,1)S(1)}, bf16[256,1024]{1,0:T(8,128)(2,1)}, u32[]{:S(2)}) copy-start(bf16[256,1024]{1,0:T(8,128)(2,1)} %copy-done.7) | copy-start | bytes 1572868
  146.6 4.6 %collective-permute-start.25 = (bf16[544,1024]{1,0:T(8,128)(2,1)}, bf16[544,1024]{1,0:T(8,128)(2,1)}, u32[]{:S(2)}, u32[]{:S(2)}) collective-permute-start(bf16[544,1024]{1,0:T(8,128)(2,1)} %get-tuple-element.110), channel_id=1, source_target_pairs={{0,4},{4,0},{8,12},{12,8},{16,20},{20,16},{24,28},{28,24},{1,5},{5... | collective-permute-start | bytes 3342344 | tf_op jit(solution)/shard_map/ppermute | solution.py:424
  147.1 2.6 %copy-start.13 = (bf16[3072,4]{0,1:T(4,128)(2,1)S(1)}, bf16[3072,4]{0,1:T(4,128)(2,1)}, u32[]{:S(2)}) copy-start(bf16[3072,4]{0,1:T(4,128)(2,1)} %param.19) | copy-start | bytes 73732
  148.6 1.2 copy-start.5
  150.2 6.6 %collective-permute-start.29 = (bf16[544,1024]{1,0:T(8,128)(2,1)}, bf16[544,1024]{1,0:T(8,128)(2,1)}, u32[]{:S(2)}, u32[]{:S(2)}) collective-permute-start(bf16[544,1024]{1,0:T(8,128)(2,1)} %get-tuple-element.111), channel_id=1, source_target_pairs={{0,4},{4,0},{8,12},{12,8},{16,20},{20,16},{24,28},{28,24},{1,5},{5... | collective-permute-start | bytes 3342344 | tf_op jit(solution)/shard_map/ppermute | solution.py:424
  150.3 6.5 %collective-permute-start.30 = (bf16[544,1024]{1,0:T(8,128)(2,1)}, bf16[544,1024]{1,0:T(8,128)(2,1)}, u32[]{:S(2)}, u32[]{:S(2)}) collective-permute-start(bf16[544,1024]{1,0:T(8,128)(2,1)} %get-tuple-element.112), channel_id=1, source_target_pairs={{0,4},{4,0},{8,12},{12,8},{16,20},{20,16},{24,28},{28,24},{1,5},{5... | collective-permute-start | bytes 3342344 | tf_op jit(solution)/shard_map/ppermute | solution.py:424
  153.2 9.6 %collective-permute-start.26 = (bf16[136,1024]{1,0:T(8,128)(2,1)S(1)}, bf16[136,1024]{1,0:T(8,128)(2,1)S(1)}, u32[]{:S(2)}, u32[]{:S(2)}) collective-permute-start(bf16[136,1024]{1,0:T(8,128)(2,1)S(1)} %get-tuple-element.159), channel_id=1, source_target_pairs={{0,8},{4,12},{8,0},{12,4},{16,24},{20,28},{24,16},{28,20},{1,9},{5... | collective-permute-start | bytes 835592 | tf_op jit(solution)/shard_map/ppermute | solution.py:416
  154.1 13.2 %collective-permute-start.27 = (bf16[136,1024]{1,0:T(8,128)(2,1)S(1)}, bf16[136,1024]{1,0:T(8,128)(2,1)S(1)}, u32[]{:S(2)}, u32[]{:S(2)}) collective-permute-start(bf16[136,1024]{1,0:T(8,128)(2,1)S(1)} %get-tuple-element.158), channel_id=1, source_target_pairs={{0,16},{4,20},{8,24},{12,28},{16,0},{20,4},{24,8},{28,12},{1,17},{... | collective-permute-start | bytes 835592 | tf_op jit(solution)/shard_map/ppermute | solution.py:416
  155.5 13.0 %collective-permute-start.28 = (bf16[136,1024]{1,0:T(8,128)(2,1)S(1)}, bf16[136,1024]{1,0:T(8,128)(2,1)S(1)}, u32[]{:S(2)}, u32[]{:S(2)}) collective-permute-start(bf16[136,1024]{1,0:T(8,128)(2,1)S(1)} %get-tuple-element.157), channel_id=1, source_target_pairs={{0,24},{4,28},{8,16},{12,20},{16,8},{20,12},{24,0},{28,4},{1,25},{... | collective-permute-start | bytes 835592 | tf_op jit(solution)/shard_map/ppermute | solution.py:416
  169.8 12.4 %collective-permute-start.34 = (bf16[64,1024]{1,0:T(8,128)(2,1)S(1)}, bf16[64,1024]{1,0:T(8,128)(2,1)S(1)}, u32[]{:S(2)}, u32[]{:S(2)}) collective-permute-start(bf16[64,1024]{1,0:T(8,128)(2,1)S(1)} %get-tuple-element.180), channel_id=1, source_target_pairs={{0,3},{1,2},{2,1},{3,0},{4,7},{5,6},{6,5},{7,4},{8,11},{9,10},{10,... | collective-permute-start | bytes 393224 | tf_op jit(solution)/shard_map/ppermute | solution.py:421
  172.2 12.6 %collective-permute-start.35 = (bf16[64,1024]{1,0:T(8,128)(2,1)S(1)}, bf16[64,1024]{1,0:T(8,128)(2,1)S(1)}, u32[]{:S(2)}, u32[]{:S(2)}) collective-permute-start(bf16[64,1024]{1,0:T(8,128)(2,1)S(1)} %get-tuple-element.179), channel_id=1, source_target_pairs={{0,2},{1,3},{2,0},{3,1},{4,6},{5,7},{6,4},{7,5},{8,10},{9,11},{10,... | collective-permute-start | bytes 393224 | tf_op jit(solution)/shard_map/ppermute | solution.py:421
  177.0 11.8 %collective-permute-start.31 = (bf16[136,1024]{1,0:T(8,128)(2,1)S(1)}, bf16[136,1024]{1,0:T(8,128)(2,1)S(1)}, u32[]{:S(2)}, u32[]{:S(2)}) collective-permute-start(bf16[136,1024]{1,0:T(8,128)(2,1)S(1)} %get-tuple-element.155), channel_id=1, source_target_pairs={{0,8},{4,12},{8,0},{12,4},{16,24},{20,28},{24,16},{28,20},{1,9},{5... | collective-permute-start | bytes 835592 | tf_op jit(solution)/shard_map/ppermute | solution.py:416
  178.3 12.0 %collective-permute-start.32 = (bf16[136,1024]{1,0:T(8,128)(2,1)S(1)}, bf16[136,1024]{1,0:T(8,128)(2,1)S(1)}, u32[]{:S(2)}, u32[]{:S(2)}) collective-permute-start(bf16[136,1024]{1,0:T(8,128)(2,1)S(1)} %get-tuple-element.154), channel_id=1, source_target_pairs={{0,16},{4,20},{8,24},{12,28},{16,0},{20,4},{24,8},{28,12},{1,17},{... | collective-permute-start | bytes 835592 | tf_op jit(solution)/shard_map/ppermute | solution.py:416
  179.1 14.5 %collective-permute-start.33 = (bf16[136,1024]{1,0:T(8,128)(2,1)S(1)}, bf16[136,1024]{1,0:T(8,128)(2,1)S(1)}, u32[]{:S(2)}, u32[]{:S(2)}) collective-permute-start(bf16[136,1024]{1,0:T(8,128)(2,1)S(1)} %get-tuple-element.153), channel_id=1, source_target_pairs={{0,24},{4,28},{8,16},{12,20},{16,8},{20,12},{24,0},{28,4},{1,25},{... | collective-permute-start | bytes 835592 | tf_op jit(solution)/shard_map/ppermute | solution.py:416
  182.2 5.3 %collective-permute-start.36 = (bf16[64,1024]{1,0:T(8,128)(2,1)S(1)}, bf16[64,1024]{1,0:T(8,128)(2,1)S(1)}, u32[]{:S(2)}, u32[]{:S(2)}) collective-permute-start(bf16[64,1024]{1,0:T(8,128)(2,1)S(1)} %get-tuple-element.178), channel_id=1, source_target_pairs={{0,1},{1,0},{2,3},{3,2},{4,5},{5,4},{6,7},{7,6},{8,9},{9,8},{10,11... | collective-permute-start | bytes 393224 | tf_op jit(solution)/shard_map/ppermute | solution.py:421
  184.8 13.8 %collective-permute-start.37 = (bf16[136,1024]{1,0:T(8,128)(2,1)S(1)}, bf16[136,1024]{1,0:T(8,128)(2,1)S(1)}, u32[]{:S(2)}, u32[]{:S(2)}) collective-permute-start(bf16[136,1024]{1,0:T(8,128)(2,1)S(1)} %get-tuple-element.151), channel_id=1, source_target_pairs={{0,8},{4,12},{8,0},{12,4},{16,24},{20,28},{24,16},{28,20},{1,9},{5... | collective-permute-start | bytes 835592 | tf_op jit(solution)/shard_map/ppermute | solution.py:416
  187.5 6.7 %copy-start.10 = (bf16[64,1024]{1,0:T(8,128)(2,1)}, bf16[64,1024]{1,0:T(8,128)(2,1)S(1)}, u32[]{:S(2)}) copy-start(bf16[64,1024]{1,0:T(8,128)(2,1)S(1)} %collective-permute-done.36) | copy-start | bytes 393220
  187.5 15.7 %collective-permute-start.38 = (bf16[136,1024]{1,0:T(8,128)(2,1)S(1)}, bf16[136,1024]{1,0:T(8,128)(2,1)S(1)}, u32[]{:S(2)}, u32[]{:S(2)}) collective-permute-start(bf16[136,1024]{1,0:T(8,128)(2,1)S(1)} %get-tuple-element.150), channel_id=1, source_target_pairs={{0,16},{4,20},{8,24},{12,28},{16,0},{20,4},{24,8},{28,12},{1,17},{... | collective-permute-start | bytes 835592 | tf_op jit(solution)/shard_map/ppermute | solution.py:416
  188.7 14.4 %collective-permute-start.39 = (bf16[136,1024]{1,0:T(8,128)(2,1)S(1)}, bf16[136,1024]{1,0:T(8,128)(2,1)S(1)}, u32[]{:S(2)}, u32[]{:S(2)}) collective-permute-start(bf16[136,1024]{1,0:T(8,128)(2,1)S(1)} %get-tuple-element.149), channel_id=1, source_target_pairs={{0,24},{4,28},{8,16},{12,20},{16,8},{20,12},{24,0},{28,4},{1,25},{... | collective-permute-start | bytes 835592 | tf_op jit(solution)/shard_map/ppermute | solution.py:416
  194.9 8.3 %collective-permute-start.40 = (bf16[64,1024]{1,0:T(8,128)(2,1)S(1)}, bf16[64,1024]{1,0:T(8,128)(2,1)S(1)}, u32[]{:S(2)}, u32[]{:S(2)}) collective-permute-start(bf16[64,1024]{1,0:T(8,128)(2,1)S(1)} %get-tuple-element.177), channel_id=1, source_target_pairs={{0,3},{1,2},{2,1},{3,0},{4,7},{5,6},{6,5},{7,4},{8,11},{9,10},{10,... | collective-permute-start | bytes 393224 | tf_op jit(solution)/shard_map/ppermute | solution.py:421
  196.3 8.9 %collective-permute-start.41 = (bf16[64,1024]{1,0:T(8,128)(2,1)S(1)}, bf16[64,1024]{1,0:T(8,128)(2,1)S(1)}, u32[]{:S(2)}, u32[]{:S(2)}) collective-permute-start(bf16[64,1024]{1,0:T(8,128)(2,1)S(1)} %get-tuple-element.176), channel_id=1, source_target_pairs={{0,2},{1,3},{2,0},{3,1},{4,6},{5,7},{6,4},{7,5},{8,10},{9,11},{10,... | collective-permute-start | bytes 393224 | tf_op jit(solution)/shard_map/ppermute | solution.py:421
  198.6 6.7 %collective-permute-start.42 = (bf16[64,1024]{1,0:T(8,128)(2,1)S(1)}, bf16[64,1024]{1,0:T(8,128)(2,1)S(1)}, u32[]{:S(2)}, u32[]{:S(2)}) collective-permute-start(bf16[64,1024]{1,0:T(8,128)(2,1)S(1)} %get-tuple-element.175), channel_id=1, source_target_pairs={{0,1},{1,0},{2,3},{3,2},{4,5},{5,4},{6,7},{7,6},{8,9},{9,8},{10,11... | collective-permute-start | bytes 393224 | tf_op jit(solution)/shard_map/ppermute | solution.py:421
  205.8 11.0 %copy-start.11 = (bf16[64,1024]{1,0:T(8,128)(2,1)S(1)}, bf16[64,1024]{1,0:T(8,128)(2,1)}, u32[]{:S(2)}) copy-start(bf16[64,1024]{1,0:T(8,128)(2,1)} %copy-done.10) | copy-start | bytes 393220
  206.6 7.0 %collective-permute-start.43 = (bf16[64,1024]{1,0:T(8,128)(2,1)S(1)}, bf16[64,1024]{1,0:T(8,128)(2,1)S(1)}, u32[]{:S(2)}, u32[]{:S(2)}) collective-permute-start(bf16[64,1024]{1,0:T(8,128)(2,1)S(1)} %get-tuple-element.174), channel_id=1, source_target_pairs={{0,3},{1,2},{2,1},{3,0},{4,7},{5,6},{6,5},{7,4},{8,11},{9,10},{10,... | collective-permute-start | bytes 393224 | tf_op jit(solution)/shard_map/ppermute | solution.py:421
  209.8 7.0 %collective-permute-start.44 = (bf16[64,1024]{1,0:T(8,128)(2,1)S(1)}, bf16[64,1024]{1,0:T(8,128)(2,1)S(1)}, u32[]{:S(2)}, u32[]{:S(2)}) collective-permute-start(bf16[64,1024]{1,0:T(8,128)(2,1)S(1)} %get-tuple-element.173), channel_id=1, source_target_pairs={{0,2},{1,3},{2,0},{3,1},{4,6},{5,7},{6,4},{7,5},{8,10},{9,11},{10,... | collective-permute-start | bytes 393224 | tf_op jit(solution)/shard_map/ppermute | solution.py:421
  209.8 7.0 %collective-permute-start.45 = (bf16[64,1024]{1,0:T(8,128)(2,1)S(1)}, bf16[64,1024]{1,0:T(8,128)(2,1)}, u32[]{:S(2)}, u32[]{:S(2)}) collective-permute-start(bf16[64,1024]{1,0:T(8,128)(2,1)S(1)} %get-tuple-element.172), channel_id=1, source_target_pairs={{0,1},{1,0},{2,3},{3,2},{4,5},{5,4},{6,7},{7,6},{8,9},{9,8},{10,11... | collective-permute-start | bytes 393224 | tf_op jit(solution)/shard_map/ppermute | solution.py:421
  211.0 8.0 %copy-start.1 = (bf16[256,1024]{1,0:T(8,128)(2,1)S(1)}, bf16[256,1024]{1,0:T(8,128)(2,1)}, u32[]{:S(2)}) copy-start(bf16[256,1024]{1,0:T(8,128)(2,1)} %param.13) | copy-start | bytes 1572868

commit v4 on v3

--- a/solution.py
+++ b/solution.py
@@ -108,7 +108,7 @@
 
 VMEM = pl.BlockSpec(memory_space=pltpu.VMEM)
 ANY = pl.BlockSpec(memory_space=pl.ANY)
-VMEM_LIMIT = 40 * 1024 * 1024
+VMEM_LIMIT = 26 * 1024 * 1024
 
 
 def gate_up_first(rows, gate_weight, up_weight):
@@ -162,6 +162,31 @@
     )(rows, *first, gate_weight, up_weight, down_weight)
 
 
+def state_kernel(place_ref, lengths_ref, rates_ref, keys, values, out):
+    block_len = keys.shape[0]
+    heads, size, _ = out.shape
+    base = place_ref[0]
+    start = jnp.int32(0)
+    last_start = start
+    for i in range(lengths_ref.shape[0]):
+        last_start = jnp.where(start < base + block_len, start, last_start)
+        start = start + lengths_ref[i]
+    index = lax.broadcasted_iota(jnp.int32, (block_len, size), 0)
+    left = (block_len - index).astype(F32)
+    same = base + index >= last_start
+    dims = (((0,), (0,)), ((), ()))
+    for h in range(heads):
+        cols = slice(h * size, (h + 1) * size)
+        weight = jnp.where(same, jnp.exp(-rates_ref[h] * left), 0.0)
+        weighted = keys[:, cols].astype(F32) * weight
+        high = weighted.astype(BF)
+        low = (weighted - high.astype(F32)).astype(BF)
+        v = values[:, cols]
+        state = lax.dot_general(high, v, dims, preferred_element_type=F32)
+        state = state + lax.dot_general(low, v, dims, preferred_element_type=F32)
+        out[h] = state.astype(BF)
+
+
 def together(values):
     names = list(values)
     joined = lax.optimization_barrier(tuple(values[name] for name in names))
@@ -182,7 +207,6 @@
     down_weight,
     routes,
 ):
-    highest = lax.Precision.HIGHEST
     seq_count = lax.axis_size("seq")
     exp_count = lax.axis_size("exp")
     seq_index = lax.axis_index("seq")
@@ -206,13 +230,13 @@
     key_heads = keys.reshape(block_len, head_count, head_size)
     value_heads = values.reshape(block_len, head_count, head_size)
 
-    distance_end = (block_len - local_index).astype(F32)
-    same_last = (doc_of == doc_of[-1]).astype(F32)
-    end_weight = jnp.exp(-rates[None, :] * distance_end[:, None]) * same_last[:, None]
-    weighted_keys = end_weight[:, :, None] * key_heads.astype(F32)
-    end_state = jnp.einsum(
-        "tha,thb->hab", weighted_keys, value_heads.astype(F32), precision=highest
-    ).astype(BF)
+    smem = pl.BlockSpec(memory_space=pltpu.SMEM)
+    end_state = pl.pallas_call(
+        state_kernel,
+        out_shape=jax.ShapeDtypeStruct((head_count, head_size, head_size), BF),
+        in_specs=[smem] * 3 + [VMEM] * 2,
+        out_specs=VMEM,
+    )(block_base.reshape(1), doc_lengths, rates, keys, values)
 
     half_heads = head_count // 2
     head_at = core * half_heads

time: 220 us -> 215 us (0.977)
  waiting for transfers between devices: 91.5 us -> 86.3 us
  starting transfers between devices: 60.5 us -> 63.7 us
    ppermute x9, waiting for transfers between devices: 21 us -> 16.8 us  [body(): done['table', g] = lax.ppermute(block, 'seq', xor_pairs(seq_count, 2 * g))]
    ppermute x9, starting transfers between devices: 12.8 us -> 15.4 us  [body(): done['own', step] = lax.ppermute(block, 'exp', xor_pairs(exp_count, step))]
    pallas_call x0 -> x1, Pallas kernels: none -> 2.68 us  [body(): pl.pallas_call(state_kernel, out_shape=jax.ShapeDtypeStruct((head_count,...]
    convert_element_type x3 -> x2, other arithmetic: 5.34 us -> 4.28 us  [body(): sums[i] = (kept[i].astype(F32) + done['got', i].astype(F32)).astype(BF)]
  transfers between devices with their start and end apart: 46 -> 46, of which waited for: 23 -> 22; matrix products, arithmetic and copies ran while one was open for 8% -> 9% of each run, Pallas kernels for 7% -> 7%
where the time goes in v4:
time: 215 us
  waiting for transfers between devices  86.3 us (40%)
  starting transfers between devices  63.7 us (30%)
  Pallas kernels  25 us (12%)
  matrix products  15.6 us (7%)
  other arithmetic  14.6 us (7%)
  local copies, waits for them, and re-layouts  4.69 us (2%)
  between operations  4.65 us (2%)
    ppermute x5, waiting for transfers between devices, body(): lax.ppermute(load, 'exp', (ins if has_in else []) + (outs if has_out else...  27.2 us
    ppermute x9, waiting for transfers between devices, body(): done['group', g] = lax.ppermute(block, 'seq', xor_pairs(seq_count, 2 * g))  25.6 us
    ppermute x5, starting transfers between devices, body(): lax.ppermute(load, 'exp', (ins if has_in else []) + (outs if has_out else...  17.7 us
    ppermute x9, waiting for transfers between devices, body(): done['table', g] = lax.ppermute(block, 'seq', xor_pairs(seq_count, 2 * g))  16.8 us
    ppermute x9, starting transfers between devices, body(): done['own', step] = lax.ppermute(block, 'exp', xor_pairs(exp_count, step))  15.4 us
    pallas_call x2, Pallas kernels, expert_last(): pl.pallas_call(functools.partial(expert_kernel, width), out_shape=tuple((...  13.9 us
    ppermute x9, starting transfers between devices, body(): done['table', g] = lax.ppermute(block, 'seq', xor_pairs(seq_count, 2 * g))  11.9 us
    ppermute x9, waiting for transfers between devices, body(): done['own', step] = lax.ppermute(block, 'exp', xor_pairs(exp_count, step))  10.9 us
  transfers between devices with their start and end apart: 46, of which 22 were waited for; matrix products, arithmetic and copies ran while one was open for 9% of the time, Pallas kernels for 7%

profile of v4, /device:TPU:0, one launch (start us, length us, event | category | flops | bytes accessed | tf_op | source)
XLA Modules:
  0.0 214.6 jit_solution(15921795280034463744)
XLA Ops:
  0.0 2.7 %shard_map.118 = bf16[8,128,128]{2,1,0:T(8,128)(2,1)} custom-call(s32[1]{0:T(128)} %bitcast.3.place_ref, s32[16]{0:T(128)} %lengths_ref.1, f32[8]{0:T(128)} %rates_ref.1, bf16[256,1024]{1,0:T(8,128)(2,1)} %keys.1, bf16[256,1024]{1,0:T(8,128)(2,1)} %values.1), custom_call_target="tpu_custom_call" | custom-call | tf_op jit(solution)/shard_map/pallas_call | solution.py:234
  8.2 1.0 fusion.58
  9.3 2.6 %collective-permute-start.1 = (bf16[4,128,128]{2,1,0:T(8,128)(2,1)S(1)}, bf16[4,128,128]{2,1,0:T(8,128)(2,1)S(1)}, u32[]{:S(2)}, u32[]{:S(2)}) collective-permute-start(bf16[4,128,128]{2,1,0:T(8,128)(2,1)S(1)} %fusion.58), channel_id=1, source_target_pairs={{0,8},{4,12},{8,0},{12,4},{16,24},{20,28},{24,16},{28,20},{1,9},{5... | collective-permute-start | bytes 393224 | tf_op jit(solution)/shard_map/ppermute | solution.py:261
  11.8 1.5 collective-permute-start.2
  14.6 1.4 collective-permute-done.1
  16.1 4.2 %collective-permute-done.2 = bf16[4,128,128]{2,1,0:T(8,128)(2,1)S(1)} collective-permute-done((bf16[4,128,128]{2,1,0:T(8,128)(2,1)S(1)}, bf16[4,128,128]{2,1,0:T(8,128)(2,1)S(1)}, u32[]{:S(2)}, u32[]{:S(2)}) %collective-permute-start.2) | collective-permute-done | bytes 131104 | tf_op jit(solution)/shard_map/ppermute | solution.py:261
  20.3 1.1 broadcast_select_fusion.6
  21.5 1.0 copy.34
  24.0 1.9 multiply_reduce_fusion.1
  26.1 2.3 %fusion.16 = bf16[256,1024]{1,0:T(8,128)(2,1)S(1)} fusion(bf16[256,1024]{0,1:T(8,128)(2,1)S(1)} %bitcast.53, bf16[1024,3072]{1,0:T(8,128)(2,1)} %param.18), kind=kOutput, calls=%fused_computation.32 | convolution fusion | flops 537133056 | bytes 3145728 | tf_op jit(solution)/shard_map/dot_general | solution.py:337
  28.4 3.5 %collective-permute-start.5 = (bf16[256,1024]{1,0:T(8,128)(2,1)S(1)}, bf16[256,1024]{1,0:T(8,128)(2,1)S(1)}, u32[]{:S(2)}, u32[]{:S(2)}) collective-permute-start(bf16[256,1024]{1,0:T(8,128)(2,1)S(1)} %fusion.16), channel_id=1, source_target_pairs={{0,1},{3,2},{4,5},{7,6},{8,9},{11,10},{12,13},{15,14},{16,17},{19,... | collective-permute-start | bytes 1572872 | tf_op jit(solution)/shard_map/ppermute | solution.py:355
  32.0 2.3 %fusion.19 = bf16[256,1024]{1,0:T(8,128)(2,1)S(1)} fusion(bf16[256,1024]{0,1:T(8,128)(2,1)S(1)} %bitcast.54, bf16[1024,3072]{1,0:T(8,128)(2,1)} %param.18), kind=kOutput, calls=%fused_computation.33 | convolution fusion | flops 537133056 | bytes 3145728 | tf_op jit(solution)/shard_map/dot_general | solution.py:337
  34.3 9.2 %collective-permute-done.5 = bf16[256,1024]{1,0:T(8,128)(2,1)S(1)} collective-permute-done((bf16[256,1024]{1,0:T(8,128)(2,1)S(1)}, bf16[256,1024]{1,0:T(8,128)(2,1)S(1)}, u32[]{:S(2)}, u32[]{:S(2)}) %collective-permute-start.5) | collective-permute-done | bytes 524320 | tf_op jit(solution)/shard_map/ppermute | solution.py:355
  44.4 7.2 %collective-permute-start.6 = (bf16[256,1024]{1,0:T(8,128)(2,1)S(1)}, bf16[256,1024]{1,0:T(8,128)(2,1)S(1)}, u32[]{:S(2)}, u32[]{:S(2)}) collective-permute-start(bf16[256,1024]{1,0:T(8,128)(2,1)S(1)} %fusion.19), channel_id=1, source_target_pairs={{0,1},{3,2},{4,5},{7,6},{8,9},{11,10},{12,13},{15,14},{16,17},{19,... | collective-permute-start | bytes 1572872 | tf_op jit(solution)/shard_map/ppermute | solution.py:355
  51.8 2.3 %fusion.22 = bf16[256,1024]{1,0:T(8,128)(2,1)S(1)} fusion(bf16[256,1024]{0,1:T(8,128)(2,1)S(1)} %bitcast.55, bf16[1024,3072]{1,0:T(8,128)(2,1)} %param.18), kind=kOutput, calls=%fused_computation.34 | convolution fusion | flops 537133056 | bytes 3145728 | tf_op jit(solution)/shard_map/dot_general | solution.py:337
  54.2 8.0 %collective-permute-done.6 = bf16[256,1024]{1,0:T(8,128)(2,1)S(1)} collective-permute-done((bf16[256,1024]{1,0:T(8,128)(2,1)S(1)}, bf16[256,1024]{1,0:T(8,128)(2,1)S(1)}, u32[]{:S(2)}, u32[]{:S(2)}) %collective-permute-start.6) | collective-permute-done | bytes 524320 | tf_op jit(solution)/shard_map/ppermute | solution.py:355
  63.4 4.2 %collective-permute-start.8 = (bf16[256,1024]{1,0:T(8,128)(2,1)S(1)}, bf16[256,1024]{1,0:T(8,128)(2,1)S(1)}, u32[]{:S(2)}, u32[]{:S(2)}) collective-permute-start(bf16[256,1024]{1,0:T(8,128)(2,1)S(1)} %broadcast_select_fusion.3), channel_id=1, source_target_pairs={{0,1},{3,2},{1,0},{2,3},{4,5},{7,6},{5,4},{6,7},{8,9},{11,10},{9,8... | collective-permute-start | bytes 1572872 | tf_op jit(solution)/shard_map/ppermute | solution.py:355
  67.7 10.0 %collective-permute-done.8 = bf16[256,1024]{1,0:T(8,128)(2,1)S(1)} collective-permute-done((bf16[256,1024]{1,0:T(8,128)(2,1)S(1)}, bf16[256,1024]{1,0:T(8,128)(2,1)S(1)}, u32[]{:S(2)}, u32[]{:S(2)}) %collective-permute-start.8) | collective-permute-done | bytes 524320 | tf_op jit(solution)/shard_map/ppermute | solution.py:355
  79.3 1.3 collective-permute-start.10
  81.3 1.3 collective-permute-start.12
  83.5 1.4 collective-permute-start.14
  84.9 5.4 %collective-permute-done.12 = bf16[136,1024]{1,0:T(8,128)(2,1)S(1)} collective-permute-done((bf16[136,1024]{1,0:T(8,128)(2,1)S(1)}, bf16[136,1024]{1,0:T(8,128)(2,1)S(1)}, u32[]{:S(2)}, u32[]{:S(2)}) %collective-permute-start.12) | collective-permute-done | bytes 278560 | tf_op jit(solution)/shard_map/ppermute | solution.py:369
  90.3 4.1 %collective-permute-done.13 = bf16[136,1024]{1,0:T(8,128)(2,1)S(1)} collective-permute-done((bf16[136,1024]{1,0:T(8,128)(2,1)S(1)}, bf16[136,1024]{1,0:T(8,128)(2,1)S(1)}, u32[]{:S(2)}, u32[]{:S(2)}) %collective-permute-start.13) | collective-permute-done | bytes 278560 | tf_op jit(solution)/shard_map/ppermute | solution.py:369
  94.8 1.5 collective-permute-start.15
  98.1 1.3 collective-permute-start.17
  99.4 1.3 collective-permute-start.18
  100.7 6.0 %collective-permute-done.16 = bf16[136,1024]{1,0:T(8,128)(2,1)S(1)} collective-permute-done((bf16[136,1024]{1,0:T(8,128)(2,1)S(1)}, bf16[136,1024]{1,0:T(8,128)(2,1)S(1)}, u32[]{:S(2)}, u32[]{:S(2)}) %collective-permute-start.16) | collective-permute-done | bytes 278560 | tf_op jit(solution)/shard_map/ppermute | solution.py:369
  106.6 5.0 %collective-permute-done.17 = bf16[136,1024]{1,0:T(8,128)(2,1)S(1)} collective-permute-done((bf16[136,1024]{1,0:T(8,128)(2,1)S(1)}, bf16[136,1024]{1,0:T(8,128)(2,1)S(1)}, u32[]{:S(2)}, u32[]{:S(2)}) %collective-permute-start.17) | collective-permute-done | bytes 278560 | tf_op jit(solution)/shard_map/ppermute | solution.py:369
  111.7 1.1 collective-permute-done.18
  113.8 1.2 collective-permute-start.20
  115.0 1.1 collective-permute-start.21
  116.1 1.2 collective-permute-start.22
  117.4 4.2 %shard_map.119 = (f32[544,640]{1,0:T(8,128)S(1)}, f32[544,640]{1,0:T(8,128)S(1)}, f32[544,128]{1,0:T(8,128)S(1)}) custom-call(bf16[544,1024]{1,0:T(8,128)(2,1)S(1)} %constant_dynamic-update-slice_fusion.refs_0_, bf16[544,1024]{1,0:T(8,128)(2,1)S(1)} %constant_dynamic-update-slice_fusion.4.refs_1_, bf16[1,3072,640]{2,1,0:T(8,128)(2,1)S(1)} %copy-done.2, ...), custom_call_target="tpu_custom_call" | custom-call | flops 2852126720 | bytes 10256384 | tf_op jit(solution)/shard_map/pallas_call | solution.py:118
  121.6 4.2 %shard_map.120 = (f32[544,640]{1,0:T(8,128)S(1)}, f32[544,640]{1,0:T(8,128)S(1)}, f32[544,128]{1,0:T(8,128)S(1)}) custom-call(bf16[544,1024]{1,0:T(8,128)(2,1)S(1)} %collective-permute-done.19.refs_0_, bf16[544,1024]{1,0:T(8,128)(2,1)S(1)} %collective-permute-done.23.refs_1_, bf16[1,3072,640]{2,1,0:T(8,128)(2,1)S(1)} %copy-done.2, ...), custom_call_target="tpu_custom_call" | custom-call | flops 2852126720 | bytes 10256384 | tf_op jit(solution)/shard_map/pallas_call | solution.py:118
  125.8 3.9 %collective-permute-done.21 = bf16[136,1024]{1,0:T(8,128)(2,1)S(1)} collective-permute-done((bf16[136,1024]{1,0:T(8,128)(2,1)S(1)}, bf16[136,1024]{1,0:T(8,128)(2,1)S(1)}, u32[]{:S(2)}, u32[]{:S(2)}) %collective-permute-start.21) | collective-permute-done | bytes 278560 | tf_op jit(solution)/shard_map/ppermute | solution.py:369
  130.0 6.4 %shard_map.121 = (bf16[544,1024]{1,0:T(8,128)(2,1)S(1)}, bf16[544,1024]{1,0:T(8,128)(2,1)S(1)}, bf16[544,1024]{1,0:T(8,128)(2,1)S(1)}) custom-call(bf16[544,1024]{1,0:T(8,128)(2,1)S(1)} %constant_dynamic-update-slice_fusion.8.rows, f32[544,640]{1,0:T(8,128)S(1)} %get-tuple-element.99.gate_in, f32[544,640]{1,0:T(8,128)S(1)} %get-tuple-element.100.up_in, ...), custom_call_target="tpu_custom_call" | custom-call | flops 3565158400 | bytes 13795328 | tf_op jit(solution)/shard_map/pallas_call | solution.py:144
  136.4 7.5 %shard_map.122 = (bf16[544,1024]{1,0:T(8,128)(2,1)}, bf16[544,1024]{1,0:T(8,128)(2,1)}, bf16[544,1024]{1,0:T(8,128)(2,1)}) custom-call(bf16[544,1024]{1,0:T(8,128)(2,1)S(1)} %collective-permute-done.24.rows, f32[544,640]{1,0:T(8,128)S(1)} %get-tuple-element.107.gate_in, f32[544,640]{1,0:T(8,128)S(1)} %get-tuple-element.108.up_in, ...), custom_call_target="tpu_custom_call" | custom-call | flops 3565158400 | bytes 13795328 | tf_op jit(solution)/shard_map/pallas_call | solution.py:144
  144.5 1.8 multiply_reduce_fusion
  146.2 1.1 copy-done.5
  148.8 1.7 add_convert_fusion.2
  151.5 1.3 collective-permute-start.27
  152.8 1.3 collective-permute-start.28
  154.1 6.0 %collective-permute-done.26 = bf16[136,1024]{1,0:T(8,128)(2,1)S(1)} collective-permute-done((bf16[136,1024]{1,0:T(8,128)(2,1)S(1)}, bf16[136,1024]{1,0:T(8,128)(2,1)S(1)}, u32[]{:S(2)}, u32[]{:S(2)}) %collective-permute-start.26) | collective-permute-done | bytes 278560 | tf_op jit(solution)/shard_map/ppermute | solution.py:440
  160.1 4.5 %collective-permute-done.27 = bf16[136,1024]{1,0:T(8,128)(2,1)S(1)} collective-permute-done((bf16[136,1024]{1,0:T(8,128)(2,1)S(1)}, bf16[136,1024]{1,0:T(8,128)(2,1)S(1)}, u32[]{:S(2)}, u32[]{:S(2)}) %collective-permute-start.27) | collective-permute-done | bytes 278560 | tf_op jit(solution)/shard_map/ppermute | solution.py:440
  164.6 1.1 collective-permute-done.28
  167.1 2.4 %collective-permute-start.34 = (bf16[64,1024]{1,0:T(8,128)(2,1)S(1)}, bf16[64,1024]{1,0:T(8,128)(2,1)S(1)}, u32[]{:S(2)}, u32[]{:S(2)}) collective-permute-start(bf16[64,1024]{1,0:T(8,128)(2,1)S(1)} %get-tuple-element.180), channel_id=1, source_target_pairs={{0,3},{1,2},{2,1},{3,0},{4,7},{5,6},{6,5},{7,4},{8,11},{9,10},{10,... | collective-permute-start | bytes 393224 | tf_op jit(solution)/shard_map/ppermute | solution.py:445
  169.5 2.6 %add_convert_fusion = (bf16[544,1024]{1,0:T(8,128)(2,1)S(1)}, bf16[544,1024]{1,0:T(8,128)(2,1)S(1)}) fusion(bf16[544,1024]{1,0:T(8,128)(2,1)} %collective-permute-done.30, bf16[544,1024]{1,0:T(8,128)(2,1)S(1)} %get-tuple-element.124, bf16[544,1024]{1,0:T(8,128)(2,1)} %collective-permute-done.29, bf16[544,1024]{1,0:T(8,128)(2,1)S(1)} %get-tuple-element.116), kind=kLoop, calls=%fused_computation.1 | loop fusion | flops 4456448 | bytes 6684672 | tf_op jit(solution)/shard_map/convert_element_type | solution.py:454
  172.2 1.4 collective-permute-start.31
  174.3 1.5 collective-permute-start.33
  175.8 3.0 %collective-permute-start.35 = (bf16[64,1024]{1,0:T(8,128)(2,1)S(1)}, bf16[64,1024]{1,0:T(8,128)(2,1)S(1)}, u32[]{:S(2)}, u32[]{:S(2)}) collective-permute-start(bf16[64,1024]{1,0:T(8,128)(2,1)S(1)} %get-tuple-element.179), channel_id=1, source_target_pairs={{0,2},{1,3},{2,0},{3,1},{4,6},{5,7},{6,4},{7,5},{8,10},{9,11},{10,... | collective-permute-start | bytes 393224 | tf_op jit(solution)/shard_map/ppermute | solution.py:445
  178.9 2.9 %collective-permute-done.35 = bf16[64,1024]{1,0:T(8,128)(2,1)S(1)} collective-permute-done((bf16[64,1024]{1,0:T(8,128)(2,1)S(1)}, bf16[64,1024]{1,0:T(8,128)(2,1)S(1)}, u32[]{:S(2)}, u32[]{:S(2)}) %collective-permute-start.35) | collective-permute-done | bytes 131104 | tf_op jit(solution)/shard_map/ppermute | solution.py:445
  181.8 2.9 %collective-permute-start.37 = (bf16[136,1024]{1,0:T(8,128)(2,1)S(1)}, bf16[136,1024]{1,0:T(8,128)(2,1)S(1)}, u32[]{:S(2)}, u32[]{:S(2)}) collective-permute-start(bf16[136,1024]{1,0:T(8,128)(2,1)S(1)} %get-tuple-element.151), channel_id=1, source_target_pairs={{0,8},{4,12},{8,0},{12,4},{16,24},{20,28},{24,16},{28,20},{1,9},{5... | collective-permute-start | bytes 835592 | tf_op jit(solution)/shard_map/ppermute | solution.py:440
  185.2 1.4 collective-permute-start.39
  186.6 2.1 collective-permute-done.33
  190.1 1.4 collective-permute-start.40
  191.5 2.1 collective-permute-start.41
  193.9 2.0 collective-permute-start.42
  195.9 2.8 %collective-permute-done.38 = bf16[136,1024]{1,0:T(8,128)(2,1)S(1)} collective-permute-done((bf16[136,1024]{1,0:T(8,128)(2,1)S(1)}, bf16[136,1024]{1,0:T(8,128)(2,1)S(1)}, u32[]{:S(2)}, u32[]{:S(2)}) %collective-permute-start.38) | collective-permute-done | bytes 278560 | tf_op jit(solution)/shard_map/ppermute | solution.py:440
  198.6 2.1 collective-permute-done.41
  202.1 2.0 collective-permute-start.43
  204.1 2.4 %collective-permute-start.45 = (bf16[64,1024]{1,0:T(8,128)(2,1)S(1)}, bf16[64,1024]{1,0:T(8,128)(2,1)}, u32[]{:S(2)}, u32[]{:S(2)}) collective-permute-start(bf16[64,1024]{1,0:T(8,128)(2,1)S(1)} %get-tuple-element.172), channel_id=1, source_target_pairs={{0,1},{1,0},{2,3},{3,2},{4,5},{5,4},{6,7},{7,6},{8,9},{9,8},{10,11... | collective-permute-start | bytes 393224 | tf_op jit(solution)/shard_map/ppermute | solution.py:445
  206.5 2.6 %collective-permute-done.43 = bf16[64,1024]{1,0:T(8,128)(2,1)S(1)} collective-permute-done((bf16[64,1024]{1,0:T(8,128)(2,1)S(1)}, bf16[64,1024]{1,0:T(8,128)(2,1)S(1)}, u32[]{:S(2)}, u32[]{:S(2)}) %collective-permute-start.43) | collective-permute-done | bytes 131104 | tf_op jit(solution)/shard_map/ppermute | solution.py:445
  209.1 3.3 %collective-permute-done.44 = bf16[64,1024]{1,0:T(8,128)(2,1)S(1)} collective-permute-done((bf16[64,1024]{1,0:T(8,128)(2,1)S(1)}, bf16[64,1024]{1,0:T(8,128)(2,1)S(1)}, u32[]{:S(2)}, u32[]{:S(2)}) %collective-permute-start.44) | collective-permute-done | bytes 131104 | tf_op jit(solution)/shard_map/ppermute | solution.py:445
  212.4 1.4 add_convert_fusion.11
  (150 shorter events, 22.8 us)
Async XLA Ops:
  0.0 23.0 %copy-start = (bf16[256,1024]{1,0:T(8,128)(2,1)S(1)}, bf16[256,1024]{1,0:T(8,128)(2,1)}, u32[]{:S(2)}) copy-start(bf16[256,1024]{1,0:T(8,128)(2,1)} %param.13) | copy-start | bytes 1572868
  0.0 3.2 %copy-start.15 = (s32[16]{0:T(128)S(1)}, s32[16]{0:T(128)}, u32[]{:S(2)}) copy-start(s32[16]{0:T(128)} %lengths_ref.1) | copy-start | bytes 196
  0.0 7.4 %copy-start.16 = (f32[8]{0:T(128)S(1)}, f32[8]{0:T(128)}, u32[]{:S(2)}) copy-start(f32[8]{0:T(128)} %rates_ref.1) | copy-start | bytes 100
  0.0 21.5 %copy-start.7 = (bf16[256,1024]{1,0:T(8,128)(2,1)S(1)}, bf16[256,1024]{1,0:T(8,128)(2,1)}, u32[]{:S(2)}) copy-start(bf16[256,1024]{1,0:T(8,128)(2,1)} %values.1) | copy-start | bytes 1572868
  2.7 5.5 %collective-permute-start = (bf16[8,128,128]{2,1,0:T(8,128)(2,1)}, bf16[8,128,128]{2,1,0:T(8,128)(2,1)S(1)}, u32[]{:S(2)}, u32[]{:S(2)}) collective-permute-start(bf16[8,128,128]{2,1,0:T(8,128)(2,1)} %shard_map.118), channel_id=1, source_target_pairs={{0,4},{4,0},{8,12},{12,8},{16,20},{20,16},{24,28},{28,24},{1,5},{5... | collective-permute-start | bytes 786440 | tf_op jit(solution)/shard_map/ppermute | solution.py:243
  9.2 13.5 %copy-start.11 = (bf16[8,128,128]{2,1,0:T(8,128)(2,1)S(1)}, bf16[8,128,128]{2,1,0:T(8,128)(2,1)}, u32[]{:S(2)}) copy-start(bf16[8,128,128]{2,1,0:T(8,128)(2,1)} %shard_map.118) | copy-start | bytes 786436
  9.3 6.8 %collective-permute-start.1 = (bf16[4,128,128]{2,1,0:T(8,128)(2,1)S(1)}, bf16[4,128,128]{2,1,0:T(8,128)(2,1)S(1)}, u32[]{:S(2)}, u32[]{:S(2)}) collective-permute-start(bf16[4,128,128]{2,1,0:T(8,128)(2,1)S(1)} %fusion.58), channel_id=1, source_target_pairs={{0,8},{4,12},{8,0},{12,4},{16,24},{20,28},{24,16},{28,20},{1,9},{5... | collective-permute-start | bytes 393224 | tf_op jit(solution)/shard_map/ppermute | solution.py:261
  11.8 8.4 %collective-permute-start.2 = (bf16[4,128,128]{2,1,0:T(8,128)(2,1)S(1)}, bf16[4,128,128]{2,1,0:T(8,128)(2,1)S(1)}, u32[]{:S(2)}, u32[]{:S(2)}) collective-permute-start(bf16[4,128,128]{2,1,0:T(8,128)(2,1)S(1)} %fusion.58), channel_id=1, source_target_pairs={{0,16},{4,20},{8,24},{12,28},{16,0},{20,4},{24,8},{28,12},{1,17},{... | collective-permute-start | bytes 393224 | tf_op jit(solution)/shard_map/ppermute | solution.py:261
  13.3 6.9 %collective-permute-start.3 = (bf16[4,128,128]{2,1,0:T(8,128)(2,1)S(1)}, bf16[4,128,128]{2,1,0:T(8,128)(2,1)S(1)}, u32[]{:S(2)}, u32[]{:S(2)}) collective-permute-start(bf16[4,128,128]{2,1,0:T(8,128)(2,1)S(1)} %fusion.58), channel_id=1, source_target_pairs={{0,24},{4,28},{8,16},{12,20},{16,8},{20,12},{24,0},{28,4},{1,25},{... | collective-permute-start | bytes 393224 | tf_op jit(solution)/shard_map/ppermute | solution.py:261
  21.3 1.4 collective-permute-start.4
  23.0 1.0 copy-start.12
  26.1 5.9 %copy-start.13 = (s32[256,2]{0,1:T(2,128)S(1)}, s32[256,2]{0,1:T(2,128)}, u32[]{:S(2)}) copy-start(s32[256,2]{0,1:T(2,128)} %param.23) | copy-start | bytes 6148
  28.4 15.1 %collective-permute-start.5 = (bf16[256,1024]{1,0:T(8,128)(2,1)S(1)}, bf16[256,1024]{1,0:T(8,128)(2,1)S(1)}, u32[]{:S(2)}, u32[]{:S(2)}) collective-permute-start(bf16[256,1024]{1,0:T(8,128)(2,1)S(1)} %fusion.16), channel_id=1, source_target_pairs={{0,1},{3,2},{4,5},{7,6},{8,9},{11,10},{12,13},{15,14},{16,17},{19,... | collective-permute-start | bytes 1572872 | tf_op jit(solution)/shard_map/ppermute | solution.py:355
  43.7 10.5 %collective-permute-start.7 = (bf16[256,1024]{1,0:T(8,128)(2,1)S(1)}, bf16[256,1024]{1,0:T(8,128)(2,1)S(1)}, u32[]{:S(2)}, u32[]{:S(2)}) collective-permute-start(bf16[256,1024]{1,0:T(8,128)(2,1)S(1)} %add_convert_fusion.8), channel_id=1, source_target_pairs={{1,2},{2,1},{5,6},{6,5},{9,10},{10,9},{13,14},{14,13},{17,18},{18,... | collective-permute-start | bytes 1572872 | tf_op jit(solution)/shard_map/ppermute | solution.py:360
  44.4 17.7 %collective-permute-start.6 = (bf16[256,1024]{1,0:T(8,128)(2,1)S(1)}, bf16[256,1024]{1,0:T(8,128)(2,1)S(1)}, u32[]{:S(2)}, u32[]{:S(2)}) collective-permute-start(bf16[256,1024]{1,0:T(8,128)(2,1)S(1)} %fusion.19), channel_id=1, source_target_pairs={{0,1},{3,2},{4,5},{7,6},{8,9},{11,10},{12,13},{15,14},{16,17},{19,... | collective-permute-start | bytes 1572872 | tf_op jit(solution)/shard_map/ppermute | solution.py:355
  54.2 8.9 %copy-start.6 = (bf16[256,3072]{1,0:T(8,128)(2,1)S(1)}, bf16[256,3072]{1,0:T(8,128)(2,1)}, u32[]{:S(2)}) copy-start(bf16[256,3072]{1,0:T(8,128)(2,1)} %param.12) | copy-start | bytes 4718596
  62.4 5.3 %collective-permute-start.9 = (bf16[256,1024]{1,0:T(8,128)(2,1)S(1)}, bf16[256,1024]{1,0:T(8,128)(2,1)S(1)}, u32[]{:S(2)}, u32[]{:S(2)}) collective-permute-start(bf16[256,1024]{1,0:T(8,128)(2,1)S(1)} %add_convert_fusion.6), channel_id=1, source_target_pairs={{1,2},{2,1},{5,6},{6,5},{9,10},{10,9},{13,14},{14,13},{17,18},{18,... | collective-permute-start | bytes 1572872 | tf_op jit(solution)/shard_map/ppermute | solution.py:360
  63.4 14.3 %collective-permute-start.8 = (bf16[256,1024]{1,0:T(8,128)(2,1)S(1)}, bf16[256,1024]{1,0:T(8,128)(2,1)S(1)}, u32[]{:S(2)}, u32[]{:S(2)}) collective-permute-start(bf16[256,1024]{1,0:T(8,128)(2,1)S(1)} %broadcast_select_fusion.3), channel_id=1, source_target_pairs={{0,1},{3,2},{1,0},{2,3},{4,5},{7,6},{5,4},{6,7},{8,9},{11,10},{9,8... | collective-permute-start | bytes 1572872 | tf_op jit(solution)/shard_map/ppermute | solution.py:355
  78.1 3.2 %copy-start.10 = (bf16[256,1024]{1,0:T(8,128)(2,1)}, bf16[256,1024]{1,0:T(8,128)(2,1)S(1)}, u32[]{:S(2)}) copy-start(bf16[256,1024]{1,0:T(8,128)(2,1)S(1)} %broadcast_select_fusion.2) | copy-start | bytes 1572868
  78.3 16.1 %collective-permute-start.11 = (bf16[256,1024]{1,0:T(8,128)(2,1)S(1)}, bf16[256,1024]{1,0:T(8,128)(2,1)S(1)}, u32[]{:S(2)}, u32[]{:S(2)}) collective-permute-start(bf16[256,1024]{1,0:T(8,128)(2,1)S(1)} %add_convert_fusion.4), channel_id=1, source_target_pairs={{1,2},{2,1},{5,6},{6,5},{9,10},{10,9},{13,14},{14,13},{17,18},{18,... | collective-permute-start | bytes 1572872 | tf_op jit(solution)/shard_map/ppermute | solution.py:360
  79.3 15.1 %collective-permute-start.10 = (bf16[256,1024]{1,0:T(8,128)(2,1)S(1)}, bf16[256,1024]{1,0:T(8,128)(2,1)S(1)}, u32[]{:S(2)}, u32[]{:S(2)}) collective-permute-start(bf16[256,1024]{1,0:T(8,128)(2,1)S(1)} %add_convert_fusion.5), channel_id=1, source_target_pairs={{1,0},{2,3},{5,4},{6,7},{9,8},{10,11},{13,12},{14,15},{17,16},{18,... | collective-permute-start | bytes 1572872 | tf_op jit(solution)/shard_map/ppermute | solution.py:355
  81.3 9.0 %collective-permute-start.12 = (bf16[136,1024]{1,0:T(8,128)(2,1)S(1)}, bf16[136,1024]{1,0:T(8,128)(2,1)S(1)}, u32[]{:S(2)}, u32[]{:S(2)}) collective-permute-start(bf16[136,1024]{1,0:T(8,128)(2,1)S(1)} %get-tuple-element.170), channel_id=1, source_target_pairs={{0,8},{4,12},{8,0},{12,4},{16,24},{20,28},{24,16},{28,20},{1,9},{5... | collective-permute-start | bytes 835592 | tf_op jit(solution)/shard_map/ppermute | solution.py:369
  82.6 11.7 %collective-permute-start.13 = (bf16[136,1024]{1,0:T(8,128)(2,1)S(1)}, bf16[136,1024]{1,0:T(8,128)(2,1)S(1)}, u32[]{:S(2)}, u32[]{:S(2)}) collective-permute-start(bf16[136,1024]{1,0:T(8,128)(2,1)S(1)} %get-tuple-element.169), channel_id=1, source_target_pairs={{0,16},{4,20},{8,24},{12,28},{16,0},{20,4},{24,8},{28,12},{1,17},{... | collective-permute-start | bytes 835592 | tf_op jit(solution)/shard_map/ppermute | solution.py:369
  83.5 10.9 %collective-permute-start.14 = (bf16[136,1024]{1,0:T(8,128)(2,1)S(1)}, bf16[136,1024]{1,0:T(8,128)(2,1)S(1)}, u32[]{:S(2)}, u32[]{:S(2)}) collective-permute-start(bf16[136,1024]{1,0:T(8,128)(2,1)S(1)} %get-tuple-element.168), channel_id=1, source_target_pairs={{0,24},{4,28},{8,16},{12,20},{16,8},{20,12},{24,0},{28,4},{1,25},{... | collective-permute-start | bytes 835592 | tf_op jit(solution)/shard_map/ppermute | solution.py:369
  94.5 18.3 %collective-permute-start.19 = (bf16[544,1024]{1,0:T(8,128)(2,1)S(1)}, bf16[544,1024]{1,0:T(8,128)(2,1)S(1)}, u32[]{:S(2)}, u32[]{:S(2)}) collective-permute-start(bf16[544,1024]{1,0:T(8,128)(2,1)S(1)} %constant_dynamic-update-slice_fusion.refs_0_), channel_id=1, source_target_pairs={{0,4},{4,0},{8,12},{12,8},{16,20},{20,16},{24,28},{28,24},{1,5},{5... | collective-permute-start | bytes 3342344 | tf_op jit(solution)/shard_map/ppermute | solution.py:372
  94.8 18.0 %collective-permute-start.15 = (bf16[256,1024]{1,0:T(8,128)(2,1)S(1)}, bf16[256,1024]{1,0:T(8,128)(2,1)S(1)}, u32[]{:S(2)}, u32[]{:S(2)}) collective-permute-start(bf16[256,1024]{1,0:T(8,128)(2,1)S(1)} %add_convert_fusion.3), channel_id=1, source_target_pairs={{1,0},{2,3},{5,4},{6,7},{9,8},{10,11},{13,12},{14,15},{17,16},{18,... | collective-permute-start | bytes 1572872 | tf_op jit(solution)/shard_map/ppermute | solution.py:355
  96.4 16.7 %copy-start.8 = (bf16[256,1024]{1,0:T(8,128)(2,1)}, bf16[256,1024]{1,0:T(8,128)(2,1)S(1)}, u32[]{:S(2)}) copy-start(bf16[256,1024]{1,0:T(8,128)(2,1)S(1)} %broadcast_select_fusion.1) | copy-start | bytes 1572868
  97.0 20.4 %copy-start.3 = (bf16[1,3072,640]{2,1,0:T(8,128)(2,1)S(1)}, bf16[1,3072,640]{2,1,0:T(8,128)(2,1)}, u32[]{:S(2)}) copy-start(bf16[1,3072,640]{2,1,0:T(8,128)(2,1)} %up_hbm.3) | copy-start | bytes 11796484
  97.1 9.5 %collective-permute-start.16 = (bf16[136,1024]{1,0:T(8,128)(2,1)S(1)}, bf16[136,1024]{1,0:T(8,128)(2,1)S(1)}, u32[]{:S(2)}, u32[]{:S(2)}) collective-permute-start(bf16[136,1024]{1,0:T(8,128)(2,1)S(1)} %get-tuple-element.166), channel_id=1, source_target_pairs={{0,8},{4,12},{8,0},{12,4},{16,24},{20,28},{24,16},{28,20},{1,9},{5... | collective-permute-start | bytes 835592 | tf_op jit(solution)/shard_map/ppermute | solution.py:369
  98.1 13.6 %collective-permute-start.17 = (bf16[136,1024]{1,0:T(8,128)(2,1)S(1)}, bf16[136,1024]{1,0:T(8,128)(2,1)S(1)}, u32[]{:S(2)}, u32[]{:S(2)}) collective-permute-start(bf16[136,1024]{1,0:T(8,128)(2,1)S(1)} %get-tuple-element.165), channel_id=1, source_target_pairs={{0,16},{4,20},{8,24},{12,28},{16,0},{20,4},{24,8},{28,12},{1,17},{... | collective-permute-start | bytes 835592 | tf_op jit(solution)/shard_map/ppermute | solution.py:369
  99.4 13.4 %collective-permute-start.18 = (bf16[136,1024]{1,0:T(8,128)(2,1)S(1)}, bf16[136,1024]{1,0:T(8,128)(2,1)S(1)}, u32[]{:S(2)}, u32[]{:S(2)}) collective-permute-start(bf16[136,1024]{1,0:T(8,128)(2,1)S(1)} %get-tuple-element.164), channel_id=1, source_target_pairs={{0,24},{4,28},{8,16},{12,20},{16,8},{20,12},{24,0},{28,4},{1,25},{... | collective-permute-start | bytes 835592 | tf_op jit(solution)/shard_map/ppermute | solution.py:369
  112.9 8.7 %collective-permute-start.23 = (bf16[544,1024]{1,0:T(8,128)(2,1)S(1)}, bf16[544,1024]{1,0:T(8,128)(2,1)S(1)}, u32[]{:S(2)}, u32[]{:S(2)}) collective-permute-start(bf16[544,1024]{1,0:T(8,128)(2,1)S(1)} %constant_dynamic-update-slice_fusion.4.refs_1_), channel_id=1, source_target_pairs={{0,4},{4,0},{8,12},{12,8},{16,20},{20,16},{24,28},{28,24},{1,5},{5... | collective-permute-start | bytes 3342344 | tf_op jit(solution)/shard_map/ppermute | solution.py:372
  113.1 3.1 %copy-start.9 = (bf16[256,1024]{1,0:T(8,128)(2,1)}, bf16[256,1024]{1,0:T(8,128)(2,1)S(1)}, u32[]{:S(2)}) copy-start(bf16[256,1024]{1,0:T(8,128)(2,1)S(1)} %broadcast_select_fusion) | copy-start | bytes 1572868
  113.1 4.3 %copy-start.2 = (bf16[1,3072,640]{2,1,0:T(8,128)(2,1)S(1)}, bf16[1,3072,640]{2,1,0:T(8,128)(2,1)}, u32[]{:S(2)}) copy-start(bf16[1,3072,640]{2,1,0:T(8,128)(2,1)} %gate_hbm.3) | copy-start | bytes 11796484
  113.8 12.0 %collective-permute-start.20 = (bf16[136,1024]{1,0:T(8,128)(2,1)S(1)}, bf16[136,1024]{1,0:T(8,128)(2,1)S(1)}, u32[]{:S(2)}, u32[]{:S(2)}) collective-permute-start(bf16[136,1024]{1,0:T(8,128)(2,1)S(1)} %get-tuple-element.162), channel_id=1, source_target_pairs={{0,8},{4,12},{8,0},{12,4},{16,24},{20,28},{24,16},{28,20},{1,9},{5... | collective-permute-start | bytes 835592 | tf_op jit(solution)/shard_map/ppermute | solution.py:369
  115.0 14.7 %collective-permute-start.21 = (bf16[136,1024]{1,0:T(8,128)(2,1)S(1)}, bf16[136,1024]{1,0:T(8,128)(2,1)S(1)}, u32[]{:S(2)}, u32[]{:S(2)}) collective-permute-start(bf16[136,1024]{1,0:T(8,128)(2,1)S(1)} %get-tuple-element.161), channel_id=1, source_target_pairs={{0,16},{4,20},{8,24},{12,28},{16,0},{20,4},{24,8},{28,12},{1,17},{... | collective-permute-start | bytes 835592 | tf_op jit(solution)/shard_map/ppermute | solution.py:369
  116.1 13.6 %collective-permute-start.22 = (bf16[136,1024]{1,0:T(8,128)(2,1)S(1)}, bf16[136,1024]{1,0:T(8,128)(2,1)S(1)}, u32[]{:S(2)}, u32[]{:S(2)}) collective-permute-start(bf16[136,1024]{1,0:T(8,128)(2,1)S(1)} %get-tuple-element.160), channel_id=1, source_target_pairs={{0,24},{4,28},{8,16},{12,20},{16,8},{20,12},{24,0},{28,4},{1,25},{... | collective-permute-start | bytes 835592 | tf_op jit(solution)/shard_map/ppermute | solution.py:369
  121.6 8.4 %copy-start.4 = (bf16[1,640,3072]{2,1,0:T(8,128)(2,1)S(1)}, bf16[1,640,3072]{2,1,0:T(8,128)(2,1)}, u32[]{:S(2)}) copy-start(bf16[1,640,3072]{2,1,0:T(8,128)(2,1)} %down_hbm.3) | copy-start | bytes 11796484
  129.9 6.5 %collective-permute-start.24 = (bf16[544,1024]{1,0:T(8,128)(2,1)S(1)}, bf16[544,1024]{1,0:T(8,128)(2,1)S(1)}, u32[]{:S(2)}, u32[]{:S(2)}) collective-permute-start(bf16[544,1024]{1,0:T(8,128)(2,1)S(1)} %constant_dynamic-update-slice_fusion.8.rows), channel_id=1, source_target_pairs={{0,4},{4,0},{8,12},{12,8},{16,20},{20,16},{24,28},{28,24},{1,5},{5... | collective-permute-start | bytes 3342344 | tf_op jit(solution)/shard_map/ppermute | solution.py:372
  143.9 4.9 %collective-permute-start.25 = (bf16[544,1024]{1,0:T(8,128)(2,1)}, bf16[544,1024]{1,0:T(8,128)(2,1)}, u32[]{:S(2)}, u32[]{:S(2)}) collective-permute-start(bf16[544,1024]{1,0:T(8,128)(2,1)} %get-tuple-element.110), channel_id=1, source_target_pairs={{0,4},{4,0},{8,12},{12,8},{16,20},{20,16},{24,28},{28,24},{1,5},{5... | collective-permute-start | bytes 3342344 | tf_op jit(solution)/shard_map/ppermute | solution.py:448
  144.5 2.9 %copy-start.14 = (bf16[3072,4]{0,1:T(4,128)(2,1)S(1)}, bf16[3072,4]{0,1:T(4,128)(2,1)}, u32[]{:S(2)}) copy-start(bf16[3072,4]{0,1:T(4,128)(2,1)} %param.19) | copy-start | bytes 73732
  146.2 1.2 copy-start.5
  147.9 6.2 %collective-permute-start.29 = (bf16[544,1024]{1,0:T(8,128)(2,1)}, bf16[544,1024]{1,0:T(8,128)(2,1)}, u32[]{:S(2)}, u32[]{:S(2)}) collective-permute-start(bf16[544,1024]{1,0:T(8,128)(2,1)} %get-tuple-element.111), channel_id=1, source_target_pairs={{0,4},{4,0},{8,12},{12,8},{16,20},{20,16},{24,28},{28,24},{1,5},{5... | collective-permute-start | bytes 3342344 | tf_op jit(solution)/shard_map/ppermute | solution.py:448
  148.0 6.2 %collective-permute-start.30 = (bf16[544,1024]{1,0:T(8,128)(2,1)}, bf16[544,1024]{1,0:T(8,128)(2,1)}, u32[]{:S(2)}, u32[]{:S(2)}) collective-permute-start(bf16[544,1024]{1,0:T(8,128)(2,1)} %get-tuple-element.112), channel_id=1, source_target_pairs={{0,4},{4,0},{8,12},{12,8},{16,20},{20,16},{24,28},{28,24},{1,5},{5... | collective-permute-start | bytes 3342344 | tf_op jit(solution)/shard_map/ppermute | solution.py:448
  150.5 9.6 %collective-permute-start.26 = (bf16[136,1024]{1,0:T(8,128)(2,1)S(1)}, bf16[136,1024]{1,0:T(8,128)(2,1)S(1)}, u32[]{:S(2)}, u32[]{:S(2)}) collective-permute-start(bf16[136,1024]{1,0:T(8,128)(2,1)S(1)} %get-tuple-element.159), channel_id=1, source_target_pairs={{0,8},{4,12},{8,0},{12,4},{16,24},{20,28},{24,16},{28,20},{1,9},{5... | collective-permute-start | bytes 835592 | tf_op jit(solution)/shard_map/ppermute | solution.py:440
  151.5 13.2 %collective-permute-start.27 = (bf16[136,1024]{1,0:T(8,128)(2,1)S(1)}, bf16[136,1024]{1,0:T(8,128)(2,1)S(1)}, u32[]{:S(2)}, u32[]{:S(2)}) collective-permute-start(bf16[136,1024]{1,0:T(8,128)(2,1)S(1)} %get-tuple-element.158), channel_id=1, source_target_pairs={{0,16},{4,20},{8,24},{12,28},{16,0},{20,4},{24,8},{28,12},{1,17},{... | collective-permute-start | bytes 835592 | tf_op jit(solution)/shard_map/ppermute | solution.py:440
  152.8 13.0 %collective-permute-start.28 = (bf16[136,1024]{1,0:T(8,128)(2,1)S(1)}, bf16[136,1024]{1,0:T(8,128)(2,1)S(1)}, u32[]{:S(2)}, u32[]{:S(2)}) collective-permute-start(bf16[136,1024]{1,0:T(8,128)(2,1)S(1)} %get-tuple-element.157), channel_id=1, source_target_pairs={{0,24},{4,28},{8,16},{12,20},{16,8},{20,12},{24,0},{28,4},{1,25},{... | collective-permute-start | bytes 835592 | tf_op jit(solution)/shard_map/ppermute | solution.py:440
  167.1 11.7 %collective-permute-start.34 = (bf16[64,1024]{1,0:T(8,128)(2,1)S(1)}, bf16[64,1024]{1,0:T(8,128)(2,1)S(1)}, u32[]{:S(2)}, u32[]{:S(2)}) collective-permute-start(bf16[64,1024]{1,0:T(8,128)(2,1)S(1)} %get-tuple-element.180), channel_id=1, source_target_pairs={{0,3},{1,2},{2,1},{3,0},{4,7},{5,6},{6,5},{7,4},{8,11},{9,10},{10,... | collective-permute-start | bytes 393224 | tf_op jit(solution)/shard_map/ppermute | solution.py:445
  172.2 13.0 %collective-permute-start.31 = (bf16[136,1024]{1,0:T(8,128)(2,1)S(1)}, bf16[136,1024]{1,0:T(8,128)(2,1)S(1)}, u32[]{:S(2)}, u32[]{:S(2)}) collective-permute-start(bf16[136,1024]{1,0:T(8,128)(2,1)S(1)} %get-tuple-element.155), channel_id=1, source_target_pairs={{0,8},{4,12},{8,0},{12,4},{16,24},{20,28},{24,16},{28,20},{1,9},{5... | collective-permute-start | bytes 835592 | tf_op jit(solution)/shard_map/ppermute | solution.py:440
  173.6 13.1 %collective-permute-start.32 = (bf16[136,1024]{1,0:T(8,128)(2,1)S(1)}, bf16[136,1024]{1,0:T(8,128)(2,1)S(1)}, u32[]{:S(2)}, u32[]{:S(2)}) collective-permute-start(bf16[136,1024]{1,0:T(8,128)(2,1)S(1)} %get-tuple-element.154), channel_id=1, source_target_pairs={{0,16},{4,20},{8,24},{12,28},{16,0},{20,4},{24,8},{28,12},{1,17},{... | collective-permute-start | bytes 835592 | tf_op jit(solution)/shard_map/ppermute | solution.py:440
  174.3 14.4 %collective-permute-start.33 = (bf16[136,1024]{1,0:T(8,128)(2,1)S(1)}, bf16[136,1024]{1,0:T(8,128)(2,1)S(1)}, u32[]{:S(2)}, u32[]{:S(2)}) collective-permute-start(bf16[136,1024]{1,0:T(8,128)(2,1)S(1)} %get-tuple-element.153), channel_id=1, source_target_pairs={{0,24},{4,28},{8,16},{12,20},{16,8},{20,12},{24,0},{28,4},{1,25},{... | collective-permute-start | bytes 835592 | tf_op jit(solution)/shard_map/ppermute | solution.py:440
  175.8 6.0 %collective-permute-start.35 = (bf16[64,1024]{1,0:T(8,128)(2,1)S(1)}, bf16[64,1024]{1,0:T(8,128)(2,1)S(1)}, u32[]{:S(2)}, u32[]{:S(2)}) collective-permute-start(bf16[64,1024]{1,0:T(8,128)(2,1)S(1)} %get-tuple-element.179), channel_id=1, source_target_pairs={{0,2},{1,3},{2,0},{3,1},{4,6},{5,7},{6,4},{7,5},{8,10},{9,11},{10,... | collective-permute-start | bytes 393224 | tf_op jit(solution)/shard_map/ppermute | solution.py:445
  178.8 5.9 %collective-permute-start.36 = (bf16[64,1024]{1,0:T(8,128)(2,1)S(1)}, bf16[64,1024]{1,0:T(8,128)(2,1)S(1)}, u32[]{:S(2)}, u32[]{:S(2)}) collective-permute-start(bf16[64,1024]{1,0:T(8,128)(2,1)S(1)} %get-tuple-element.178), channel_id=1, source_target_pairs={{0,1},{1,0},{2,3},{3,2},{4,5},{5,4},{6,7},{7,6},{8,9},{9,8},{10,11... | collective-permute-start | bytes 393224 | tf_op jit(solution)/shard_map/ppermute | solution.py:445
  181.8 12.1 %collective-permute-start.37 = (bf16[136,1024]{1,0:T(8,128)(2,1)S(1)}, bf16[136,1024]{1,0:T(8,128)(2,1)S(1)}, u32[]{:S(2)}, u32[]{:S(2)}) collective-permute-start(bf16[136,1024]{1,0:T(8,128)(2,1)S(1)} %get-tuple-element.151), channel_id=1, source_target_pairs={{0,8},{4,12},{8,0},{12,4},{16,24},{20,28},{24,16},{28,20},{1,9},{5... | collective-permute-start | bytes 835592 | tf_op jit(solution)/shard_map/ppermute | solution.py:440
  184.7 14.0 %collective-permute-start.38 = (bf16[136,1024]{1,0:T(8,128)(2,1)S(1)}, bf16[136,1024]{1,0:T(8,128)(2,1)S(1)}, u32[]{:S(2)}, u32[]{:S(2)}) collective-permute-start(bf16[136,1024]{1,0:T(8,128)(2,1)S(1)} %get-tuple-element.150), channel_id=1, source_target_pairs={{0,16},{4,20},{8,24},{12,28},{16,0},{20,4},{24,8},{28,12},{1,17},{... | collective-permute-start | bytes 835592 | tf_op jit(solution)/shard_map/ppermute | solution.py:440
  185.2 13.4 %collective-permute-start.39 = (bf16[136,1024]{1,0:T(8,128)(2,1)S(1)}, bf16[136,1024]{1,0:T(8,128)(2,1)S(1)}, u32[]{:S(2)}, u32[]{:S(2)}) collective-permute-start(bf16[136,1024]{1,0:T(8,128)(2,1)S(1)} %get-tuple-element.149), channel_id=1, source_target_pairs={{0,24},{4,28},{8,16},{12,20},{16,8},{20,12},{24,0},{28,4},{1,25},{... | collective-permute-start | bytes 835592 | tf_op jit(solution)/shard_map/ppermute | solution.py:440
  190.1 8.6 %collective-permute-start.40 = (bf16[64,1024]{1,0:T(8,128)(2,1)S(1)}, bf16[64,1024]{1,0:T(8,128)(2,1)S(1)}, u32[]{:S(2)}, u32[]{:S(2)}) collective-permute-start(bf16[64,1024]{1,0:T(8,128)(2,1)S(1)} %get-tuple-element.177), channel_id=1, source_target_pairs={{0,3},{1,2},{2,1},{3,0},{4,7},{5,6},{6,5},{7,4},{8,11},{9,10},{10,... | collective-permute-start | bytes 393224 | tf_op jit(solution)/shard_map/ppermute | solution.py:445
  191.5 9.3 %collective-permute-start.41 = (bf16[64,1024]{1,0:T(8,128)(2,1)S(1)}, bf16[64,1024]{1,0:T(8,128)(2,1)S(1)}, u32[]{:S(2)}, u32[]{:S(2)}) collective-permute-start(bf16[64,1024]{1,0:T(8,128)(2,1)S(1)} %get-tuple-element.176), channel_id=1, source_target_pairs={{0,2},{1,3},{2,0},{3,1},{4,6},{5,7},{6,4},{7,5},{8,10},{9,11},{10,... | collective-permute-start | bytes 393224 | tf_op jit(solution)/shard_map/ppermute | solution.py:445
  193.9 6.9 %collective-permute-start.42 = (bf16[64,1024]{1,0:T(8,128)(2,1)S(1)}, bf16[64,1024]{1,0:T(8,128)(2,1)S(1)}, u32[]{:S(2)}, u32[]{:S(2)}) collective-permute-start(bf16[64,1024]{1,0:T(8,128)(2,1)S(1)} %get-tuple-element.175), channel_id=1, source_target_pairs={{0,1},{1,0},{2,3},{3,2},{4,5},{5,4},{6,7},{7,6},{8,9},{9,8},{10,11... | collective-permute-start | bytes 393224 | tf_op jit(solution)/shard_map/ppermute | solution.py:445
  202.1 7.0 %collective-permute-start.43 = (bf16[64,1024]{1,0:T(8,128)(2,1)S(1)}, bf16[64,1024]{1,0:T(8,128)(2,1)S(1)}, u32[]{:S(2)}, u32[]{:S(2)}) collective-permute-start(bf16[64,1024]{1,0:T(8,128)(2,1)S(1)} %get-tuple-element.174), channel_id=1, source_target_pairs={{0,3},{1,2},{2,1},{3,0},{4,7},{5,6},{6,5},{7,4},{8,11},{9,10},{10,... | collective-permute-start | bytes 393224 | tf_op jit(solution)/shard_map/ppermute | solution.py:445
  204.1 8.3 %collective-permute-start.44 = (bf16[64,1024]{1,0:T(8,128)(2,1)S(1)}, bf16[64,1024]{1,0:T(8,128)(2,1)S(1)}, u32[]{:S(2)}, u32[]{:S(2)}) collective-permute-start(bf16[64,1024]{1,0:T(8,128)(2,1)S(1)} %get-tuple-element.173), channel_id=1, source_target_pairs={{0,2},{1,3},{2,0},{3,1},{4,6},{5,7},{6,4},{7,5},{8,10},{9,11},{10,... | collective-permute-start | bytes 393224 | tf_op jit(solution)/shard_map/ppermute | solution.py:445
  204.1 8.3 %collective-permute-start.45 = (bf16[64,1024]{1,0:T(8,128)(2,1)S(1)}, bf16[64,1024]{1,0:T(8,128)(2,1)}, u32[]{:S(2)}, u32[]{:S(2)}) collective-permute-start(bf16[64,1024]{1,0:T(8,128)(2,1)S(1)} %get-tuple-element.172), channel_id=1, source_target_pairs={{0,1},{1,0},{2,3},{3,2},{4,5},{5,4},{6,7},{7,6},{8,9},{9,8},{10,11... | collective-permute-start | bytes 393224 | tf_op jit(solution)/shard_map/ppermute | solution.py:445
  206.5 8.1 %copy-start.1 = (bf16[256,1024]{1,0:T(8,128)(2,1)S(1)}, bf16[256,1024]{1,0:T(8,128)(2,1)}, u32[]{:S(2)}) copy-start(bf16[256,1024]{1,0:T(8,128)(2,1)} %param.13) | copy-start | bytes 1572868

commit v5 on v4

--- a/solution.py
+++ b/solution.py
@@ -185,6 +185,43 @@
         state = lax.dot_general(high, v, dims, preferred_element_type=F32)
         state = state + lax.dot_general(low, v, dims, preferred_element_type=F32)
         out[h] = state.astype(BF)
+
+
+def inside_kernel(place_ref, lengths_ref, rates_ref, queries, keys, values, out, same_out):
+    block_len = queries.shape[0]
+    heads = rates_ref.shape[0]
+    size = queries.shape[1] // heads
+    base = place_ref[0]
+    index = lax.broadcasted_iota(jnp.int32, (block_len, 1), 0)
+    start = jnp.int32(0)
+    doc_start = jnp.zeros((block_len, 1), jnp.int32)
+    for i in range(lengths_ref.shape[0]):
+        doc_start = jnp.where(base + index >= start, start, doc_start)
+        start = start + lengths_ref[i]
+    row = lax.broadcasted_iota(jnp.int32, (block_len, block_len), 0)
+    col = lax.broadcasted_iota(jnp.int32, (block_len, block_len), 1)
+    allowed = (col <= row) & (base + col >= doc_start)
+    lag = jnp.maximum(row - col, 0).astype(F32)
+    same_out[...] = jnp.broadcast_to(jnp.where(doc_start <= base, 1.0, 0.0), same_out.shape)
+    for h in range(heads):
+        cols = slice(h * size, (h + 1) * size)
+        scores = lax.dot_general(
+            queries[:, cols], keys[:, cols], (((1,), (1,)), ((), ())), preferred_element_type=F32
+        )
+        decay = jnp.where(allowed, jnp.exp(-rates_ref[h] * lag), 0.0)
+        out[:, cols] = dot((scores * decay).astype(BF), values[:, cols])
+
+
+def attention_kernel(rates_ref, queries, inside, same, carried, out):
+    block_len = queries.shape[0]
+    heads, size, _ = carried.shape
+    index = lax.broadcasted_iota(jnp.int32, (block_len, size), 0).astype(F32)
+    for h in range(heads):
+        cols = slice(h * size, (h + 1) * size)
+        scale = jnp.exp(-rates_ref[h] * index) * same[...]
+        raw = inside[:, cols] + dot(queries[:, cols], carried[h]) * scale
+        mean = jnp.mean(raw * raw, axis=-1, keepdims=True)
+        out[:, cols] = (raw * lax.rsqrt(mean + EPSILON)).astype(BF)
 
 
 def together(values):
@@ -270,6 +307,21 @@
     take_first = (middle - 1 >= middle_start).astype(F32)
     take_carried = jnp.where(chip_base - 1 >= middle_start, block_decay, 0.0)
     carried_second = take_first * first_state + take_carried[:, None, None] * carried_first
+    inside, same = pl.pallas_call(
+        inside_kernel,
+        out_shape=(
+            jax.ShapeDtypeStruct(queries.shape, F32),
+            jax.ShapeDtypeStruct((block_len, head_size), F32),
+        ),
+        in_specs=[smem] * 3 + [VMEM] * 3,
+        out_specs=(VMEM, VMEM),
+        cost_estimate=pl.CostEstimate(
+            flops=4 * block_len * block_len * queries.shape[1],
+            bytes_accessed=10 * block_len * queries.shape[1],
+            transcendentals=head_count * block_len * block_len,
+        ),
+    )(block_base.reshape(1), doc_lengths, rates, queries, keys, values)
+    carried_first, inside = lax.optimization_barrier((carried_first, inside))
     carried_first = carried_first.astype(BF)
     carried_second = carried_second.astype(BF)
     carried_mine = jnp.where(core == 0, carried_first, carried_second)
@@ -284,31 +336,13 @@
         axis=0,
     )
 
-    scores = jnp.einsum("thd,uhd->htu", query_heads, key_heads, preferred_element_type=F32)
-    lag_steps = local_index[:, None] - local_index[None, :]
-    allowed = (lag_steps >= 0) & (doc_of[:, None] == doc_of[None, :])
-    decay_mask = jnp.where(
-        allowed[None],
-        jnp.exp(-rates[:, None, None] * jnp.maximum(lag_steps, 0).astype(F32)[None]),
-        0.0,
-    )
-    scaled_scores = (scores * decay_mask).astype(BF)
-    inside_term = jnp.einsum(
-        "htu,uhd->thd", scaled_scores, value_heads, preferred_element_type=F32
-    )
-    carried_term = jnp.einsum(
-        "thd,hde->the", query_heads, carried_rounded, preferred_element_type=F32
-    )
-    carry_scale = (
-        jnp.exp(-rates[None, :] * local_index.astype(F32)[:, None])
-        * (doc_of == doc_of[0]).astype(F32)[:, None]
-    )
-    heads_raw = inside_term + carried_term * carry_scale[:, :, None]
-    attention = (
-        (heads_raw * lax.rsqrt(jnp.mean(heads_raw * heads_raw, axis=-1, keepdims=True) + EPSILON))
-        .astype(BF)
-        .reshape(block_len, head_count * head_size)
-    )
+    attention = pl.pallas_call(
+        attention_kernel,
+        out_shape=jax.ShapeDtypeStruct(queries.shape, BF),
+        in_specs=[smem] + [VMEM] * 4,
+        out_specs=VMEM,
+    )(rates, queries, inside, same, carried_rounded)
+
     expert_ids = jnp.arange(experts, dtype=jnp.int32)
     chosen = routes[:, :, None] == expert_ids[None, None, :]
     onehot = jnp.sum(chosen.astype(jnp.int32), axis=1)

time: 215 us -> 214 us (level)
  Pallas kernels: 25 us -> 31.3 us
  waiting for transfers between devices: 86.3 us -> 83.8 us
    pallas_call x0 -> x2, Pallas kernels: none -> 6.3 us  [the longest x1 3.46 us: body(): pl.pallas_call(inside_kernel, out_shape=(jax.ShapeDtypeStruct(queries.sha...]
    ppermute x3, waiting for transfers between devices: 5.62 us -> 2.8 us  [body(): lax.ppermute(chip_state, 'seq', xor_pairs(seq_count, 2 * step))]
    dot_general x2 -> x0, matrix products: 2.29 us -> none  [the longest x1 1.94 us: body(): jnp.einsum('htu,uhd->thd', scaled_scores, value_heads, preferred_element_...]
  transfers between devices with their start and end apart: 46 -> 46, of which waited for: 22 -> 22; matrix products, arithmetic and copies ran while one was open for 9% -> 8% of each run, Pallas kernels for 7% -> 9%
where the time goes in v5:
time: 214 us
  waiting for transfers between devices  83.8 us (39%)
  starting transfers between devices  63.7 us (30%)
  Pallas kernels  31.3 us (15%)
  matrix products  13.5 us (6%)
  other arithmetic  13.3 us (6%)
  between operations  4.64 us (2%)
  local copies, waits for them, and re-layouts  3.3 us (2%)
    ppermute x5, waiting for transfers between devices, body(): lax.ppermute(load, 'exp', (ins if has_in else []) + (outs if has_out else...  26.7 us
    ppermute x9, waiting for transfers between devices, body(): done['group', g] = lax.ppermute(block, 'seq', xor_pairs(seq_count, 2 * g))  25.3 us
    ppermute x5, starting transfers between devices, body(): lax.ppermute(load, 'exp', (ins if has_in else []) + (outs if has_out else...  17.7 us
    ppermute x9, waiting for transfers between devices, body(): done['table', g] = lax.ppermute(block, 'seq', xor_pairs(seq_count, 2 * g))  16.8 us
    ppermute x9, starting transfers between devices, body(): done['own', step] = lax.ppermute(block, 'exp', xor_pairs(exp_count, step))  15.4 us
    pallas_call x2, Pallas kernels, expert_last(): pl.pallas_call(functools.partial(expert_kernel, width), out_shape=tuple((...  13.9 us
    ppermute x9, starting transfers between devices, body(): done['table', g] = lax.ppermute(block, 'seq', xor_pairs(seq_count, 2 * g))  12 us
    ppermute x9, waiting for transfers between devices, body(): done['own', step] = lax.ppermute(block, 'exp', xor_pairs(exp_count, step))  10.8 us
  transfers between devices with their start and end apart: 46, of which 22 were waited for; matrix products, arithmetic and copies ran while one was open for 8% of the time, Pallas kernels for 9%

profile of v5, /device:TPU:0, one launch (start us, length us, event | category | flops | bytes accessed | tf_op | source)
XLA Modules:
  0.0 213.6 jit_solution(9932616408726937193)
XLA Ops:
  0.0 2.6 %shard_map.118 = bf16[8,128,128]{2,1,0:T(8,128)(2,1)} custom-call(s32[1]{0:T(128)} %bitcast.1.place_ref, s32[16]{0:T(128)} %lengths_ref.3, f32[8]{0:T(128)} %rates_ref.5, bf16[256,1024]{1,0:T(8,128)(2,1)} %keys.3, bf16[256,1024]{1,0:T(8,128)(2,1)} %values.3), custom_call_target="tpu_custom_call" | custom-call | tf_op jit(solution)/shard_map/pallas_call | solution.py:271
  7.4 1.0 fusion.40
  8.4 2.6 %collective-permute-start.1 = (bf16[4,128,128]{2,1,0:T(8,128)(2,1)S(1)}, bf16[4,128,128]{2,1,0:T(8,128)(2,1)S(1)}, u32[]{:S(2)}, u32[]{:S(2)}) collective-permute-start(bf16[4,128,128]{2,1,0:T(8,128)(2,1)S(1)} %fusion.40), channel_id=1, source_target_pairs={{0,8},{4,12},{8,0},{12,4},{16,24},{20,28},{24,16},{28,20},{1,9},{5... | collective-permute-start | bytes 393224 | tf_op jit(solution)/shard_map/ppermute | solution.py:298
  11.0 1.5 collective-permute-start.2
  13.2 3.5 %shard_map.119 = (f32[256,1024]{1,0:T(8,128)}, f32[256,128]{1,0:T(8,128)}) custom-call(s32[1]{0:T(128)} %bitcast.1.place_ref, s32[16]{0:T(128)} %lengths_ref.3, f32[8]{0:T(128)} %rates_ref.5, bf16[256,1024]{1,0:T(8,128)(2,1)} %queries.3, bf16[256,1024]{1,0:T(8,128)(2,1)} %keys.3, bf16[256,1024]{1,0:T(8,128)(2,1)} %values.3), custom_call_target="tpu_custom_call" | custom-call | flops 268435456 | bytes 2621440 | tf_op jit(solution)/shard_map/pallas_call | solution.py:310
  16.6 2.8 %collective-permute-done.2 = bf16[4,128,128]{2,1,0:T(8,128)(2,1)S(1)} collective-permute-done((bf16[4,128,128]{2,1,0:T(8,128)(2,1)S(1)}, bf16[4,128,128]{2,1,0:T(8,128)(2,1)S(1)}, u32[]{:S(2)}, u32[]{:S(2)}) %collective-permute-start.2) | collective-permute-done | bytes 131104 | tf_op jit(solution)/shard_map/ppermute | solution.py:298
  19.8 1.3 collective-permute-done.4
  21.9 2.8 %shard_map.120 = bf16[256,1024]{1,0:T(8,128)(2,1)} custom-call(f32[8]{0:T(128)} %rates_ref.5, bf16[256,1024]{1,0:T(8,128)(2,1)} %queries.3, f32[256,1024]{1,0:T(8,128)} %get-tuple-element.75.inside, f32[256,128]{1,0:T(8,128)} %get-tuple-element.76.same, bf16[8,128,128]{2,1,0:T(8,128)(2,1)} %pad_maximum_fusion.5.carried), custom_call_target="tpu_custom_call" | custom-call | tf_op jit(solution)/shard_map/pallas_call | solution.py:339
  24.7 2.5 %fusion.12 = bf16[256,1024]{1,0:T(8,128)(2,1)S(1)} fusion(bf16[256,1024]{1,0:T(8,128)(2,1)} %shard_map.120, bf16[1024,3072]{1,0:T(8,128)(2,1)} %param.18), kind=kOutput, calls=%fused_computation.26 | convolution fusion | flops 537133056 | bytes 3145728 | tf_op jit(solution)/shard_map/dot_general | solution.py:371
  27.3 3.5 %collective-permute-start.5 = (bf16[256,1024]{1,0:T(8,128)(2,1)S(1)}, bf16[256,1024]{1,0:T(8,128)(2,1)S(1)}, u32[]{:S(2)}, u32[]{:S(2)}) collective-permute-start(bf16[256,1024]{1,0:T(8,128)(2,1)S(1)} %fusion.12), channel_id=1, source_target_pairs={{0,1},{3,2},{4,5},{7,6},{8,9},{11,10},{12,13},{15,14},{16,17},{19,... | collective-permute-start | bytes 1572872 | tf_op jit(solution)/shard_map/ppermute | solution.py:389
  30.8 2.3 %fusion.15 = bf16[256,1024]{1,0:T(8,128)(2,1)S(1)} fusion(bf16[256,1024]{1,0:T(8,128)(2,1)S(1)} %copy-done.10, bf16[1024,3072]{1,0:T(8,128)(2,1)} %param.18), kind=kOutput, calls=%fused_computation.27 | convolution fusion | flops 537133056 | bytes 3145728 | tf_op jit(solution)/shard_map/dot_general | solution.py:371
  33.2 9.1 %collective-permute-done.5 = bf16[256,1024]{1,0:T(8,128)(2,1)S(1)} collective-permute-done((bf16[256,1024]{1,0:T(8,128)(2,1)S(1)}, bf16[256,1024]{1,0:T(8,128)(2,1)S(1)}, u32[]{:S(2)}, u32[]{:S(2)}) %collective-permute-start.5) | collective-permute-done | bytes 524320 | tf_op jit(solution)/shard_map/ppermute | solution.py:389
  43.1 7.2 %collective-permute-start.6 = (bf16[256,1024]{1,0:T(8,128)(2,1)S(1)}, bf16[256,1024]{1,0:T(8,128)(2,1)S(1)}, u32[]{:S(2)}, u32[]{:S(2)}) collective-permute-start(bf16[256,1024]{1,0:T(8,128)(2,1)S(1)} %fusion.15), channel_id=1, source_target_pairs={{0,1},{3,2},{4,5},{7,6},{8,9},{11,10},{12,13},{15,14},{16,17},{19,... | collective-permute-start | bytes 1572872 | tf_op jit(solution)/shard_map/ppermute | solution.py:389
  50.5 2.4 %fusion.18 = bf16[256,1024]{1,0:T(8,128)(2,1)S(1)} fusion(bf16[256,1024]{1,0:T(8,128)(2,1)S(1)} %copy-done.10, bf16[1024,3072]{1,0:T(8,128)(2,1)} %param.18), kind=kOutput, calls=%fused_computation.28 | convolution fusion | flops 537133056 | bytes 3145728 | tf_op jit(solution)/shard_map/dot_general | solution.py:371
  52.9 7.8 %collective-permute-done.6 = bf16[256,1024]{1,0:T(8,128)(2,1)S(1)} collective-permute-done((bf16[256,1024]{1,0:T(8,128)(2,1)S(1)}, bf16[256,1024]{1,0:T(8,128)(2,1)S(1)}, u32[]{:S(2)}, u32[]{:S(2)}) %collective-permute-start.6) | collective-permute-done | bytes 524320 | tf_op jit(solution)/shard_map/ppermute | solution.py:389
  62.0 4.2 %collective-permute-start.8 = (bf16[256,1024]{1,0:T(8,128)(2,1)S(1)}, bf16[256,1024]{1,0:T(8,128)(2,1)S(1)}, u32[]{:S(2)}, u32[]{:S(2)}) collective-permute-start(bf16[256,1024]{1,0:T(8,128)(2,1)S(1)} %broadcast_select_fusion.3), channel_id=1, source_target_pairs={{0,1},{3,2},{1,0},{2,3},{4,5},{7,6},{5,4},{6,7},{8,9},{11,10},{9,8... | collective-permute-start | bytes 1572872 | tf_op jit(solution)/shard_map/ppermute | solution.py:389
  66.2 9.9 %collective-permute-done.8 = bf16[256,1024]{1,0:T(8,128)(2,1)S(1)} collective-permute-done((bf16[256,1024]{1,0:T(8,128)(2,1)S(1)}, bf16[256,1024]{1,0:T(8,128)(2,1)S(1)}, u32[]{:S(2)}, u32[]{:S(2)}) %collective-permute-start.8) | collective-permute-done | bytes 524320 | tf_op jit(solution)/shard_map/ppermute | solution.py:389
  77.7 1.3 collective-permute-start.10
  79.7 1.3 collective-permute-start.12
  81.9 1.4 collective-permute-start.14
  83.3 5.3 %collective-permute-done.12 = bf16[136,1024]{1,0:T(8,128)(2,1)S(1)} collective-permute-done((bf16[136,1024]{1,0:T(8,128)(2,1)S(1)}, bf16[136,1024]{1,0:T(8,128)(2,1)S(1)}, u32[]{:S(2)}, u32[]{:S(2)}) %collective-permute-start.12) | collective-permute-done | bytes 278560 | tf_op jit(solution)/shard_map/ppermute | solution.py:403
  88.5 4.0 %collective-permute-done.13 = bf16[136,1024]{1,0:T(8,128)(2,1)S(1)} collective-permute-done((bf16[136,1024]{1,0:T(8,128)(2,1)S(1)}, bf16[136,1024]{1,0:T(8,128)(2,1)S(1)}, u32[]{:S(2)}, u32[]{:S(2)}) %collective-permute-start.13) | collective-permute-done | bytes 278560 | tf_op jit(solution)/shard_map/ppermute | solution.py:403
  93.1 1.5 collective-permute-start.15
  97.1 1.4 collective-permute-start.17
  98.4 1.3 collective-permute-start.18
  99.7 6.0 %collective-permute-done.16 = bf16[136,1024]{1,0:T(8,128)(2,1)S(1)} collective-permute-done((bf16[136,1024]{1,0:T(8,128)(2,1)S(1)}, bf16[136,1024]{1,0:T(8,128)(2,1)S(1)}, u32[]{:S(2)}, u32[]{:S(2)}) %collective-permute-start.16) | collective-permute-done | bytes 278560 | tf_op jit(solution)/shard_map/ppermute | solution.py:403
  105.7 5.1 %collective-permute-done.17 = bf16[136,1024]{1,0:T(8,128)(2,1)S(1)} collective-permute-done((bf16[136,1024]{1,0:T(8,128)(2,1)S(1)}, bf16[136,1024]{1,0:T(8,128)(2,1)S(1)}, u32[]{:S(2)}, u32[]{:S(2)}) %collective-permute-start.17) | collective-permute-done | bytes 278560 | tf_op jit(solution)/shard_map/ppermute | solution.py:403
  110.7 1.1 collective-permute-done.18
  112.9 1.2 collective-permute-start.20
  114.1 1.1 collective-permute-start.21
  115.2 1.2 collective-permute-start.22
  116.4 4.2 %shard_map.121 = (f32[544,640]{1,0:T(8,128)S(1)}, f32[544,640]{1,0:T(8,128)S(1)}, f32[544,128]{1,0:T(8,128)S(1)}) custom-call(bf16[544,1024]{1,0:T(8,128)(2,1)S(1)} %constant_dynamic-update-slice_fusion.refs_0_, bf16[544,1024]{1,0:T(8,128)(2,1)S(1)} %constant_dynamic-update-slice_fusion.4.refs_1_, bf16[1,3072,640]{2,1,0:T(8,128)(2,1)S(1)} %copy-done.1, ...), custom_call_target="tpu_custom_call" | custom-call | flops 2852126720 | bytes 10256384 | tf_op jit(solution)/shard_map/pallas_call | solution.py:118
  120.7 4.2 %shard_map.122 = (f32[544,640]{1,0:T(8,128)S(1)}, f32[544,640]{1,0:T(8,128)S(1)}, f32[544,128]{1,0:T(8,128)S(1)}) custom-call(bf16[544,1024]{1,0:T(8,128)(2,1)S(1)} %collective-permute-done.19.refs_0_, bf16[544,1024]{1,0:T(8,128)(2,1)S(1)} %collective-permute-done.23.refs_1_, bf16[1,3072,640]{2,1,0:T(8,128)(2,1)S(1)} %copy-done.1, ...), custom_call_target="tpu_custom_call" | custom-call | flops 2852126720 | bytes 10256384 | tf_op jit(solution)/shard_map/pallas_call | solution.py:118
  124.9 2.6 %collective-permute-done.21 = bf16[136,1024]{1,0:T(8,128)(2,1)S(1)} collective-permute-done((bf16[136,1024]{1,0:T(8,128)(2,1)S(1)}, bf16[136,1024]{1,0:T(8,128)(2,1)S(1)}, u32[]{:S(2)}, u32[]{:S(2)}) %collective-permute-start.21) | collective-permute-done | bytes 278560 | tf_op jit(solution)/shard_map/ppermute | solution.py:403
  127.5 1.3 collective-permute-done.22
  129.0 6.4 %shard_map.123 = (bf16[544,1024]{1,0:T(8,128)(2,1)S(1)}, bf16[544,1024]{1,0:T(8,128)(2,1)S(1)}, bf16[544,1024]{1,0:T(8,128)(2,1)S(1)}) custom-call(bf16[544,1024]{1,0:T(8,128)(2,1)S(1)} %constant_dynamic-update-slice_fusion.8.rows, f32[544,640]{1,0:T(8,128)S(1)} %get-tuple-element.107.gate_in, f32[544,640]{1,0:T(8,128)S(1)} %get-tuple-element.108.up_in, ...), custom_call_target="tpu_custom_call" | custom-call | flops 3565158400 | bytes 13795328 | tf_op jit(solution)/shard_map/pallas_call | solution.py:144
  135.4 7.5 %shard_map.124 = (bf16[544,1024]{1,0:T(8,128)(2,1)}, bf16[544,1024]{1,0:T(8,128)(2,1)}, bf16[544,1024]{1,0:T(8,128)(2,1)}) custom-call(bf16[544,1024]{1,0:T(8,128)(2,1)S(1)} %collective-permute-done.24.rows, f32[544,640]{1,0:T(8,128)S(1)} %get-tuple-element.115.gate_in, f32[544,640]{1,0:T(8,128)S(1)} %get-tuple-element.116.up_in, ...), custom_call_target="tpu_custom_call" | custom-call | flops 3565158400 | bytes 13795328 | tf_op jit(solution)/shard_map/pallas_call | solution.py:144
  143.5 1.7 multiply_reduce_fusion
  145.3 1.2 copy-done.4
  147.8 1.7 add_convert_fusion.2
  150.5 1.4 collective-permute-start.27
  151.9 1.3 collective-permute-start.28
  153.2 6.0 %collective-permute-done.26 = bf16[136,1024]{1,0:T(8,128)(2,1)S(1)} collective-permute-done((bf16[136,1024]{1,0:T(8,128)(2,1)S(1)}, bf16[136,1024]{1,0:T(8,128)(2,1)S(1)}, u32[]{:S(2)}, u32[]{:S(2)}) %collective-permute-start.26) | collective-permute-done | bytes 278560 | tf_op jit(solution)/shard_map/ppermute | solution.py:474
  159.2 4.5 %collective-permute-done.27 = bf16[136,1024]{1,0:T(8,128)(2,1)S(1)} collective-permute-done((bf16[136,1024]{1,0:T(8,128)(2,1)S(1)}, bf16[136,1024]{1,0:T(8,128)(2,1)S(1)}, u32[]{:S(2)}, u32[]{:S(2)}) %collective-permute-start.27) | collective-permute-done | bytes 278560 | tf_op jit(solution)/shard_map/ppermute | solution.py:474
  163.7 1.1 collective-permute-done.28
  166.1 2.4 %collective-permute-start.34 = (bf16[64,1024]{1,0:T(8,128)(2,1)S(1)}, bf16[64,1024]{1,0:T(8,128)(2,1)S(1)}, u32[]{:S(2)}, u32[]{:S(2)}) collective-permute-start(bf16[64,1024]{1,0:T(8,128)(2,1)S(1)} %get-tuple-element.187), channel_id=1, source_target_pairs={{0,3},{1,2},{2,1},{3,0},{4,7},{5,6},{6,5},{7,4},{8,11},{9,10},{10,... | collective-permute-start | bytes 393224 | tf_op jit(solution)/shard_map/ppermute | solution.py:479
  168.5 2.6 %add_convert_fusion = (bf16[544,1024]{1,0:T(8,128)(2,1)S(1)}, bf16[544,1024]{1,0:T(8,128)(2,1)S(1)}) fusion(bf16[544,1024]{1,0:T(8,128)(2,1)} %collective-permute-done.30, bf16[544,1024]{1,0:T(8,128)(2,1)S(1)} %get-tuple-element.132, bf16[544,1024]{1,0:T(8,128)(2,1)} %collective-permute-done.29, bf16[544,1024]{1,0:T(8,128)(2,1)S(1)} %get-tuple-element.124), kind=kLoop, calls=%fused_computation.1 | loop fusion | flops 4456448 | bytes 6684672 | tf_op jit(solution)/shard_map/convert_element_type | solution.py:488
  171.2 1.4 collective-permute-start.31
  173.3 1.4 collective-permute-start.33
  174.8 3.0 %collective-permute-start.35 = (bf16[64,1024]{1,0:T(8,128)(2,1)S(1)}, bf16[64,1024]{1,0:T(8,128)(2,1)S(1)}, u32[]{:S(2)}, u32[]{:S(2)}) collective-permute-start(bf16[64,1024]{1,0:T(8,128)(2,1)S(1)} %get-tuple-element.186), channel_id=1, source_target_pairs={{0,2},{1,3},{2,0},{3,1},{4,6},{5,7},{6,4},{7,5},{8,10},{9,11},{10,... | collective-permute-start | bytes 393224 | tf_op jit(solution)/shard_map/ppermute | solution.py:479
  177.9 2.9 %collective-permute-done.35 = bf16[64,1024]{1,0:T(8,128)(2,1)S(1)} collective-permute-done((bf16[64,1024]{1,0:T(8,128)(2,1)S(1)}, bf16[64,1024]{1,0:T(8,128)(2,1)S(1)}, u32[]{:S(2)}, u32[]{:S(2)}) %collective-permute-start.35) | collective-permute-done | bytes 131104 | tf_op jit(solution)/shard_map/ppermute | solution.py:479
  180.8 2.9 %collective-permute-start.37 = (bf16[136,1024]{1,0:T(8,128)(2,1)S(1)}, bf16[136,1024]{1,0:T(8,128)(2,1)S(1)}, u32[]{:S(2)}, u32[]{:S(2)}) collective-permute-start(bf16[136,1024]{1,0:T(8,128)(2,1)S(1)} %get-tuple-element.158), channel_id=1, source_target_pairs={{0,8},{4,12},{8,0},{12,4},{16,24},{20,28},{24,16},{28,20},{1,9},{5... | collective-permute-start | bytes 835592 | tf_op jit(solution)/shard_map/ppermute | solution.py:474
  184.3 1.4 collective-permute-start.39
  185.7 2.1 collective-permute-done.33
  189.1 1.4 collective-permute-start.40
  190.6 2.1 collective-permute-start.41
  192.9 2.0 collective-permute-start.42
  194.9 2.8 %collective-permute-done.38 = bf16[136,1024]{1,0:T(8,128)(2,1)S(1)} collective-permute-done((bf16[136,1024]{1,0:T(8,128)(2,1)S(1)}, bf16[136,1024]{1,0:T(8,128)(2,1)S(1)}, u32[]{:S(2)}, u32[]{:S(2)}) %collective-permute-start.38) | collective-permute-done | bytes 278560 | tf_op jit(solution)/shard_map/ppermute | solution.py:474
  197.7 2.1 collective-permute-done.41
  201.2 2.0 collective-permute-start.43
  203.1 2.5 %collective-permute-start.45 = (bf16[64,1024]{1,0:T(8,128)(2,1)S(1)}, bf16[64,1024]{1,0:T(8,128)(2,1)S(1)}, u32[]{:S(2)}, u32[]{:S(2)}) collective-permute-start(bf16[64,1024]{1,0:T(8,128)(2,1)S(1)} %get-tuple-element.179), channel_id=1, source_target_pairs={{0,1},{1,0},{2,3},{3,2},{4,5},{5,4},{6,7},{7,6},{8,9},{9,8},{10,11... | collective-permute-start | bytes 393224 | tf_op jit(solution)/shard_map/ppermute | solution.py:479
  205.6 2.6 %collective-permute-done.43 = bf16[64,1024]{1,0:T(8,128)(2,1)S(1)} collective-permute-done((bf16[64,1024]{1,0:T(8,128)(2,1)S(1)}, bf16[64,1024]{1,0:T(8,128)(2,1)S(1)}, u32[]{:S(2)}, u32[]{:S(2)}) %collective-permute-start.43) | collective-permute-done | bytes 131104 | tf_op jit(solution)/shard_map/ppermute | solution.py:479
  208.2 3.2 %collective-permute-done.44 = bf16[64,1024]{1,0:T(8,128)(2,1)S(1)} collective-permute-done((bf16[64,1024]{1,0:T(8,128)(2,1)S(1)}, bf16[64,1024]{1,0:T(8,128)(2,1)S(1)}, u32[]{:S(2)}, u32[]{:S(2)}) %collective-permute-start.44) | collective-permute-done | bytes 131104 | tf_op jit(solution)/shard_map/ppermute | solution.py:479
  211.4 1.4 add_convert_fusion.11
  (132 shorter events, 21.5 us)
Async XLA Ops:
  0.0 146.4 %copy-start = (bf16[3072,4]{0,1:T(4,128)(2,1)S(1)}, bf16[3072,4]{0,1:T(4,128)(2,1)}, u32[]{:S(2)}) copy-start(bf16[3072,4]{0,1:T(4,128)(2,1)} %param.19) | copy-start | bytes 73732
  0.0 3.1 %copy-start.12 = (s32[16]{0:T(128)S(1)}, s32[16]{0:T(128)}, u32[]{:S(2)}) copy-start(s32[16]{0:T(128)} %lengths_ref.3) | copy-start | bytes 196
  0.0 4.7 %copy-start.13 = (f32[8]{0:T(128)S(1)}, f32[8]{0:T(128)}, u32[]{:S(2)}) copy-start(f32[8]{0:T(128)} %rates_ref.5) | copy-start | bytes 100
  2.6 4.8 %collective-permute-start = (bf16[8,128,128]{2,1,0:T(8,128)(2,1)}, bf16[8,128,128]{2,1,0:T(8,128)(2,1)S(1)}, u32[]{:S(2)}, u32[]{:S(2)}) collective-permute-start(bf16[8,128,128]{2,1,0:T(8,128)(2,1)} %shard_map.118), channel_id=1, source_target_pairs={{0,4},{4,0},{8,12},{12,8},{16,20},{20,16},{24,28},{28,24},{1,5},{5... | collective-permute-start | bytes 786440 | tf_op jit(solution)/shard_map/ppermute | solution.py:280
  8.4 8.2 %collective-permute-start.1 = (bf16[4,128,128]{2,1,0:T(8,128)(2,1)S(1)}, bf16[4,128,128]{2,1,0:T(8,128)(2,1)S(1)}, u32[]{:S(2)}, u32[]{:S(2)}) collective-permute-start(bf16[4,128,128]{2,1,0:T(8,128)(2,1)S(1)} %fusion.40), channel_id=1, source_target_pairs={{0,8},{4,12},{8,0},{12,4},{16,24},{20,28},{24,16},{28,20},{1,9},{5... | collective-permute-start | bytes 393224 | tf_op jit(solution)/shard_map/ppermute | solution.py:298
  11.0 8.4 %collective-permute-start.2 = (bf16[4,128,128]{2,1,0:T(8,128)(2,1)S(1)}, bf16[4,128,128]{2,1,0:T(8,128)(2,1)S(1)}, u32[]{:S(2)}, u32[]{:S(2)}) collective-permute-start(bf16[4,128,128]{2,1,0:T(8,128)(2,1)S(1)} %fusion.40), channel_id=1, source_target_pairs={{0,16},{4,20},{8,24},{12,28},{16,0},{20,4},{24,8},{28,12},{1,17},{... | collective-permute-start | bytes 393224 | tf_op jit(solution)/shard_map/ppermute | solution.py:298
  12.5 6.9 %collective-permute-start.3 = (bf16[4,128,128]{2,1,0:T(8,128)(2,1)S(1)}, bf16[4,128,128]{2,1,0:T(8,128)(2,1)S(1)}, u32[]{:S(2)}, u32[]{:S(2)}) collective-permute-start(bf16[4,128,128]{2,1,0:T(8,128)(2,1)S(1)} %fusion.40), channel_id=1, source_target_pairs={{0,24},{4,28},{8,16},{12,20},{16,8},{20,12},{24,0},{28,4},{1,25},{... | collective-permute-start | bytes 393224 | tf_op jit(solution)/shard_map/ppermute | solution.py:298
  13.2 6.4 %copy-start.9 = (bf16[8,128,128]{2,1,0:T(8,128)(2,1)S(1)}, bf16[8,128,128]{2,1,0:T(8,128)(2,1)}, u32[]{:S(2)}) copy-start(bf16[8,128,128]{2,1,0:T(8,128)(2,1)} %shard_map.118) | copy-start | bytes 786436
  19.7 1.4 collective-permute-start.4
  24.7 6.1 %copy-start.11 = (s32[256,2]{0,1:T(2,128)S(1)}, s32[256,2]{0,1:T(2,128)}, u32[]{:S(2)}) copy-start(s32[256,2]{0,1:T(2,128)} %param.23) | copy-start | bytes 6148
  24.7 6.1 %copy-start.10 = (bf16[256,1024]{1,0:T(8,128)(2,1)S(1)}, bf16[256,1024]{1,0:T(8,128)(2,1)}, u32[]{:S(2)}) copy-start(bf16[256,1024]{1,0:T(8,128)(2,1)} %shard_map.120) | copy-start | bytes 1572868
  27.3 15.0 %collective-permute-start.5 = (bf16[256,1024]{1,0:T(8,128)(2,1)S(1)}, bf16[256,1024]{1,0:T(8,128)(2,1)S(1)}, u32[]{:S(2)}, u32[]{:S(2)}) collective-permute-start(bf16[256,1024]{1,0:T(8,128)(2,1)S(1)} %fusion.12), channel_id=1, source_target_pairs={{0,1},{3,2},{4,5},{7,6},{8,9},{11,10},{12,13},{15,14},{16,17},{19,... | collective-permute-start | bytes 1572872 | tf_op jit(solution)/shard_map/ppermute | solution.py:389
  42.4 10.5 %collective-permute-start.7 = (bf16[256,1024]{1,0:T(8,128)(2,1)S(1)}, bf16[256,1024]{1,0:T(8,128)(2,1)S(1)}, u32[]{:S(2)}, u32[]{:S(2)}) collective-permute-start(bf16[256,1024]{1,0:T(8,128)(2,1)S(1)} %add_convert_fusion.8), channel_id=1, source_target_pairs={{1,2},{2,1},{5,6},{6,5},{9,10},{10,9},{13,14},{14,13},{17,18},{18,... | collective-permute-start | bytes 1572872 | tf_op jit(solution)/shard_map/ppermute | solution.py:394
  43.1 17.6 %collective-permute-start.6 = (bf16[256,1024]{1,0:T(8,128)(2,1)S(1)}, bf16[256,1024]{1,0:T(8,128)(2,1)S(1)}, u32[]{:S(2)}, u32[]{:S(2)}) collective-permute-start(bf16[256,1024]{1,0:T(8,128)(2,1)S(1)} %fusion.15), channel_id=1, source_target_pairs={{0,1},{3,2},{4,5},{7,6},{8,9},{11,10},{12,13},{15,14},{16,17},{19,... | collective-permute-start | bytes 1572872 | tf_op jit(solution)/shard_map/ppermute | solution.py:389
  52.9 8.7 %copy-start.5 = (bf16[256,3072]{1,0:T(8,128)(2,1)S(1)}, bf16[256,3072]{1,0:T(8,128)(2,1)}, u32[]{:S(2)}) copy-start(bf16[256,3072]{1,0:T(8,128)(2,1)} %param.12) | copy-start | bytes 4718596
  60.9 5.3 %collective-permute-start.9 = (bf16[256,1024]{1,0:T(8,128)(2,1)S(1)}, bf16[256,1024]{1,0:T(8,128)(2,1)S(1)}, u32[]{:S(2)}, u32[]{:S(2)}) collective-permute-start(bf16[256,1024]{1,0:T(8,128)(2,1)S(1)} %add_convert_fusion.6), channel_id=1, source_target_pairs={{1,2},{2,1},{5,6},{6,5},{9,10},{10,9},{13,14},{14,13},{17,18},{18,... | collective-permute-start | bytes 1572872 | tf_op jit(solution)/shard_map/ppermute | solution.py:394
  62.0 14.1 %collective-permute-start.8 = (bf16[256,1024]{1,0:T(8,128)(2,1)S(1)}, bf16[256,1024]{1,0:T(8,128)(2,1)S(1)}, u32[]{:S(2)}, u32[]{:S(2)}) collective-permute-start(bf16[256,1024]{1,0:T(8,128)(2,1)S(1)} %broadcast_select_fusion.3), channel_id=1, source_target_pairs={{0,1},{3,2},{1,0},{2,3},{4,5},{7,6},{5,4},{6,7},{8,9},{11,10},{9,8... | collective-permute-start | bytes 1572872 | tf_op jit(solution)/shard_map/ppermute | solution.py:389
  76.5 2.5 %copy-start.8 = (bf16[256,1024]{1,0:T(8,128)(2,1)}, bf16[256,1024]{1,0:T(8,128)(2,1)S(1)}, u32[]{:S(2)}) copy-start(bf16[256,1024]{1,0:T(8,128)(2,1)S(1)} %broadcast_select_fusion.2) | copy-start | bytes 1572868
  76.7 15.9 %collective-permute-start.11 = (bf16[256,1024]{1,0:T(8,128)(2,1)S(1)}, bf16[256,1024]{1,0:T(8,128)(2,1)S(1)}, u32[]{:S(2)}, u32[]{:S(2)}) collective-permute-start(bf16[256,1024]{1,0:T(8,128)(2,1)S(1)} %add_convert_fusion.4), channel_id=1, source_target_pairs={{1,2},{2,1},{5,6},{6,5},{9,10},{10,9},{13,14},{14,13},{17,18},{18,... | collective-permute-start | bytes 1572872 | tf_op jit(solution)/shard_map/ppermute | solution.py:394
  77.7 14.9 %collective-permute-start.10 = (bf16[256,1024]{1,0:T(8,128)(2,1)S(1)}, bf16[256,1024]{1,0:T(8,128)(2,1)S(1)}, u32[]{:S(2)}, u32[]{:S(2)}) collective-permute-start(bf16[256,1024]{1,0:T(8,128)(2,1)S(1)} %add_convert_fusion.5), channel_id=1, source_target_pairs={{1,0},{2,3},{5,4},{6,7},{9,8},{10,11},{13,12},{14,15},{17,16},{18,... | collective-permute-start | bytes 1572872 | tf_op jit(solution)/shard_map/ppermute | solution.py:389
  79.7 8.8 %collective-permute-start.12 = (bf16[136,1024]{1,0:T(8,128)(2,1)S(1)}, bf16[136,1024]{1,0:T(8,128)(2,1)S(1)}, u32[]{:S(2)}, u32[]{:S(2)}) collective-permute-start(bf16[136,1024]{1,0:T(8,128)(2,1)S(1)} %get-tuple-element.177), channel_id=1, source_target_pairs={{0,8},{4,12},{8,0},{12,4},{16,24},{20,28},{24,16},{28,20},{1,9},{5... | collective-permute-start | bytes 835592 | tf_op jit(solution)/shard_map/ppermute | solution.py:403
  81.0 11.6 %collective-permute-start.13 = (bf16[136,1024]{1,0:T(8,128)(2,1)S(1)}, bf16[136,1024]{1,0:T(8,128)(2,1)S(1)}, u32[]{:S(2)}, u32[]{:S(2)}) collective-permute-start(bf16[136,1024]{1,0:T(8,128)(2,1)S(1)} %get-tuple-element.176), channel_id=1, source_target_pairs={{0,16},{4,20},{8,24},{12,28},{16,0},{20,4},{24,8},{28,12},{1,17},{... | collective-permute-start | bytes 835592 | tf_op jit(solution)/shard_map/ppermute | solution.py:403
  81.9 10.7 %collective-permute-start.14 = (bf16[136,1024]{1,0:T(8,128)(2,1)S(1)}, bf16[136,1024]{1,0:T(8,128)(2,1)S(1)}, u32[]{:S(2)}, u32[]{:S(2)}) collective-permute-start(bf16[136,1024]{1,0:T(8,128)(2,1)S(1)} %get-tuple-element.175), channel_id=1, source_target_pairs={{0,24},{4,28},{8,16},{12,20},{16,8},{20,12},{24,0},{28,4},{1,25},{... | collective-permute-start | bytes 835592 | tf_op jit(solution)/shard_map/ppermute | solution.py:403
  92.7 19.1 %collective-permute-start.19 = (bf16[544,1024]{1,0:T(8,128)(2,1)S(1)}, bf16[544,1024]{1,0:T(8,128)(2,1)S(1)}, u32[]{:S(2)}, u32[]{:S(2)}) collective-permute-start(bf16[544,1024]{1,0:T(8,128)(2,1)S(1)} %constant_dynamic-update-slice_fusion.refs_0_), channel_id=1, source_target_pairs={{0,4},{4,0},{8,12},{12,8},{16,20},{20,16},{24,28},{28,24},{1,5},{5... | collective-permute-start | bytes 3342344 | tf_op jit(solution)/shard_map/ppermute | solution.py:406
  93.1 18.8 %collective-permute-start.15 = (bf16[256,1024]{1,0:T(8,128)(2,1)S(1)}, bf16[256,1024]{1,0:T(8,128)(2,1)S(1)}, u32[]{:S(2)}, u32[]{:S(2)}) collective-permute-start(bf16[256,1024]{1,0:T(8,128)(2,1)S(1)} %add_convert_fusion.3), channel_id=1, source_target_pairs={{1,0},{2,3},{5,4},{6,7},{9,8},{10,11},{13,12},{14,15},{17,16},{18,... | collective-permute-start | bytes 1572872 | tf_op jit(solution)/shard_map/ppermute | solution.py:389
  94.6 0.8 copy-start.6
  96.1 20.3 %copy-start.2 = (bf16[1,3072,640]{2,1,0:T(8,128)(2,1)S(1)}, bf16[1,3072,640]{2,1,0:T(8,128)(2,1)}, u32[]{:S(2)}) copy-start(bf16[1,3072,640]{2,1,0:T(8,128)(2,1)} %up_hbm.3) | copy-start | bytes 11796484
  96.2 9.5 %collective-permute-start.16 = (bf16[136,1024]{1,0:T(8,128)(2,1)S(1)}, bf16[136,1024]{1,0:T(8,128)(2,1)S(1)}, u32[]{:S(2)}, u32[]{:S(2)}) collective-permute-start(bf16[136,1024]{1,0:T(8,128)(2,1)S(1)} %get-tuple-element.173), channel_id=1, source_target_pairs={{0,8},{4,12},{8,0},{12,4},{16,24},{20,28},{24,16},{28,20},{1,9},{5... | collective-permute-start | bytes 835592 | tf_op jit(solution)/shard_map/ppermute | solution.py:403
  97.1 13.7 %collective-permute-start.17 = (bf16[136,1024]{1,0:T(8,128)(2,1)S(1)}, bf16[136,1024]{1,0:T(8,128)(2,1)S(1)}, u32[]{:S(2)}, u32[]{:S(2)}) collective-permute-start(bf16[136,1024]{1,0:T(8,128)(2,1)S(1)} %get-tuple-element.172), channel_id=1, source_target_pairs={{0,16},{4,20},{8,24},{12,28},{16,0},{20,4},{24,8},{28,12},{1,17},{... | collective-permute-start | bytes 835592 | tf_op jit(solution)/shard_map/ppermute | solution.py:403
  98.4 13.4 %collective-permute-start.18 = (bf16[136,1024]{1,0:T(8,128)(2,1)S(1)}, bf16[136,1024]{1,0:T(8,128)(2,1)S(1)}, u32[]{:S(2)}, u32[]{:S(2)}) collective-permute-start(bf16[136,1024]{1,0:T(8,128)(2,1)S(1)} %get-tuple-element.171), channel_id=1, source_target_pairs={{0,24},{4,28},{8,16},{12,20},{16,8},{20,12},{24,0},{28,4},{1,25},{... | collective-permute-start | bytes 835592 | tf_op jit(solution)/shard_map/ppermute | solution.py:403
  111.9 8.7 %collective-permute-start.23 = (bf16[544,1024]{1,0:T(8,128)(2,1)S(1)}, bf16[544,1024]{1,0:T(8,128)(2,1)S(1)}, u32[]{:S(2)}, u32[]{:S(2)}) collective-permute-start(bf16[544,1024]{1,0:T(8,128)(2,1)S(1)} %constant_dynamic-update-slice_fusion.4.refs_1_), channel_id=1, source_target_pairs={{0,4},{4,0},{8,12},{12,8},{16,20},{20,16},{24,28},{28,24},{1,5},{5... | collective-permute-start | bytes 3342344 | tf_op jit(solution)/shard_map/ppermute | solution.py:406
  112.1 0.8 copy-start.7
  112.1 4.3 %copy-start.1 = (bf16[1,3072,640]{2,1,0:T(8,128)(2,1)S(1)}, bf16[1,3072,640]{2,1,0:T(8,128)(2,1)}, u32[]{:S(2)}) copy-start(bf16[1,3072,640]{2,1,0:T(8,128)(2,1)} %gate_hbm.3) | copy-start | bytes 11796484
  112.9 12.0 %collective-permute-start.20 = (bf16[136,1024]{1,0:T(8,128)(2,1)S(1)}, bf16[136,1024]{1,0:T(8,128)(2,1)S(1)}, u32[]{:S(2)}, u32[]{:S(2)}) collective-permute-start(bf16[136,1024]{1,0:T(8,128)(2,1)S(1)} %get-tuple-element.169), channel_id=1, source_target_pairs={{0,8},{4,12},{8,0},{12,4},{16,24},{20,28},{24,16},{28,20},{1,9},{5... | collective-permute-start | bytes 835592 | tf_op jit(solution)/shard_map/ppermute | solution.py:403
  114.1 13.4 %collective-permute-start.21 = (bf16[136,1024]{1,0:T(8,128)(2,1)S(1)}, bf16[136,1024]{1,0:T(8,128)(2,1)S(1)}, u32[]{:S(2)}, u32[]{:S(2)}) collective-permute-start(bf16[136,1024]{1,0:T(8,128)(2,1)S(1)} %get-tuple-element.168), channel_id=1, source_target_pairs={{0,16},{4,20},{8,24},{12,28},{16,0},{20,4},{24,8},{28,12},{1,17},{... | collective-permute-start | bytes 835592 | tf_op jit(solution)/shard_map/ppermute | solution.py:403
  115.2 13.6 %collective-permute-start.22 = (bf16[136,1024]{1,0:T(8,128)(2,1)S(1)}, bf16[136,1024]{1,0:T(8,128)(2,1)S(1)}, u32[]{:S(2)}, u32[]{:S(2)}) collective-permute-start(bf16[136,1024]{1,0:T(8,128)(2,1)S(1)} %get-tuple-element.167), channel_id=1, source_target_pairs={{0,24},{4,28},{8,16},{12,20},{16,8},{20,12},{24,0},{28,4},{1,25},{... | collective-permute-start | bytes 835592 | tf_op jit(solution)/shard_map/ppermute | solution.py:403
  120.6 8.4 %copy-start.3 = (bf16[1,640,3072]{2,1,0:T(8,128)(2,1)S(1)}, bf16[1,640,3072]{2,1,0:T(8,128)(2,1)}, u32[]{:S(2)}) copy-start(bf16[1,640,3072]{2,1,0:T(8,128)(2,1)} %down_hbm.3) | copy-start | bytes 11796484
  128.9 6.5 %collective-permute-start.24 = (bf16[544,1024]{1,0:T(8,128)(2,1)S(1)}, bf16[544,1024]{1,0:T(8,128)(2,1)S(1)}, u32[]{:S(2)}, u32[]{:S(2)}) collective-permute-start(bf16[544,1024]{1,0:T(8,128)(2,1)S(1)} %constant_dynamic-update-slice_fusion.8.rows), channel_id=1, source_target_pairs={{0,4},{4,0},{8,12},{12,8},{16,20},{20,16},{24,28},{28,24},{1,5},{5... | collective-permute-start | bytes 3342344 | tf_op jit(solution)/shard_map/ppermute | solution.py:406
  143.0 4.8 %collective-permute-start.25 = (bf16[544,1024]{1,0:T(8,128)(2,1)}, bf16[544,1024]{1,0:T(8,128)(2,1)}, u32[]{:S(2)}, u32[]{:S(2)}) collective-permute-start(bf16[544,1024]{1,0:T(8,128)(2,1)} %get-tuple-element.118), channel_id=1, source_target_pairs={{0,4},{4,0},{8,12},{12,8},{16,20},{20,16},{24,28},{28,24},{1,5},{5... | collective-permute-start | bytes 3342344 | tf_op jit(solution)/shard_map/ppermute | solution.py:482
  145.3 1.2 copy-start.4
  146.9 6.2 %collective-permute-start.29 = (bf16[544,1024]{1,0:T(8,128)(2,1)}, bf16[544,1024]{1,0:T(8,128)(2,1)}, u32[]{:S(2)}, u32[]{:S(2)}) collective-permute-start(bf16[544,1024]{1,0:T(8,128)(2,1)} %get-tuple-element.119), channel_id=1, source_target_pairs={{0,4},{4,0},{8,12},{12,8},{16,20},{20,16},{24,28},{28,24},{1,5},{5... | collective-permute-start | bytes 3342344 | tf_op jit(solution)/shard_map/ppermute | solution.py:482
  147.0 6.2 %collective-permute-start.30 = (bf16[544,1024]{1,0:T(8,128)(2,1)}, bf16[544,1024]{1,0:T(8,128)(2,1)}, u32[]{:S(2)}, u32[]{:S(2)}) collective-permute-start(bf16[544,1024]{1,0:T(8,128)(2,1)} %get-tuple-element.120), channel_id=1, source_target_pairs={{0,4},{4,0},{8,12},{12,8},{16,20},{20,16},{24,28},{28,24},{1,5},{5... | collective-permute-start | bytes 3342344 | tf_op jit(solution)/shard_map/ppermute | solution.py:482
  149.6 9.6 %collective-permute-start.26 = (bf16[136,1024]{1,0:T(8,128)(2,1)S(1)}, bf16[136,1024]{1,0:T(8,128)(2,1)S(1)}, u32[]{:S(2)}, u32[]{:S(2)}) collective-permute-start(bf16[136,1024]{1,0:T(8,128)(2,1)S(1)} %get-tuple-element.166), channel_id=1, source_target_pairs={{0,8},{4,12},{8,0},{12,4},{16,24},{20,28},{24,16},{28,20},{1,9},{5... | collective-permute-start | bytes 835592 | tf_op jit(solution)/shard_map/ppermute | solution.py:474
  150.5 13.2 %collective-permute-start.27 = (bf16[136,1024]{1,0:T(8,128)(2,1)S(1)}, bf16[136,1024]{1,0:T(8,128)(2,1)S(1)}, u32[]{:S(2)}, u32[]{:S(2)}) collective-permute-start(bf16[136,1024]{1,0:T(8,128)(2,1)S(1)} %get-tuple-element.165), channel_id=1, source_target_pairs={{0,16},{4,20},{8,24},{12,28},{16,0},{20,4},{24,8},{28,12},{1,17},{... | collective-permute-start | bytes 835592 | tf_op jit(solution)/shard_map/ppermute | solution.py:474
  151.9 12.9 %collective-permute-start.28 = (bf16[136,1024]{1,0:T(8,128)(2,1)S(1)}, bf16[136,1024]{1,0:T(8,128)(2,1)S(1)}, u32[]{:S(2)}, u32[]{:S(2)}) collective-permute-start(bf16[136,1024]{1,0:T(8,128)(2,1)S(1)} %get-tuple-element.164), channel_id=1, source_target_pairs={{0,24},{4,28},{8,16},{12,20},{16,8},{20,12},{24,0},{28,4},{1,25},{... | collective-permute-start | bytes 835592 | tf_op jit(solution)/shard_map/ppermute | solution.py:474
  166.1 11.7 %collective-permute-start.34 = (bf16[64,1024]{1,0:T(8,128)(2,1)S(1)}, bf16[64,1024]{1,0:T(8,128)(2,1)S(1)}, u32[]{:S(2)}, u32[]{:S(2)}) collective-permute-start(bf16[64,1024]{1,0:T(8,128)(2,1)S(1)} %get-tuple-element.187), channel_id=1, source_target_pairs={{0,3},{1,2},{2,1},{3,0},{4,7},{5,6},{6,5},{7,4},{8,11},{9,10},{10,... | collective-permute-start | bytes 393224 | tf_op jit(solution)/shard_map/ppermute | solution.py:479
  171.2 13.1 %collective-permute-start.31 = (bf16[136,1024]{1,0:T(8,128)(2,1)S(1)}, bf16[136,1024]{1,0:T(8,128)(2,1)S(1)}, u32[]{:S(2)}, u32[]{:S(2)}) collective-permute-start(bf16[136,1024]{1,0:T(8,128)(2,1)S(1)} %get-tuple-element.162), channel_id=1, source_target_pairs={{0,8},{4,12},{8,0},{12,4},{16,24},{20,28},{24,16},{28,20},{1,9},{5... | collective-permute-start | bytes 835592 | tf_op jit(solution)/shard_map/ppermute | solution.py:474
  172.6 13.1 %collective-permute-start.32 = (bf16[136,1024]{1,0:T(8,128)(2,1)S(1)}, bf16[136,1024]{1,0:T(8,128)(2,1)S(1)}, u32[]{:S(2)}, u32[]{:S(2)}) collective-permute-start(bf16[136,1024]{1,0:T(8,128)(2,1)S(1)} %get-tuple-element.161), channel_id=1, source_target_pairs={{0,16},{4,20},{8,24},{12,28},{16,0},{20,4},{24,8},{28,12},{1,17},{... | collective-permute-start | bytes 835592 | tf_op jit(solution)/shard_map/ppermute | solution.py:474
  173.3 14.5 %collective-permute-start.33 = (bf16[136,1024]{1,0:T(8,128)(2,1)S(1)}, bf16[136,1024]{1,0:T(8,128)(2,1)S(1)}, u32[]{:S(2)}, u32[]{:S(2)}) collective-permute-start(bf16[136,1024]{1,0:T(8,128)(2,1)S(1)} %get-tuple-element.160), channel_id=1, source_target_pairs={{0,24},{4,28},{8,16},{12,20},{16,8},{20,12},{24,0},{28,4},{1,25},{... | collective-permute-start | bytes 835592 | tf_op jit(solution)/shard_map/ppermute | solution.py:474
  174.8 6.0 %collective-permute-start.35 = (bf16[64,1024]{1,0:T(8,128)(2,1)S(1)}, bf16[64,1024]{1,0:T(8,128)(2,1)S(1)}, u32[]{:S(2)}, u32[]{:S(2)}) collective-permute-start(bf16[64,1024]{1,0:T(8,128)(2,1)S(1)} %get-tuple-element.186), channel_id=1, source_target_pairs={{0,2},{1,3},{2,0},{3,1},{4,6},{5,7},{6,4},{7,5},{8,10},{9,11},{10,... | collective-permute-start | bytes 393224 | tf_op jit(solution)/shard_map/ppermute | solution.py:479
  177.8 5.9 %collective-permute-start.36 = (bf16[64,1024]{1,0:T(8,128)(2,1)S(1)}, bf16[64,1024]{1,0:T(8,128)(2,1)S(1)}, u32[]{:S(2)}, u32[]{:S(2)}) collective-permute-start(bf16[64,1024]{1,0:T(8,128)(2,1)S(1)} %get-tuple-element.185), channel_id=1, source_target_pairs={{0,1},{1,0},{2,3},{3,2},{4,5},{5,4},{6,7},{7,6},{8,9},{9,8},{10,11... | collective-permute-start | bytes 393224 | tf_op jit(solution)/shard_map/ppermute | solution.py:479
  180.8 12.0 %collective-permute-start.37 = (bf16[136,1024]{1,0:T(8,128)(2,1)S(1)}, bf16[136,1024]{1,0:T(8,128)(2,1)S(1)}, u32[]{:S(2)}, u32[]{:S(2)}) collective-permute-start(bf16[136,1024]{1,0:T(8,128)(2,1)S(1)} %get-tuple-element.158), channel_id=1, source_target_pairs={{0,8},{4,12},{8,0},{12,4},{16,24},{20,28},{24,16},{28,20},{1,9},{5... | collective-permute-start | bytes 835592 | tf_op jit(solution)/shard_map/ppermute | solution.py:474
  183.7 14.0 %collective-permute-start.38 = (bf16[136,1024]{1,0:T(8,128)(2,1)S(1)}, bf16[136,1024]{1,0:T(8,128)(2,1)S(1)}, u32[]{:S(2)}, u32[]{:S(2)}) collective-permute-start(bf16[136,1024]{1,0:T(8,128)(2,1)S(1)} %get-tuple-element.157), channel_id=1, source_target_pairs={{0,16},{4,20},{8,24},{12,28},{16,0},{20,4},{24,8},{28,12},{1,17},{... | collective-permute-start | bytes 835592 | tf_op jit(solution)/shard_map/ppermute | solution.py:474
  184.3 13.4 %collective-permute-start.39 = (bf16[136,1024]{1,0:T(8,128)(2,1)S(1)}, bf16[136,1024]{1,0:T(8,128)(2,1)S(1)}, u32[]{:S(2)}, u32[]{:S(2)}) collective-permute-start(bf16[136,1024]{1,0:T(8,128)(2,1)S(1)} %get-tuple-element.156), channel_id=1, source_target_pairs={{0,24},{4,28},{8,16},{12,20},{16,8},{20,12},{24,0},{28,4},{1,25},{... | collective-permute-start | bytes 835592 | tf_op jit(solution)/shard_map/ppermute | solution.py:474
  189.1 8.6 %collective-permute-start.40 = (bf16[64,1024]{1,0:T(8,128)(2,1)S(1)}, bf16[64,1024]{1,0:T(8,128)(2,1)S(1)}, u32[]{:S(2)}, u32[]{:S(2)}) collective-permute-start(bf16[64,1024]{1,0:T(8,128)(2,1)S(1)} %get-tuple-element.184), channel_id=1, source_target_pairs={{0,3},{1,2},{2,1},{3,0},{4,7},{5,6},{6,5},{7,4},{8,11},{9,10},{10,... | collective-permute-start | bytes 393224 | tf_op jit(solution)/shard_map/ppermute | solution.py:479
  190.6 9.3 %collective-permute-start.41 = (bf16[64,1024]{1,0:T(8,128)(2,1)S(1)}, bf16[64,1024]{1,0:T(8,128)(2,1)S(1)}, u32[]{:S(2)}, u32[]{:S(2)}) collective-permute-start(bf16[64,1024]{1,0:T(8,128)(2,1)S(1)} %get-tuple-element.183), channel_id=1, source_target_pairs={{0,2},{1,3},{2,0},{3,1},{4,6},{5,7},{6,4},{7,5},{8,10},{9,11},{10,... | collective-permute-start | bytes 393224 | tf_op jit(solution)/shard_map/ppermute | solution.py:479
  192.9 7.0 %collective-permute-start.42 = (bf16[64,1024]{1,0:T(8,128)(2,1)S(1)}, bf16[64,1024]{1,0:T(8,128)(2,1)S(1)}, u32[]{:S(2)}, u32[]{:S(2)}) collective-permute-start(bf16[64,1024]{1,0:T(8,128)(2,1)S(1)} %get-tuple-element.182), channel_id=1, source_target_pairs={{0,1},{1,0},{2,3},{3,2},{4,5},{5,4},{6,7},{7,6},{8,9},{9,8},{10,11... | collective-permute-start | bytes 393224 | tf_op jit(solution)/shard_map/ppermute | solution.py:479
  201.2 7.0 %collective-permute-start.43 = (bf16[64,1024]{1,0:T(8,128)(2,1)S(1)}, bf16[64,1024]{1,0:T(8,128)(2,1)S(1)}, u32[]{:S(2)}, u32[]{:S(2)}) collective-permute-start(bf16[64,1024]{1,0:T(8,128)(2,1)S(1)} %get-tuple-element.181), channel_id=1, source_target_pairs={{0,3},{1,2},{2,1},{3,0},{4,7},{5,6},{6,5},{7,4},{8,11},{9,10},{10,... | collective-permute-start | bytes 393224 | tf_op jit(solution)/shard_map/ppermute | solution.py:479
  203.1 8.3 %collective-permute-start.44 = (bf16[64,1024]{1,0:T(8,128)(2,1)S(1)}, bf16[64,1024]{1,0:T(8,128)(2,1)S(1)}, u32[]{:S(2)}, u32[]{:S(2)}) collective-permute-start(bf16[64,1024]{1,0:T(8,128)(2,1)S(1)} %get-tuple-element.180), channel_id=1, source_target_pairs={{0,2},{1,3},{2,0},{3,1},{4,6},{5,7},{6,4},{7,5},{8,10},{9,11},{10,... | collective-permute-start | bytes 393224 | tf_op jit(solution)/shard_map/ppermute | solution.py:479
  203.1 8.3 %collective-permute-start.45 = (bf16[64,1024]{1,0:T(8,128)(2,1)S(1)}, bf16[64,1024]{1,0:T(8,128)(2,1)S(1)}, u32[]{:S(2)}, u32[]{:S(2)}) collective-permute-start(bf16[64,1024]{1,0:T(8,128)(2,1)S(1)} %get-tuple-element.179), channel_id=1, source_target_pairs={{0,1},{1,0},{2,3},{3,2},{4,5},{5,4},{6,7},{7,6},{8,9},{9,8},{10,11... | collective-permute-start | bytes 393224 | tf_op jit(solution)/shard_map/ppermute | solution.py:479
